TPU v7x, 32 devices: a whole 2x2x4 slice. The times are simulated.
32 devices in a mesh: gx: 2 (over y), gy: 4 (over x, core), off: 4 (over z).
Axes of the slice: x: 2, y: 2, z: 4, core: 2. Of those that a mesh axis runs over, the one named last changes fastest.
Arguments:
- volume: float32 [8, 256, 512], P(None, 'gx', 'gy'), may hold values from -3 to 3
- strength: float32 [8, 256, 512], P(None, 'gx', 'gy'), may hold values from 1 to 8
Outputs:
- denoised: float32 [8, 256, 512], P(None, 'gx', 'gy')
All inputs are finite; a program needn't handle non-finite values.
Results may differ from a plain program's by a relative error of at most 0.00002.
Values sent between devices are 32-bit elements; how exact they have to be, the bound alone decides.
No kernel may reach another device: no remote copies, remote signals or barrier semaphores. Data moves between devices by JAX's collectives and lax.ppermute only.
A program may use at most 64 MiB of HBM per device.

v0:
```python
import math

import jax
import jax.numpy as jnp
from jax import lax
from jax.sharding import PartitionSpec as P

KERNEL_EDGE = math.exp(-0.5) / (1.0 + 2.0 * math.exp(-0.5))
KERNEL_MID = 1.0 / (1.0 + 2.0 * math.exp(-0.5))


def with_halo(cells, sides, width):
    for axis, dim in sides:
        count = lax.axis_size(axis)
        ends = count - 1
        head = lax.slice_in_dim(cells, 0, width, axis=dim)
        tail = lax.slice_in_dim(cells, cells.shape[dim] - width, cells.shape[dim], axis=dim)
        cells = jnp.concatenate(
            [
                lax.ppermute(tail, axis, [(i, (i + 1) % count) for i in range(ends)]),
                cells,
                lax.ppermute(head, axis, [((i + 1) % count, i) for i in range(ends)]),
            ],
            axis=dim,
        )
    return cells


def merged(part, axis, combine):
    gathered = jax.tree.map(lambda a: lax.all_gather(a, axis), part)

    def take(source):
        return jax.tree.map(lambda a: lax.dynamic_index_in_dim(a, source, 0, False), gathered)

    return lax.fori_loop(
        1, lax.axis_size(axis), lambda source, state: combine(state, take(source)), take(0)
    )


def patch_weight(center_block, shifted, strength):
    difference = center_block - shifted
    squares = difference * difference
    squares = KERNEL_EDGE * (squares[:-2] + squares[2:]) + KERNEL_MID * squares[1:-1]
    squares = KERNEL_EDGE * (squares[:, :-2] + squares[:, 2:]) + KERNEL_MID * squares[:, 1:-1]
    squares = (
        KERNEL_EDGE * (squares[:, :, :-2] + squares[:, :, 2:]) + KERNEL_MID * squares[:, :, 1:-1]
    )
    weight = jnp.exp(-squares / strength)
    return (weight, weight * shifted[1:-1, 1:-1, 1:-1])


def accumulate(extended, strength, z_start, z_length, numbers_of, turns):
    rows_x = extended.shape[1] - 6
    rows_y = extended.shape[2] - 6
    block_shape = (z_length + 2, rows_x + 2, rows_y + 2)
    center_block = lax.dynamic_slice(extended, (z_start + 2, 2, 2), block_shape)

    def offset_terms(number):
        shift_z = number // 25
        shift_x = number // 5 % 5
        shift_y = number % 5
        shifted = lax.dynamic_slice(extended, (shift_z, shift_x, shift_y), block_shape)
        weight, values_here = patch_weight(center_block, shifted, strength)
        keep = (number < 125) & (number != 62)
        weight = jnp.where(keep, weight, 0.0)
        values_here = jnp.where(keep, values_here, 0.0)
        return (weight, values_here)

    def one_turn(turn_index, totals):
        weights, weighted_values = jax.vmap(offset_terms)(numbers_of(turn_index))
        return (
            jnp.maximum(totals[0], jnp.max(weights, axis=0)),
            totals[1] + jnp.sum(weights, axis=0),
            totals[2] + jnp.sum(weighted_values, axis=0),
        )

    empty = jnp.zeros((z_length, rows_x, rows_y), jnp.float32)
    return lax.fori_loop(0, turns, one_turn, (empty, empty, empty))


def combine_partials(first, second):
    return (jnp.maximum(first[0], second[0]), first[1] + second[1], first[2] + second[2])


def finish(top, total, weighted, center_values):
    return (weighted + top * center_values) / (total + top)


def shards(volume, strength):
    group_count = lax.axis_size("off")
    device_index = lax.axis_index("off")
    depth = volume.shape[0]
    extended = with_halo(volume, (("gx", 1), ("gy", 2)), 3)
    extended = jnp.pad(extended, ((3, 3), (0, 0), (0, 0)))
    rounds = -(-125 // group_count)
    batch = -(-rounds // 8)
    turns = -(-rounds // batch)

    def numbers_mine(turn_index):
        return (
            turn_index * batch + jnp.arange(batch, dtype=jnp.int32)
        ) * group_count + device_index

    totals = accumulate(extended, strength, jnp.int32(0), depth, numbers_mine, turns)
    top, total, weighted = merged(totals, "off", combine_partials)
    result = finish(top, total, weighted, volume)
    return result


def solution(mesh):
    return jax.shard_map(
        shards,
        mesh=mesh,
        in_specs=(P(None, "gx", "gy"), P(None, "gx", "gy")),
        out_specs=P(None, "gx", "gy"),
        check_vma=False,
    )
```

profile of v0, /device:TPU:0, one launch (start us, length us, event | category | flops | bytes accessed | tf_op | source)
XLA Modules:
  0.0 440.3 jit_solution(13568557837226701039)
XLA Ops:
  7.6 4.9 %collective-permute-start = (f32[8,3,128]{1,0,2:T(8,128)S(1)}, f32[8,3,128]{1,0,2:T(8,128)S(1)}, u32[]{:S(2)}, u32[]{:S(2)}) collective-permute-start(f32[8,3,128]{1,0,2:T(8,128)S(1)} %copy.3), channel_id=1, source_target_pairs={{0,16},{1,17},{2,18},{3,19},{4,20},{5,21},{6,22},{7,23},{8,24},{9,... | collective-permute-start | bytes 36872 | tf_op jit(solution)/shard_map/ppermute | solution.py:20
  15.3 8.3 %collective-permute-done = f32[8,3,128]{1,0,2:T(8,128)S(1)} collective-permute-done((f32[8,3,128]{1,0,2:T(8,128)S(1)}, f32[8,3,128]{1,0,2:T(8,128)S(1)}, u32[]{:S(2)}, u32[]{:S(2)}) %collective-permute-start) | collective-permute-done | bytes 12320 | tf_op jit(solution)/shard_map/ppermute | solution.py:20
  23.6 4.4 %collective-permute-done.1 = f32[8,3,128]{1,0,2:T(8,128)S(1)} collective-permute-done((f32[8,3,128]{1,0,2:T(8,128)S(1)}, f32[8,3,128]{1,0,2:T(8,128)S(1)}, u32[]{:S(2)}, u32[]{:S(2)}) %collective-permute-start.1) | collective-permute-done | bytes 12320 | tf_op jit(solution)/shard_map/ppermute | solution.py:22
  44.4 239.1 %while.45 = (s32[]{:T(128)}, f32[8,128,128]{2,1,0:T(8,128)}, f32[8,128,128]{2,1,0:T(8,128)}, f32[8,128,128]{2,1,0:T(8,128)}, s32[]{:T(128)}, /*index=5*/f32[10,1...) while((s32[]{:T(128)}, f32[8,128,128]{2,1,0:T(8,128)}, ...), condition=%wide.region_4.5_spmd.clone, body=%wide.region_0.4_spmd.clone.sunk | while | flops 12330030 | bytes 42629180 | solution.py:78
  44.5 16.3 %while.46 = (s32[]{:T(128)}, f32[14,134,134]{2,1,0:T(8,128)S(1)}, s32[4,3]{1,0:T(4,128)S(1)}, f32[4,10,130,130]{3,2,1,0:T(8,128)}, s32[]{:T(128)}) while((s32[]{:T(128)}, f32[14,134,134]{2,1,0:T(8,128)S(1)}, s32[4,3]{1,0:T(4,128)S(1)}, f32[4,10,130,130]{3,2,1,0:T(8,128)}, s32[]{:T(128)}) %tuple.107), condition=%wide.while_cond, body=%wide.while_body.sunk | while | flops 2 | bytes 2070801 | solution.py:62
  60.8 3.5 subtract_multiply_fusion.2
  66.1 4.2 select_reduce_fusion.4
  72.4 16.3 %while.46 = (s32[]{:T(128)}, f32[14,134,134]{2,1,0:T(8,128)S(1)}, s32[4,3]{1,0:T(4,128)S(1)}, f32[4,10,130,130]{3,2,1,0:T(8,128)}, s32[]{:T(128)}) while((s32[]{:T(128)}, f32[14,134,134]{2,1,0:T(8,128)S(1)}, s32[4,3]{1,0:T(4,128)S(1)}, f32[4,10,130,130]{3,2,1,0:T(8,128)}, s32[]{:T(128)}) %tuple.107), condition=%wide.while_cond, body=%wide.while_body.sunk | while | flops 2 | bytes 2070801 | solution.py:62
  88.8 3.5 subtract_multiply_fusion.2
  94.0 4.2 select_reduce_fusion.4
  102.6 16.3 %while.46 = (s32[]{:T(128)}, f32[14,134,134]{2,1,0:T(8,128)S(1)}, s32[4,3]{1,0:T(4,128)S(1)}, f32[4,10,130,130]{3,2,1,0:T(8,128)}, s32[]{:T(128)}) while((s32[]{:T(128)}, f32[14,134,134]{2,1,0:T(8,128)S(1)}, s32[4,3]{1,0:T(4,128)S(1)}, f32[4,10,130,130]{3,2,1,0:T(8,128)}, s32[]{:T(128)}) %tuple.107), condition=%wide.while_cond, body=%wide.while_body.sunk | while | flops 2 | bytes 2070801 | solution.py:62
  118.9 3.5 subtract_multiply_fusion.2
  124.2 4.2 select_reduce_fusion.4
  132.8 16.3 %while.46 = (s32[]{:T(128)}, f32[14,134,134]{2,1,0:T(8,128)S(1)}, s32[4,3]{1,0:T(4,128)S(1)}, f32[4,10,130,130]{3,2,1,0:T(8,128)}, s32[]{:T(128)}) while((s32[]{:T(128)}, f32[14,134,134]{2,1,0:T(8,128)S(1)}, s32[4,3]{1,0:T(4,128)S(1)}, f32[4,10,130,130]{3,2,1,0:T(8,128)}, s32[]{:T(128)}) %tuple.107), condition=%wide.while_cond, body=%wide.while_body.sunk | while | flops 2 | bytes 2070801 | solution.py:62
  149.1 3.5 subtract_multiply_fusion.2
  154.4 4.2 select_reduce_fusion.4
  162.9 16.3 %while.46 = (s32[]{:T(128)}, f32[14,134,134]{2,1,0:T(8,128)S(1)}, s32[4,3]{1,0:T(4,128)S(1)}, f32[4,10,130,130]{3,2,1,0:T(8,128)}, s32[]{:T(128)}) while((s32[]{:T(128)}, f32[14,134,134]{2,1,0:T(8,128)S(1)}, s32[4,3]{1,0:T(4,128)S(1)}, f32[4,10,130,130]{3,2,1,0:T(8,128)}, s32[]{:T(128)}) %tuple.107), condition=%wide.while_cond, body=%wide.while_body.sunk | while | flops 2 | bytes 2070801 | solution.py:62
  179.3 3.5 subtract_multiply_fusion.2
  184.5 4.2 select_reduce_fusion.4
  193.1 16.3 %while.46 = (s32[]{:T(128)}, f32[14,134,134]{2,1,0:T(8,128)S(1)}, s32[4,3]{1,0:T(4,128)S(1)}, f32[4,10,130,130]{3,2,1,0:T(8,128)}, s32[]{:T(128)}) while((s32[]{:T(128)}, f32[14,134,134]{2,1,0:T(8,128)S(1)}, s32[4,3]{1,0:T(4,128)S(1)}, f32[4,10,130,130]{3,2,1,0:T(8,128)}, s32[]{:T(128)}) %tuple.107), condition=%wide.while_cond, body=%wide.while_body.sunk | while | flops 2 | bytes 2070801 | solution.py:62
  209.4 3.5 subtract_multiply_fusion.2
  214.7 4.2 select_reduce_fusion.4
  223.2 16.3 %while.46 = (s32[]{:T(128)}, f32[14,134,134]{2,1,0:T(8,128)S(1)}, s32[4,3]{1,0:T(4,128)S(1)}, f32[4,10,130,130]{3,2,1,0:T(8,128)}, s32[]{:T(128)}) while((s32[]{:T(128)}, f32[14,134,134]{2,1,0:T(8,128)S(1)}, s32[4,3]{1,0:T(4,128)S(1)}, f32[4,10,130,130]{3,2,1,0:T(8,128)}, s32[]{:T(128)}) %tuple.107), condition=%wide.while_cond, body=%wide.while_body.sunk | while | flops 2 | bytes 2070801 | solution.py:62
  239.6 3.5 subtract_multiply_fusion.2
  244.8 4.2 select_reduce_fusion.4
  253.4 16.3 %while.46 = (s32[]{:T(128)}, f32[14,134,134]{2,1,0:T(8,128)S(1)}, s32[4,3]{1,0:T(4,128)S(1)}, f32[4,10,130,130]{3,2,1,0:T(8,128)}, s32[]{:T(128)}) while((s32[]{:T(128)}, f32[14,134,134]{2,1,0:T(8,128)S(1)}, s32[4,3]{1,0:T(4,128)S(1)}, f32[4,10,130,130]{3,2,1,0:T(8,128)}, s32[]{:T(128)}) %tuple.107), condition=%wide.while_cond, body=%wide.while_body.sunk | while | flops 2 | bytes 2070801 | solution.py:62
  269.7 3.5 subtract_multiply_fusion.2
  275.0 4.2 select_reduce_fusion.4
  284.9 46.2 %all-gather.7.cloned.1.call-done = f32[32,128,128]{2,1,0:T(8,128)} async-done(((f32[8,128,128]{2,1,0:T(8,128)}), f32[32,128,128]{2,1,0:T(8,128)}) %all-gather.7.cloned.1.call-update) | async-done | bytes 2097168 | tf_op jit(solution)/shard_map/all_gather | solution.py:30
  332.2 45.2 %all-gather.9.cloned.1.call-done = f32[32,128,128]{2,1,0:T(8,128)} async-done(((f32[8,128,128]{2,1,0:T(8,128)}), f32[32,128,128]{2,1,0:T(8,128)}) %all-gather.9.cloned.1.call-update) | async-done | bytes 2097168 | tf_op jit(solution)/shard_map/all_gather | solution.py:30
  378.4 45.2 %all-gather.11.cloned.1.call-done = f32[32,128,128]{2,1,0:T(8,128)} async-done(((f32[8,128,128]{2,1,0:T(8,128)}), f32[32,128,128]{2,1,0:T(8,128)}) %all-gather.11.cloned.1.call-update) | async-done | bytes 2097168 | tf_op jit(solution)/shard_map/all_gather | solution.py:30
  424.7 8.1 %while.43 = (s32[]{:T(128)}, f32[8,128,128]{2,1,0:T(8,128)S(1)}, f32[8,128,128]{2,1,0:T(8,128)S(1)}, f32[8,128,128]{2,1,0:T(8,128)S(1)}, f32[4,8,128,128]{3,2,1,...) while((s32[]{:T(128)}, f32[8,128,128]{2,1,0:T(8,128)S(1)}, ...), condition=%wide.region_6.7_spmd, body=%wide.region_5.6_spmd.sunk | while | flops 393221 | bytes 4718743 | solution.py:35
  (229 shorter events, 210.5 us)
Async XLA Ops:
  6.5 324.6 %all-gather.7.cloned.1.call-start = ((), (), s32[]{:S(2)}) async-start(), calls=%async_computation | async-start | bytes 2621440 | tf_op jit(solution)/shard_map/all_gather | solution.py:30
  7.6 16.0 %collective-permute-start = (f32[8,3,128]{1,0,2:T(8,128)S(1)}, f32[8,3,128]{1,0,2:T(8,128)S(1)}, u32[]{:S(2)}, u32[]{:S(2)}) collective-permute-start(f32[8,3,128]{1,0,2:T(8,128)S(1)} %copy.3), channel_id=1, source_target_pairs={{0,16},{1,17},{2,18},{3,19},{4,20},{5,21},{6,22},{7,23},{8,24},{9,... | collective-permute-start | bytes 36872 | tf_op jit(solution)/shard_map/ppermute | solution.py:20
  12.8 15.3 %collective-permute-start.1 = (f32[8,3,128]{1,0,2:T(8,128)S(1)}, f32[8,3,128]{1,0,2:T(8,128)S(1)}, u32[]{:S(2)}, u32[]{:S(2)}) collective-permute-start(f32[8,3,128]{1,0,2:T(8,128)S(1)} %copy.4), channel_id=1, source_target_pairs={{16,0},{17,1},{18,2},{19,3},{20,4},{21,5},{22,6},{23,7},{24,8},{25... | collective-permute-start | bytes 36872 | tf_op jit(solution)/shard_map/ppermute | solution.py:22
  28.1 2.6 collective-permute-start.2
  29.4 4.8 %collective-permute-start.3 = (f32[8,134,3]{1,0,2:T(8,128)S(1)}, f32[8,134,3]{1,0,2:T(8,128)S(1)}, u32[]{:S(2)}, u32[]{:S(2)}) collective-permute-start(f32[8,134,3]{1,0,2:T(8,128)S(1)} %get-tuple-element.516), channel_id=1, source_target_pairs={{4,0},{8,4},{12,8},{5,1},{9,5},{13,9},{6,2},{10,6},{14,10},{7,3},{... | collective-permute-start | bytes 38600 | tf_op jit(solution)/shard_map/ppermute | solution.py:22
  35.3 1.4 copy-start
  65.0 1.1 copy-start.1
  92.9 1.1 copy-start.1
  123.1 1.1 copy-start.1
  153.2 1.1 copy-start.1
  183.4 1.1 copy-start.1
  213.6 1.1 copy-start.1
  243.7 1.1 copy-start.1
  273.9 1.1 copy-start.1
  283.4 93.9 %all-gather.9.cloned.1.call-start = ((), (), s32[]{:S(2)}) async-start(), calls=%async_computation.1 | async-start | bytes 2621440 | tf_op jit(solution)/shard_map/all_gather | solution.py:30
  284.2 139.4 %all-gather.11.cloned.1.call-start = ((), (), s32[]{:S(2)}) async-start(), calls=%async_computation.2 | async-start | bytes 2621440 | tf_op jit(solution)/shard_map/all_gather | solution.py:30
  424.7 8.1 %copy-start.2 = (f32[8,128,128]{2,1,0:T(8,128)S(1)}, f32[8,128,128]{2,1,0:T(8,128)}, u32[]{:S(2)}) copy-start(f32[8,128,128]{2,1,0:T(8,128)} %param.6) | copy-start | bytes 1572868
Sparse Core Ops, SparseCore 0:
  283.6 47.4 all-gather.6
  332.7 44.6 all-gather.8
  378.9 44.6 all-gather.10
where the time goes:
time: 443 us; the launch traced here: 440 us
  waiting for transfers between devices  154 us (35%)
  local copies, waits for them, and re-layouts  146 us (33%)
  other arithmetic  118 us (27%)
  between operations  13.3 us (3%)
  starting transfers between devices  8.86 us (2%)
    all_gather x3, waiting for transfers between devices, merged(): gathered = jax.tree.map(lambda a: lax.all_gather(a, axis), part)  137 us
    gather x96, local copies, waits for them, and re-layouts  131 us
    reduce_sum x8, other arithmetic, one_turn(): jnp.sum(weighted_values, axis=0)  33.6 us
    mul x8, other arithmetic, patch_weight(): squares = difference * difference  28.1 us
    add x8, other arithmetic, one_turn(): totals[2] + jnp.sum(weighted_values, axis=0)  17.2 us
    max x8, other arithmetic, one_turn(): jnp.maximum(totals[0], jnp.max(weights, axis=0))  14.1 us
  transfers between devices with their start and end apart: 7, of which 6 were waited for; matrix products, arithmetic and copies ran while one was open for 1% of the time, Pallas kernels for 0%

commit v1 on v0

v1 whole, which is shorter than its diff:
```python
import math

import jax
import jax.numpy as jnp
from jax import lax
from jax.experimental import pallas as pl
from jax.experimental.pallas import tpu as pltpu
from jax.sharding import PartitionSpec as P

EDGE = math.exp(-0.5) / (1.0 + 2.0 * math.exp(-0.5))
GAIN = math.exp(0.5)
SCALE = -(EDGE**3) * math.log2(math.e)
LANES = 128
SUBS = 8


def with_halo(cells, sides, width):
    for axis, dim in sides:
        count = lax.axis_size(axis)
        ends = count - 1
        head = lax.slice_in_dim(cells, 0, width, axis=dim)
        tail = lax.slice_in_dim(cells, cells.shape[dim] - width, cells.shape[dim], axis=dim)
        cells = jnp.concatenate(
            [
                lax.ppermute(tail, axis, [(i, (i + 1) % count) for i in range(ends)]),
                cells,
                lax.ppermute(head, axis, [((i + 1) % count, i) for i in range(ends)]),
            ],
            axis=dim,
        )
    return cells


def left(x, n):
    return x if n % LANES == 0 else pltpu.roll(x, (-n) % LANES, 1)


def right(x, n):
    return left(x, -n)


def lane_filter(x):
    return right(x, 1) + left(x, 1) + GAIN * x


def make_kernel(depth, rows, blocks):
    wide = blocks + 6

    def kernel(lower, upper, strength, out, vals, cent, energy, scale, top, total, weighted):
        base = lax.axis_index("off") * rows
        lane = lax.broadcasted_iota(jnp.int32, (SUBS, LANES), 1)

        def fill(z, _):
            windows = []
            for i in range(wide):
                at = pl.ds(base + i, SUBS, stride=blocks)
                low = lower[z, at, :]
                high = upper[z, at, :]
                vals[0, z, i] = low
                for c in range(1, 5):
                    vals[c, z, i] = jnp.where(lane < LANES - c, left(low, c), left(high, c))
                windows.append(jnp.where(lane < 2, left(low, 126), right(high, 2)))
            for i in range(blocks + 2):
                cent[0, z, i] = -2.0 * vals[2, z, i + 2]
            strips = []
            for i in range(wide):
                strip = jnp.zeros((SUBS, LANES), jnp.float32)
                for c in range(5):
                    strip = jnp.where(
                        (lane >= 1 + 4 * c) & (lane < 5 + 4 * c), right(windows[i], 1 + 3 * c), strip
                    )
                strips.append(strip)
            for i in range(blocks + 2):
                packed = jnp.zeros((SUBS, LANES), jnp.float32)
                for b in range(5):
                    packed = jnp.where(
                        (lane >= 1 + 20 * b) & (lane < 21 + 20 * b), right(strips[i + b], 20 * b), packed
                    )
                vals[5, z, i] = packed
                spread = jnp.where((lane >= 1) & (lane < 5), left(windows[i + 2], 1), 0.0)
                for n in (4, 8, 16, 32, 64):
                    spread = spread + right(spread, n)
                cent[1, z, i] = -2.0 * spread
            for i in range(blocks):
                s = strength[z, pl.ds(base + i, SUBS, stride=blocks), :]
                s = SCALE / s
                scale[0, z, i] = right(s, 1)
                spread = jnp.where((lane == 2) | (lane == 3), left(s, 124), 0.0)
                for n in (4, 8, 16, 32, 64):
                    spread = spread + right(spread, n)
                scale[1, z, i] = spread
            for i in range(blocks):
                for kind in range(2):
                    top[kind, z, i] = jnp.zeros((SUBS, LANES), jnp.float32)
                    total[kind, z, i] = jnp.zeros((SUBS, LANES), jnp.float32)
                    weighted[kind, z, i] = jnp.zeros((SUBS, LANES), jnp.float32)
            return 0

        lax.fori_loop(0, depth, fill, 0)

        def energies(plane, _):
            count = blocks + 4
            filtered = []
            for z in range(depth):
                squares = []
                for i in range(wide):
                    v = vals[plane, z, i]
                    squares.append(v * v)
                filtered.append(
                    [
                        lane_filter(squares[i] + squares[i + 2] + GAIN * squares[i + 1])
                        for i in range(count)
                    ]
                )
                if z >= 1:
                    store_energy(plane, z - 1, filtered)
                if z == 0:
                    for i in range(count):
                        energy[plane, 0, i] = filtered[0][i]
            store_energy(plane, depth - 1, filtered)
            for i in range(count):
                energy[plane, depth + 1, i] = filtered[depth - 1][i]
            return 0

        def store_energy(plane, z, filtered):
            for i in range(blocks + 4):
                e = GAIN * filtered[z][i]
                if z > 0:
                    e = e + filtered[z - 1][i]
                if z < depth - 1:
                    e = e + filtered[z + 1][i]
                energy[plane, z + 1, i] = e

        for i in range(blocks + 2, wide):
            for z in range(depth):
                vals[5, z, i] = jnp.zeros((SUBS, LANES), jnp.float32)
        lax.fori_loop(0, 6, energies, 0)

        def offset(a, plane, b, kind, mask=None):
            first, last = max(0, -a), min(depth, depth - a)
            filtered = {}

            def emit(z):
                if not first <= z < last:
                    return
                p = [cent[kind, z, i] * vals[plane, z + a, i + b] for i in range(blocks + 2)]
                filtered[z] = [
                    lane_filter(p[i] + p[i + 2] + GAIN * p[i + 1]) for i in range(blocks)
                ]

            emit(0)
            for z in range(depth):
                emit(z + 1)
                for i in range(blocks):
                    parts = [filtered[y][i] for y in (z - 1, z + 1) if y in filtered]
                    if z in filtered:
                        parts.append(GAIN * filtered[z][i])
                    if -1 <= z + a <= depth:
                        parts.append(energy[plane, z + a + 1, i + b])
                    if parts:
                        e = parts[0]
                        for part in parts[1:]:
                            e = e + part
                        w = jnp.exp2(scale[kind, z, i] * e)
                    else:
                        w = jnp.ones((SUBS, LANES), jnp.float32)
                    if mask is not None:
                        w = jnp.where(mask, 0.0, w)
                    top[kind, z, i] = jnp.maximum(top[kind, z, i], w)
                    total[kind, z, i] += w
                    if 0 <= z + a < depth:
                        weighted[kind, z, i] += w * vals[plane, z + a, i + b + 1]

        for a in range(-2, 3):
            skip = a == 0

            def one(n, _, a=a, skip=skip):
                if skip:
                    n = n + jnp.where(n >= 12, 1, 0)
                offset(a, n % 5, n // 5, 0)
                return 0

            lax.fori_loop(0, 24 if skip else 25, one, 0)
            offset(a, 5, 0, 1, mask=(lane >= 49) & (lane < 53) if skip else None)

        def finish(z, _):
            def ratio(t, s, w, v):
                return (w + t * v) / (s + t)

            for i in range(blocks):
                main = ratio(top[0, z, i], total[0, z, i], weighted[0, z, i], vals[2, z, i + 3])
                keep = (lane >= 1) & (lane < 101)
                t = jnp.where(keep, top[1, z, i], 0.0)
                s = jnp.where(keep, total[1, z, i], 0.0)
                w = jnp.where(keep, weighted[1, z, i], 0.0)
                for n in (64, 32, 16, 8, 4):
                    t = jnp.maximum(t, left(t, n))
                    s = s + left(s, n)
                    w = w + left(w, n)
                edge = ratio(t, s, w, -0.5 * cent[1, z, i + 1])
                out[z, pl.ds(i, SUBS, stride=blocks), :] = jnp.where(
                    lane < LANES - 2, left(main, 1), edge
                )
            return 0

        lax.fori_loop(0, depth, finish, 0)

    return kernel


def denoise(extended, strength):
    depth, size_x, size_y = strength.shape
    rows = size_x // lax.axis_size("off")
    blocks = rows // SUBS
    assert size_y == LANES
    tile = (SUBS, LANES)
    f32 = jnp.float32
    lower = extended[:, :, :LANES]
    upper = jnp.pad(extended[:, :, LANES:], ((0, 0), (0, 0), (0, LANES - 6)))
    return pl.pallas_call(
        make_kernel(depth, rows, blocks),
        out_shape=jax.ShapeDtypeStruct((depth, rows, size_y), f32),
        in_specs=[pl.BlockSpec(memory_space=pltpu.VMEM)] * 3,
        out_specs=pl.BlockSpec(memory_space=pltpu.VMEM),
        scratch_shapes=[
            pltpu.VMEM((6, depth, blocks + 6) + tile, f32),
            pltpu.VMEM((2, depth, blocks + 2) + tile, f32),
            pltpu.VMEM((6, depth + 2, blocks + 4) + tile, f32),
            pltpu.VMEM((2, depth, blocks) + tile, f32),
            pltpu.VMEM((2, depth, blocks) + tile, f32),
            pltpu.VMEM((2, depth, blocks) + tile, f32),
            pltpu.VMEM((2, depth, blocks) + tile, f32),
        ],
        compiler_params=pltpu.CompilerParams(vmem_limit_bytes=32 * 2**20),
    )(lower, upper, strength)


def shards(volume, strength):
    extended = with_halo(volume, (("gx", 1), ("gy", 2)), 3)
    part = denoise(extended, strength)
    return lax.all_gather(part, "off", axis=1, tiled=True)


def solution(mesh):
    return jax.shard_map(
        shards,
        mesh=mesh,
        in_specs=(P(None, "gx", "gy"), P(None, "gx", "gy")),
        out_specs=P(None, "gx", "gy"),
        check_vma=False,
    )
```

time: 443 us -> 66.3 us (0.15)
  waiting for transfers between devices: 154 us -> 4.9 us
  local copies, waits for them, and re-layouts: 146 us -> 3.44 us
  other arithmetic: 118 us -> 1.62 us
  Pallas kernels: 0 us -> 28.4 us
  blocking collectives: 0 us -> 16.9 us
  between operations: 13.3 us -> 0.09 us
    all_gather x3 -> x0, waiting for transfers between devices: 137 us -> none  [merged(): gathered = jax.tree.map(lambda a: lax.all_gather(a, axis), part)]
    gather x96 -> x0, local copies, waits for them, and re-layouts: 131 us -> none
    add x27 -> x0, other arithmetic: 35.3 us -> none  [the longest x8 17.2 us: one_turn(): totals[2] + jnp.sum(weighted_values, axis=0)]
    reduce_sum x8 -> x0, other arithmetic: 33.6 us -> none  [one_turn(): jnp.sum(weighted_values, axis=0)]
    pallas_call x0 -> x1, Pallas kernels: none -> 28.4 us  [denoise(): pl.pallas_call(make_kernel(depth, rows, blocks), out_shape=jax.ShapeDtype...]
    mul x8 -> x0, other arithmetic: 28.1 us -> none  [patch_weight(): squares = difference * difference]
    max x11 -> x0, other arithmetic: 17.6 us -> none  [the longest x8 14.1 us: one_turn(): jnp.maximum(totals[0], jnp.max(weights, axis=0))]
    all_gather x0 -> x1, blocking collectives: none -> 16.9 us  [shards(): return lax.all_gather(part, 'off', axis=1, tiled=True)]
  transfers between devices with their start and end apart: 7 -> 4, of which waited for: 6 -> 3; matrix products, arithmetic and copies ran while one was open for 1% -> 1% of each run, Pallas kernels for 0% -> 0%
where the time goes in v1:
time: 66.3 us; the launch traced here: 66 us
  Pallas kernels  28.4 us (43%)
  blocking collectives  16.9 us (25%)
  starting transfers between devices  10.6 us (16%)
  waiting for transfers between devices  4.9 us (7%)
  local copies, waits for them, and re-layouts  3.44 us (5%)
  other arithmetic  1.62 us (2%)
    pallas_call x1, Pallas kernels, denoise(): pl.pallas_call(make_kernel(depth, rows, blocks), out_shape=jax.ShapeDtype...  28.4 us
    all_gather x1, blocking collectives, shards(): return lax.all_gather(part, 'off', axis=1, tiled=True)  16.9 us
    ppermute x2, starting transfers between devices, with_halo(): lax.ppermute(tail, axis, [(i, (i + 1) % count) for i in range(ends)])  8.02 us
    ppermute x2, waiting for transfers between devices, with_halo(): lax.ppermute(head, axis, [((i + 1) % count, i) for i in range(ends)])  4.21 us
    ppermute x2, starting transfers between devices, with_halo(): lax.ppermute(head, axis, [((i + 1) % count, i) for i in range(ends)])  2.59 us
    concatenate x2, other arithmetic, with_halo(): jnp.concatenate([lax.ppermute(tail, axis, [(i, (i + 1) % count) for i in...  1.62 us
  transfers between devices with their start and end apart: 4, of which 3 were waited for; matrix products, arithmetic and copies ran while one was open for 1% of the time, Pallas kernels for 0%

profile of v1, /device:TPU:0, one launch (start us, length us, event | category | flops | bytes accessed | tf_op | source)
XLA Modules:
  0.0 66.0 jit_solution(8484282097926925580)
XLA Ops:
  0.0 0.8 %fusion.1 = (f32[8,3,128]{2,1,0:T(4,128)S(1)}, f32[8,3,128]{2,1,0:T(4,128)S(1)}) fusion(f32[8,128,128]{2,1,0:T(8,128)} %param.2), kind=kLoop, calls=%fused_computation.9 | loop fusion | bytes 49152 | tf_op jit(solution)/shard_map/slice | solution.py:22
  0.8 4.9 %collective-permute-start = (f32[8,3,128]{2,1,0:T(4,128)S(1)}, f32[8,3,128]{2,1,0:T(4,128)S(1)}, u32[]{:S(2)}, u32[]{:S(2)}) collective-permute-start(f32[8,3,128]{2,1,0:T(4,128)S(1)} %get-tuple-element.9), channel_id=1, source_target_pairs={{0,16},{1,17},{2,18},{3,19},{4,20},{5,21},{6,22},{7,23},{8,24},{9,... | collective-permute-start | bytes 36872 | tf_op jit(solution)/shard_map/ppermute | solution.py:25
  5.6 1.3 %collective-permute-start.1 = (f32[8,3,128]{2,1,0:T(4,128)S(1)}, f32[8,3,128]{2,1,0:T(4,128)S(1)}, u32[]{:S(2)}, u32[]{:S(2)}) collective-permute-start(f32[8,3,128]{2,1,0:T(4,128)S(1)} %get-tuple-element.10), channel_id=1, source_target_pairs={{16,0},{17,1},{18,2},{19,3},{20,4},{21,5},{22,6},{23,7},{24,8},{25... | collective-permute-start | bytes 36872 | tf_op jit(solution)/shard_map/ppermute | solution.py:27
  6.9 0.1 collective-permute-done
  7.1 4.2 %collective-permute-done.1 = f32[8,3,128]{2,1,0:T(4,128)S(1)} collective-permute-done((f32[8,3,128]{2,1,0:T(4,128)S(1)}, f32[8,3,128]{2,1,0:T(4,128)S(1)}, u32[]{:S(2)}, u32[]{:S(2)}) %collective-permute-start.1) | collective-permute-done | bytes 12320 | tf_op jit(solution)/shard_map/ppermute | solution.py:27
  11.3 1.1 %pad_maximum_fusion.3 = f32[8,134,128]{2,1,0:T(8,128)S(1)} fusion(f32[8,3,128]{2,1,0:T(4,128)S(1)} %collective-permute-done.1, f32[8,128,128]{2,1,0:T(8,128)} %param.2, f32[8,3,128]{2,1,0:T(4,128)S(1)} %collective-permute-done), kind=kLoop, calls=%fused_computation.7 | loop fusion | flops 274432 | bytes 1097728 | tf_op jit(solution)/shard_map/concatenate | solution.py:23
  12.4 0.2 fusion
  12.6 0.3 copy.5
  12.9 1.3 %collective-permute-start.3 = (f32[8,134,3]{1,0,2:T(8,128)S(1)}, f32[8,134,3]{1,0,2:T(8,128)S(1)}, u32[]{:S(2)}, u32[]{:S(2)}) collective-permute-start(f32[8,134,3]{1,0,2:T(8,128)S(1)} %copy.5), channel_id=1, source_target_pairs={{4,0},{8,4},{12,8},{5,1},{9,5},{13,9},{6,2},{10,6},{14,10},{7,3},{... | collective-permute-start | bytes 38600 | tf_op jit(solution)/shard_map/ppermute | solution.py:27
  14.2 0.3 copy.3
  14.5 0.0 copy-start.1
  14.6 3.2 %collective-permute-start.2 = (f32[8,134,3]{1,0,2:T(8,128)S(1)}, f32[8,134,3]{1,0,2:T(8,128)S(1)}, u32[]{:S(2)}, u32[]{:S(2)}) collective-permute-start(f32[8,134,3]{1,0,2:T(8,128)S(1)} %copy.3), channel_id=1, source_target_pairs={{0,4},{4,8},{8,12},{1,5},{5,9},{9,13},{2,6},{6,10},{10,14},{3,7},{... | collective-permute-start | bytes 38600 | tf_op jit(solution)/shard_map/ppermute | solution.py:25
  17.7 0.0 collective-permute-done.3
  17.7 0.2 copy.6
  18.0 0.6 collective-permute-done.2
  18.6 0.2 copy.4
  18.8 0.0 copy-done.1
  18.8 0.0 copy-start
  18.8 0.5 select_maximum_fusion
  19.4 0.5 copy-done
  19.9 28.4 %shard_map.28 = f32[8,32,128]{2,1,0:T(8,128)S(1)} custom-call(f32[8,134,128]{2,1,0:T(8,128)S(1)} %get-tuple-element.6.lower, f32[8,134,128]{2,1,0:T(8,128)S(1)} %get-tuple-element.5.upper, f32[8,128,128]{2,1,0:T(8,128)S(1)} %copy-done), custom_call_target="tpu_custom_call" | custom-call | tf_op jit(solution)/shard_map/pallas_call | solution.py:220
  48.3 16.9 %all_gather.3 = f32[8,128,128]{2,1,0:T(8,128)S(1)} all-gather(f32[8,32,128]{2,1,0:T(8,128)S(1)} %shard_map.28), channel_id=1, replica_groups=mesh['gx'=2,'gy'=4,'off'=4] {'off'}, dimensions={1}, use_global_device_ids=true | all-gather | bytes 655360 | tf_op jit(solution)/shard_map/all_gather | solution.py:241
  65.2 0.8 %copy.8 = f32[8,128,128]{2,1,0:T(8,128)} copy(f32[8,128,128]{2,1,0:T(8,128)S(1)} %all_gather.3) | data formatting | bytes 1048576
Async XLA Ops:
  0.8 6.3 %collective-permute-start = (f32[8,3,128]{2,1,0:T(4,128)S(1)}, f32[8,3,128]{2,1,0:T(4,128)S(1)}, u32[]{:S(2)}, u32[]{:S(2)}) collective-permute-start(f32[8,3,128]{2,1,0:T(4,128)S(1)} %get-tuple-element.9), channel_id=1, source_target_pairs={{0,16},{1,17},{2,18},{3,19},{4,20},{5,21},{6,22},{7,23},{8,24},{9,... | collective-permute-start | bytes 36872 | tf_op jit(solution)/shard_map/ppermute | solution.py:25
  5.6 5.6 %collective-permute-start.1 = (f32[8,3,128]{2,1,0:T(4,128)S(1)}, f32[8,3,128]{2,1,0:T(4,128)S(1)}, u32[]{:S(2)}, u32[]{:S(2)}) collective-permute-start(f32[8,3,128]{2,1,0:T(4,128)S(1)} %get-tuple-element.10), channel_id=1, source_target_pairs={{16,0},{17,1},{18,2},{19,3},{20,4},{21,5},{22,6},{23,7},{24,8},{25... | collective-permute-start | bytes 36872 | tf_op jit(solution)/shard_map/ppermute | solution.py:27
  12.9 4.8 %collective-permute-start.3 = (f32[8,134,3]{1,0,2:T(8,128)S(1)}, f32[8,134,3]{1,0,2:T(8,128)S(1)}, u32[]{:S(2)}, u32[]{:S(2)}) collective-permute-start(f32[8,134,3]{1,0,2:T(8,128)S(1)} %copy.5), channel_id=1, source_target_pairs={{4,0},{8,4},{12,8},{5,1},{9,5},{13,9},{6,2},{10,6},{14,10},{7,3},{... | collective-permute-start | bytes 38600 | tf_op jit(solution)/shard_map/ppermute | solution.py:27
  14.5 4.3 %copy-start.1 = (f32[8,128,128]{2,1,0:T(8,128)S(1)}, f32[8,128,128]{2,1,0:T(8,128)}, u32[]{:S(2)}) copy-start(f32[8,128,128]{2,1,0:T(8,128)} %param.2) | copy-start | bytes 1572868
  14.6 4.0 %collective-permute-start.2 = (f32[8,134,3]{1,0,2:T(8,128)S(1)}, f32[8,134,3]{1,0,2:T(8,128)S(1)}, u32[]{:S(2)}, u32[]{:S(2)}) collective-permute-start(f32[8,134,3]{1,0,2:T(8,128)S(1)} %copy.3), channel_id=1, source_target_pairs={{0,4},{4,8},{8,12},{1,5},{5,9},{9,13},{2,6},{6,10},{10,14},{3,7},{... | collective-permute-start | bytes 38600 | tf_op jit(solution)/shard_map/ppermute | solution.py:25
  18.8 1.0 %copy-start = (f32[8,128,128]{2,1,0:T(8,128)S(1)}, f32[8,128,128]{2,1,0:T(8,128)}, u32[]{:S(2)}) copy-start(f32[8,128,128]{2,1,0:T(8,128)} %strength.1) | copy-start | bytes 1572868

commit v2 on v0

v2 whole, which is shorter than its diff:
```python
import math

import jax
import jax.numpy as jnp
from jax import lax
from jax.experimental import pallas as pl
from jax.experimental.pallas import tpu as pltpu
from jax.sharding import PartitionSpec as P

EDGE = math.exp(-0.5) / (1.0 + 2.0 * math.exp(-0.5))
GAIN = math.exp(0.5)
SCALE = -(EDGE**3) * math.log2(math.e)
LANES = 128
SUBS = 8


def with_halo(cells, sides, width):
    for axis, dim in sides:
        count = lax.axis_size(axis)
        ends = count - 1
        head = lax.slice_in_dim(cells, 0, width, axis=dim)
        tail = lax.slice_in_dim(cells, cells.shape[dim] - width, cells.shape[dim], axis=dim)
        cells = jnp.concatenate(
            [
                lax.ppermute(tail, axis, [(i, (i + 1) % count) for i in range(ends)]),
                cells,
                lax.ppermute(head, axis, [((i + 1) % count, i) for i in range(ends)]),
            ],
            axis=dim,
        )
    return cells


def make_kernel(depth, rows, blocks):
    wide = blocks + 6
    tall = -(-(rows + 6) // SUBS)

    def kernel(middle, sides, strength, out, flat, vals, cent, energy, scale, top, total, weighted):
        lane = lax.broadcasted_iota(jnp.int32, (SUBS, LANES), 1)

        def fill(z, _):
            for r in range(tall):
                at = pl.ds(SUBS * r, SUBS)
                v, h = middle[z, at, :], sides[z, at, :]
                flat[3, at, :] = v
                for c in range(1, 4):
                    flat[3 + c, at, :] = pltpu.roll(jnp.where(lane < c, h, v), LANES - c, 1)
                    flat[3 - c, at, :] = pltpu.roll(jnp.where(lane >= LANES - c, h, v), c, 1)
            for i in range(wide):
                for c in range(7):
                    v = flat[c, pl.ds(i, SUBS, stride=blocks), :]
                    vals[c, z, i] = v
                    if 2 <= c <= 4 and 2 <= i < wide - 2:
                        cent[c - 2, z, i - 2] = (-2.0 * GAIN if c == 3 else -2.0) * v
            for i in range(blocks):
                scale[z, i] = SCALE / strength[z, pl.ds(i, SUBS, stride=blocks), :]
                top[z, i] = jnp.zeros((SUBS, LANES), jnp.float32)
                total[z, i] = jnp.zeros((SUBS, LANES), jnp.float32)
                weighted[z, i] = jnp.zeros((SUBS, LANES), jnp.float32)
            return 0

        lax.fori_loop(0, depth, fill, 0)

        def three(a, b, c):
            return a + c + GAIN * b

        def energies(c, _):
            count = blocks + 4
            filtered = []

            def store(z):
                for i in range(count):
                    e = GAIN * filtered[z][i] if 0 <= z < depth else None
                    for y in (z - 1, z + 1):
                        if 0 <= y < depth:
                            e = filtered[y][i] if e is None else e + filtered[y][i]
                    energy[c, z + 1, i] = e

            for z in range(depth):
                line = []
                for i in range(wide):
                    u, v, w = (vals[c + k, z, i] for k in range(3))
                    line.append(three(u * u, v * v, w * w))
                filtered.append([three(*line[i : i + 3]) for i in range(count)])
                store(z - 1)
            store(depth - 1)
            store(depth)
            return 0

        lax.fori_loop(0, 5, energies, 0)

        def offsets(a, b, group):
            first, last = max(0, -a), min(depth, depth - a)
            planes = sorted({c + k for c in group for k in range(3)})
            filtered = {}

            def emit(z):
                if not first <= z < last:
                    return
                lines = {c: [] for c in group}
                for i in range(blocks + 2):
                    v = {k: vals[k, z + a, i + b] for k in planes}
                    m = [cent[k, z, i] for k in range(3)]
                    for c in group:
                        lines[c].append(m[0] * v[c] + m[2] * v[c + 2] + m[1] * v[c + 1])
                filtered[z] = {
                    c: [three(*lines[c][i : i + 3]) for i in range(blocks)] for c in group
                }

            emit(0)
            for z in range(depth):
                emit(z + 1)
                for i in range(blocks):
                    weights = {}
                    for c in group:
                        parts = [filtered[y][c][i] for y in (z - 1, z + 1) if y in filtered]
                        if z in filtered:
                            parts.append(GAIN * filtered[z][c][i])
                        if -1 <= z + a <= depth:
                            parts.append(energy[c, z + a + 1, i + b])
                        if parts:
                            weights[c] = jnp.exp2(scale[z, i] * sum(parts[1:], parts[0]))
                        else:
                            weights[c] = jnp.ones((SUBS, LANES), jnp.float32)
                    t = top[z, i]
                    s = total[z, i]
                    for c in group:
                        t = jnp.maximum(t, weights[c])
                        s = s + weights[c]
                    top[z, i] = t
                    total[z, i] = s
                    if 0 <= z + a < depth:
                        w = weighted[z, i]
                        for c in group:
                            w = w + weights[c] * vals[c + 1, z + a, i + b + 1]
                        weighted[z, i] = w

        for a in range(-2, 3):

            def one(n, _, a=a):
                b = n + jnp.where(n >= 2, 1, 0) if a == 0 else n
                offsets(a, b, range(5))
                return 0

            lax.fori_loop(0, 4 if a == 0 else 5, one, 0)
        offsets(0, 2, (0, 1, 3, 4))

        def finish(z, _):
            for i in range(blocks):
                t = top[z, i]
                out[z, pl.ds(i, SUBS, stride=blocks), :] = (
                    weighted[z, i] + t * vals[3, z, i + 3]
                ) / (total[z, i] + t)
            return 0

        lax.fori_loop(0, depth, finish, 0)

    return kernel


def denoise(extended, strength):
    depth, size_x, size_y = strength.shape
    rows = size_x // lax.axis_size("off")
    blocks = rows // SUBS
    tall = -(-(rows + 6) // SUBS) * SUBS
    assert size_y == LANES
    start = lax.axis_index("off") * rows
    strength = lax.dynamic_slice_in_dim(strength, start, rows, 1)
    mine = lax.dynamic_slice_in_dim(extended, start, rows + 6, 1)
    mine = jnp.pad(mine, ((0, 0), (0, tall - rows - 6), (0, 0)))
    middle = mine[:, :, 3 : LANES + 3]
    sides = jnp.concatenate(
        [
            mine[:, :, LANES + 3 :],
            jnp.zeros((depth, tall, LANES - 6), jnp.float32),
            mine[:, :, :3],
        ],
        axis=2,
    )
    tile = (SUBS, LANES)
    f32 = jnp.float32
    return pl.pallas_call(
        make_kernel(depth, rows, blocks),
        out_shape=jax.ShapeDtypeStruct((depth, rows, size_y), f32),
        in_specs=[pl.BlockSpec(memory_space=pltpu.VMEM)] * 3,
        out_specs=pl.BlockSpec(memory_space=pltpu.VMEM),
        scratch_shapes=[
            pltpu.VMEM((7, tall, LANES), f32),
            pltpu.VMEM((7, depth, blocks + 6) + tile, f32),
            pltpu.VMEM((3, depth, blocks + 2) + tile, f32),
            pltpu.VMEM((5, depth + 2, blocks + 4) + tile, f32),
            pltpu.VMEM((depth, blocks) + tile, f32),
            pltpu.VMEM((depth, blocks) + tile, f32),
            pltpu.VMEM((depth, blocks) + tile, f32),
            pltpu.VMEM((depth, blocks) + tile, f32),
        ],
        compiler_params=pltpu.CompilerParams(vmem_limit_bytes=32 * 2**20),
    )(middle, sides, strength)


def shards(volume, strength):
    extended = with_halo(volume, (("gx", 1), ("gy", 2)), 3)
    part = denoise(extended, strength)
    return lax.all_gather(part, "off", axis=1, tiled=True)


def solution(mesh):
    return jax.shard_map(
        shards,
        mesh=mesh,
        in_specs=(P(None, "gx", "gy"), P(None, "gx", "gy")),
        out_specs=P(None, "gx", "gy"),
        check_vma=False,
    )
```

time: 443 us -> 49.8 us (0.11)
  waiting for transfers between devices: 154 us -> 7.46 us
  local copies, waits for them, and re-layouts: 146 us -> 3.21 us
  other arithmetic: 118 us -> 1.56 us
  blocking collectives: 0 us -> 16.4 us
  between operations: 13.3 us -> 0.11 us
  Pallas kernels: 0 us -> 12 us
    all_gather x3 -> x0, waiting for transfers between devices: 137 us -> none  [merged(): gathered = jax.tree.map(lambda a: lax.all_gather(a, axis), part)]
    gather x96 -> x0, local copies, waits for them, and re-layouts: 131 us -> none
    add x27 -> x0, other arithmetic: 35.3 us -> none  [the longest x8 17.2 us: one_turn(): totals[2] + jnp.sum(weighted_values, axis=0)]
    reduce_sum x8 -> x0, other arithmetic: 33.6 us -> none  [one_turn(): jnp.sum(weighted_values, axis=0)]
    mul x8 -> x0, other arithmetic: 28.1 us -> none  [patch_weight(): squares = difference * difference]
    max x11 -> x0, other arithmetic: 17.6 us -> none  [the longest x8 14.1 us: one_turn(): jnp.maximum(totals[0], jnp.max(weights, axis=0))]
    all_gather x0 -> x1, blocking collectives: none -> 16.4 us  [shards(): return lax.all_gather(part, 'off', axis=1, tiled=True)]
    pallas_call x0 -> x1, Pallas kernels: none -> 12 us  [denoise(): pl.pallas_call(make_kernel(depth, rows, blocks), out_shape=jax.ShapeDtype...]
  transfers between devices with their start and end apart: 7 -> 4, of which waited for: 6 -> 3; matrix products, arithmetic and copies ran while one was open for 1% -> 1% of each run, Pallas kernels for 0% -> 0%
where the time goes in v2:
time: 49.8 us; the launch traced here: 49.4 us
  blocking collectives  16.4 us (33%)
  Pallas kernels  12 us (24%)
  starting transfers between devices  8.74 us (18%)
  waiting for transfers between devices  7.46 us (15%)
  local copies, waits for them, and re-layouts  3.21 us (6%)
  other arithmetic  1.56 us (3%)
    all_gather x1, blocking collectives, shards(): return lax.all_gather(part, 'off', axis=1, tiled=True)  16.4 us
    pallas_call x1, Pallas kernels, denoise(): pl.pallas_call(make_kernel(depth, rows, blocks), out_shape=jax.ShapeDtype...  12 us
    ppermute x2, waiting for transfers between devices, with_halo(): lax.ppermute(head, axis, [((i + 1) % count, i) for i in range(ends)])  7.34 us
    ppermute x2, starting transfers between devices, with_halo(): lax.ppermute(tail, axis, [(i, (i + 1) % count) for i in range(ends)])  6.15 us
    ppermute x2, starting transfers between devices, with_halo(): lax.ppermute(head, axis, [((i + 1) % count, i) for i in range(ends)])  2.59 us
    concatenate x2, other arithmetic, with_halo(): jnp.concatenate([lax.ppermute(tail, axis, [(i, (i + 1) % count) for i in...  1.41 us
    slice x2, local copies, waits for them, and re-layouts, with_halo(): lax.slice_in_dim(cells, cells.shape[dim] - width, cells.shape[dim], axis=...  1.17 us
  transfers between devices with their start and end apart: 4, of which 3 were waited for; matrix products, arithmetic and copies ran while one was open for 1% of the time, Pallas kernels for 0%

profile of v2, /device:TPU:0, one launch (start us, length us, event | category | flops | bytes accessed | tf_op | source)
XLA Modules:
  0.0 49.4 jit_solution(10068569464660070675)
XLA Ops:
  0.0 0.0 copy-start
  0.0 0.8 %fusion.5 = (f32[8,3,128]{2,1,0:T(4,128)S(1)}, f32[8,3,128]{2,1,0:T(4,128)S(1)}) fusion(f32[8,128,128]{2,1,0:T(8,128)} %param.2), kind=kLoop, calls=%fused_computation.16 | loop fusion | bytes 49152 | tf_op jit(solution)/shard_map/slice | solution.py:22
  0.8 4.9 %collective-permute-start = (f32[8,3,128]{2,1,0:T(4,128)S(1)}, f32[8,3,128]{2,1,0:T(4,128)S(1)}, u32[]{:S(2)}, u32[]{:S(2)}) collective-permute-start(f32[8,3,128]{2,1,0:T(4,128)S(1)} %get-tuple-element.7), channel_id=1, source_target_pairs={{0,16},{1,17},{2,18},{3,19},{4,20},{5,21},{6,22},{7,23},{8,24},{9,... | collective-permute-start | bytes 36872 | tf_op jit(solution)/shard_map/ppermute | solution.py:25
  5.7 1.3 %collective-permute-start.1 = (f32[8,3,128]{2,1,0:T(4,128)S(1)}, f32[8,3,128]{2,1,0:T(4,128)S(1)}, u32[]{:S(2)}, u32[]{:S(2)}) collective-permute-start(f32[8,3,128]{2,1,0:T(4,128)S(1)} %get-tuple-element.8), channel_id=1, source_target_pairs={{16,0},{17,1},{18,2},{19,3},{20,4},{21,5},{22,6},{23,7},{24,8},{25... | collective-permute-start | bytes 36872 | tf_op jit(solution)/shard_map/ppermute | solution.py:27
  7.0 0.1 collective-permute-done
  7.1 4.2 %collective-permute-done.1 = f32[8,3,128]{2,1,0:T(4,128)S(1)} collective-permute-done((f32[8,3,128]{2,1,0:T(4,128)S(1)}, f32[8,3,128]{2,1,0:T(4,128)S(1)}, u32[]{:S(2)}, u32[]{:S(2)}) %collective-permute-start.1) | collective-permute-done | bytes 12320 | tf_op jit(solution)/shard_map/ppermute | solution.py:27
  11.3 1.1 %pad_maximum_fusion = f32[8,134,128]{2,1,0:T(8,128)S(1)} fusion(f32[8,3,128]{2,1,0:T(4,128)S(1)} %collective-permute-done.1, f32[8,128,128]{2,1,0:T(8,128)} %param.2, f32[8,3,128]{2,1,0:T(4,128)S(1)} %collective-permute-done), kind=kLoop, calls=%fused_computation.5 | loop fusion | flops 274432 | bytes 1097728 | tf_op jit(solution)/shard_map/concatenate | solution.py:23
  12.4 0.2 fusion.4
  12.6 0.3 copy.3
  13.0 1.3 %collective-permute-start.2 = (f32[8,134,3]{1,0,2:T(8,128)S(1)}, f32[8,134,3]{1,0,2:T(8,128)S(1)}, u32[]{:S(2)}, u32[]{:S(2)}) collective-permute-start(f32[8,134,3]{1,0,2:T(8,128)S(1)} %copy.3), channel_id=1, source_target_pairs={{0,4},{4,8},{8,12},{1,5},{5,9},{9,13},{2,6},{6,10},{10,14},{3,7},{... | collective-permute-start | bytes 38600 | tf_op jit(solution)/shard_map/ppermute | solution.py:25
  14.3 0.3 copy.4
  14.6 1.3 %collective-permute-start.3 = (f32[8,134,3]{1,0,2:T(8,128)S(1)}, f32[8,134,3]{1,0,2:T(8,128)S(1)}, u32[]{:S(2)}, u32[]{:S(2)}) collective-permute-start(f32[8,134,3]{1,0,2:T(8,128)S(1)} %copy.4), channel_id=1, source_target_pairs={{4,0},{8,4},{12,8},{5,1},{9,5},{13,9},{6,2},{10,6},{14,10},{7,3},{... | collective-permute-start | bytes 38600 | tf_op jit(solution)/shard_map/ppermute | solution.py:27
  15.9 0.0 copy-done
  16.0 0.1 pad.6.clone
  16.0 0.0 copy-start.1
  16.0 0.0 collective-permute-done.2
  16.0 0.2 copy.5
  16.3 3.1 %collective-permute-done.3 = f32[8,134,3]{1,0,2:T(8,128)S(1)} collective-permute-done((f32[8,134,3]{1,0,2:T(8,128)S(1)}, f32[8,134,3]{1,0,2:T(8,128)S(1)}, u32[]{:S(2)}, u32[]{:S(2)}) %collective-permute-start.3) | collective-permute-done | bytes 12896 | tf_op jit(solution)/shard_map/ppermute | solution.py:27
  19.4 0.2 copy.6
  19.7 0.0 copy-done.1
  19.7 0.3 fusion.1
  20.0 0.1 pad_slice_fusion.1
  20.1 0.2 pad_slice_fusion.2
  20.3 12.0 %shard_map.28 = f32[8,32,128]{2,1,0:T(8,128)S(1)} custom-call(f32[8,40,128]{2,1,0:T(8,128)S(1)} %get-tuple-element.11.middle, f32[8,40,128]{2,1,0:T(8,128)S(1)} %get-tuple-element.12.sides, f32[8,32,128]{2,1,0:T(8,128)S(1)} %constant_dynamic-slice_fusion.strength), custom_call_target="tpu_custom_call" | custom-call | tf_op jit(solution)/shard_map/pallas_call | solution.py:182
  32.3 16.4 %all_gather.3 = f32[8,128,128]{2,1,0:T(8,128)S(1)} all-gather(f32[8,32,128]{2,1,0:T(8,128)S(1)} %shard_map.28), channel_id=1, replica_groups=mesh['gx'=2,'gy'=4,'off'=4] {'off'}, dimensions={1}, use_global_device_ids=true | all-gather | bytes 655360 | tf_op jit(solution)/shard_map/all_gather | solution.py:204
  48.6 0.8 %copy.8 = f32[8,128,128]{2,1,0:T(8,128)} copy(f32[8,128,128]{2,1,0:T(8,128)S(1)} %all_gather.3) | data formatting | bytes 1048576
  (2 shorter events, 0.0 us)
Async XLA Ops:
  0.0 15.9 %copy-start = (f32[8,128,128]{2,1,0:T(8,128)S(1)}, f32[8,128,128]{2,1,0:T(8,128)}, u32[]{:S(2)}) copy-start(f32[8,128,128]{2,1,0:T(8,128)} %param.3) | copy-start | bytes 1572868
  0.8 6.3 %collective-permute-start = (f32[8,3,128]{2,1,0:T(4,128)S(1)}, f32[8,3,128]{2,1,0:T(4,128)S(1)}, u32[]{:S(2)}, u32[]{:S(2)}) collective-permute-start(f32[8,3,128]{2,1,0:T(4,128)S(1)} %get-tuple-element.7), channel_id=1, source_target_pairs={{0,16},{1,17},{2,18},{3,19},{4,20},{5,21},{6,22},{7,23},{8,24},{9,... | collective-permute-start | bytes 36872 | tf_op jit(solution)/shard_map/ppermute | solution.py:25
  5.7 5.6 %collective-permute-start.1 = (f32[8,3,128]{2,1,0:T(4,128)S(1)}, f32[8,3,128]{2,1,0:T(4,128)S(1)}, u32[]{:S(2)}, u32[]{:S(2)}) collective-permute-start(f32[8,3,128]{2,1,0:T(4,128)S(1)} %get-tuple-element.8), channel_id=1, source_target_pairs={{16,0},{17,1},{18,2},{19,3},{20,4},{21,5},{22,6},{23,7},{24,8},{25... | collective-permute-start | bytes 36872 | tf_op jit(solution)/shard_map/ppermute | solution.py:27
  13.0 3.1 %collective-permute-start.2 = (f32[8,134,3]{1,0,2:T(8,128)S(1)}, f32[8,134,3]{1,0,2:T(8,128)S(1)}, u32[]{:S(2)}, u32[]{:S(2)}) collective-permute-start(f32[8,134,3]{1,0,2:T(8,128)S(1)} %copy.3), channel_id=1, source_target_pairs={{0,4},{4,8},{8,12},{1,5},{5,9},{9,13},{2,6},{6,10},{10,14},{3,7},{... | collective-permute-start | bytes 38600 | tf_op jit(solution)/shard_map/ppermute | solution.py:25
  14.6 4.8 %collective-permute-start.3 = (f32[8,134,3]{1,0,2:T(8,128)S(1)}, f32[8,134,3]{1,0,2:T(8,128)S(1)}, u32[]{:S(2)}, u32[]{:S(2)}) collective-permute-start(f32[8,134,3]{1,0,2:T(8,128)S(1)} %copy.4), channel_id=1, source_target_pairs={{4,0},{8,4},{12,8},{5,1},{9,5},{13,9},{6,2},{10,6},{14,10},{7,3},{... | collective-permute-start | bytes 38600 | tf_op jit(solution)/shard_map/ppermute | solution.py:27
  16.0 3.6 %copy-start.1 = (f32[8,128,128]{2,1,0:T(8,128)S(1)}, f32[8,128,128]{2,1,0:T(8,128)}, u32[]{:S(2)}) copy-start(f32[8,128,128]{2,1,0:T(8,128)} %param.2) | copy-start | bytes 1572868

commit v3 on v2

--- a/solution.py
+++ b/solution.py
@@ -12,54 +12,103 @@
 SCALE = -(EDGE**3) * math.log2(math.e)
 LANES = 128
 SUBS = 8
-
-
-def with_halo(cells, sides, width):
-    for axis, dim in sides:
-        count = lax.axis_size(axis)
-        ends = count - 1
-        head = lax.slice_in_dim(cells, 0, width, axis=dim)
-        tail = lax.slice_in_dim(cells, cells.shape[dim] - width, cells.shape[dim], axis=dim)
-        cells = jnp.concatenate(
-            [
-                lax.ppermute(tail, axis, [(i, (i + 1) % count) for i in range(ends)]),
-                cells,
-                lax.ppermute(head, axis, [((i + 1) % count, i) for i in range(ends)]),
-            ],
-            axis=dim,
-        )
-    return cells
+VMEM = pl.BlockSpec(memory_space=pltpu.VMEM)
+
+
+def partners(count):
+    assert count % 2 == 0
+    first = [i ^ 1 for i in range(count)]
+    second = [(((i + 1) ^ 1) - 1) % count for i in range(count)]
+    return first, second
+
+
+def pack_kernel(rows):
+    blocks = rows // SUBS + 2
+
+    def kernel(volume, strips, corner, layer):
+        depth, size_x, _ = volume.shape
+        off = lax.axis_index("off")
+        lane = lax.broadcasted_iota(jnp.int32, (SUBS, LANES), 1)
+        place = (lane + 3) % LANES
+
+        def packed(start):
+            line = jnp.zeros((SUBS, LANES), jnp.float32)
+            for z in range(depth):
+                v = volume[z, pl.ds(start, SUBS), :]
+                v = pltpu.roll(v, 16 * z, 1) if z else v
+                line = jnp.where((place >= 16 * z) & (place < 16 * z + 6), v, line)
+            return line
+
+        for j in range(blocks):
+            at = jnp.clip(off * rows + SUBS * (j - 1), 0, size_x - SUBS)
+            strips[pl.ds(SUBS * j, SUBS), :] = packed(pl.multiple_of(at, SUBS))
+        at = pl.multiple_of(jnp.where(off == 0, size_x - SUBS, 0), SUBS)
+        corner[...] = packed(at)
+        for z in range(depth):
+            layer[z] = volume[z, pl.ds(at, SUBS), :]
+
+    return kernel
 
 
 def make_kernel(depth, rows, blocks):
     wide = blocks + 6
-    tall = -(-(rows + 6) // SUBS)
-
-    def kernel(middle, sides, strength, out, flat, vals, cent, energy, scale, top, total, weighted):
+    tall = rows // SUBS + 2
+
+    def kernel(
+        volume, strength, layer, near, far, near_corner, far_corner,
+        out, flat, vals, cent, energy, scale, top, total, weighted,
+    ):
         lane = lax.broadcasted_iota(jnp.int32, (SUBS, LANES), 1)
+        size_x = volume.shape[1]
+        off, offs = lax.axis_index("off"), lax.axis_size("off")
+        gx, gxs = lax.axis_index("gx"), lax.axis_size("gx")
+        gy, gys = lax.axis_index("gy"), lax.axis_size("gy")
+        start = off * rows
+        odd = gy % 2 == 1
+        outer = lane % 16 >= 13
+        closed = (outer & (gy == 0)) | ((lane % 16 < 3) & (gy == gys - 1))
+        from_near = outer == odd
+        ends = {0: (off == 0, gx == 0), tall - 1: (off == offs - 1, gx == gxs - 1)}
+
+        def side(j):
+            at = pl.ds(SUBS * j, SUBS)
+            line = jnp.where(from_near, near[at, :], far[at, :])
+            if j in ends:
+                corner = jnp.where(from_near, near_corner[...], far_corner[...])
+                corner = jnp.where(ends[j][1], 0.0, corner)
+                line = jnp.where(ends[j][0], corner, line)
+            return jnp.where(closed, 0.0, line)
+
+        lines = [side(j) for j in range(tall)]
 
         def fill(z, _):
             for r in range(tall):
                 at = pl.ds(SUBS * r, SUBS)
-                v, h = middle[z, at, :], sides[z, at, :]
+                here = jnp.clip(start + SUBS * (r - 1), 0, size_x - SUBS)
+                v = volume[z, pl.ds(pl.multiple_of(here, SUBS), SUBS), :]
+                if r in ends:
+                    v = jnp.where(ends[r][0], jnp.where(ends[r][1], 0.0, layer[z]), v)
+                h = pltpu.roll(lines[r], LANES - 16 * z, 1)
                 flat[3, at, :] = v
                 for c in range(1, 4):
                     flat[3 + c, at, :] = pltpu.roll(jnp.where(lane < c, h, v), LANES - c, 1)
                     flat[3 - c, at, :] = pltpu.roll(jnp.where(lane >= LANES - c, h, v), c, 1)
             for i in range(wide):
                 for c in range(7):
-                    v = flat[c, pl.ds(i, SUBS, stride=blocks), :]
+                    v = flat[c, pl.ds(SUBS - 3 + i, SUBS, stride=blocks), :]
                     vals[c, z, i] = v
                     if 2 <= c <= 4 and 2 <= i < wide - 2:
                         cent[c - 2, z, i - 2] = (-2.0 * GAIN if c == 3 else -2.0) * v
             for i in range(blocks):
-                scale[z, i] = SCALE / strength[z, pl.ds(i, SUBS, stride=blocks), :]
+                s = strength[z, pl.ds(start + i, SUBS, stride=blocks), :]
+                scale[z, i] = SCALE / s
                 top[z, i] = jnp.zeros((SUBS, LANES), jnp.float32)
                 total[z, i] = jnp.zeros((SUBS, LANES), jnp.float32)
                 weighted[z, i] = jnp.zeros((SUBS, LANES), jnp.float32)
             return 0
 
-        lax.fori_loop(0, depth, fill, 0)
+        for z in range(depth):
+            fill(z, 0)
 
         def three(a, b, c):
             return a + c + GAIN * b
@@ -158,32 +207,48 @@
     return kernel
 
 
-def denoise(extended, strength):
+def denoise(volume, strength):
     depth, size_x, size_y = strength.shape
-    rows = size_x // lax.axis_size("off")
+    sizes = {axis: lax.axis_size(axis) for axis in ("gx", "gy", "off")}
+    gxs, gys, offs = sizes["gx"], sizes["gy"], sizes["off"]
+    rows = size_x // offs
     blocks = rows // SUBS
-    tall = -(-(rows + 6) // SUBS) * SUBS
-    assert size_y == LANES
-    start = lax.axis_index("off") * rows
-    strength = lax.dynamic_slice_in_dim(strength, start, rows, 1)
-    mine = lax.dynamic_slice_in_dim(extended, start, rows + 6, 1)
-    mine = jnp.pad(mine, ((0, 0), (0, tall - rows - 6), (0, 0)))
-    middle = mine[:, :, 3 : LANES + 3]
-    sides = jnp.concatenate(
-        [
-            mine[:, :, LANES + 3 :],
-            jnp.zeros((depth, tall, LANES - 6), jnp.float32),
-            mine[:, :, :3],
-        ],
-        axis=2,
-    )
+    tall = rows + 2 * SUBS
+    assert size_y == LANES and offs > 1
     tile = (SUBS, LANES)
     f32 = jnp.float32
+    strips, corner, layer = pl.pallas_call(
+        pack_kernel(rows),
+        out_shape=[
+            jax.ShapeDtypeStruct((tall, LANES), f32),
+            jax.ShapeDtypeStruct(tile, f32),
+            jax.ShapeDtypeStruct((depth,) + tile, f32),
+        ],
+        in_specs=[VMEM],
+        out_specs=[VMEM] * 3,
+    )(volume)
+
+    def across(swap):
+        moves = []
+        for x in range(gxs):
+            for y in range(gys):
+                for k in range(offs):
+                    to = (x + (1 if k == 0 else -1)) % gxs
+                    moves.append(((x * gys + y) * offs + k, (to * gys + swap[y]) * offs + k))
+        return moves
+
+    axes = ("gx", "gy", "off")
+    first, second = partners(gys)
+    near = lax.ppermute(strips, "gy", list(enumerate(first)))
+    far = lax.ppermute(strips, "gy", list(enumerate(second)))
+    layer = lax.ppermute(layer, axes, across(list(range(gys))))
+    near_corner = lax.ppermute(corner, axes, across(first))
+    far_corner = lax.ppermute(corner, axes, across(second))
     return pl.pallas_call(
         make_kernel(depth, rows, blocks),
         out_shape=jax.ShapeDtypeStruct((depth, rows, size_y), f32),
-        in_specs=[pl.BlockSpec(memory_space=pltpu.VMEM)] * 3,
-        out_specs=pl.BlockSpec(memory_space=pltpu.VMEM),
+        in_specs=[VMEM] * 7,
+        out_specs=VMEM,
         scratch_shapes=[
             pltpu.VMEM((7, tall, LANES), f32),
             pltpu.VMEM((7, depth, blocks + 6) + tile, f32),
@@ -195,13 +260,24 @@
             pltpu.VMEM((depth, blocks) + tile, f32),
         ],
         compiler_params=pltpu.CompilerParams(vmem_limit_bytes=32 * 2**20),
-    )(middle, sides, strength)
+    )(volume, strength, layer, near, far, near_corner, far_corner)
+
+
+def gathered(part):
+    depth, rows, size_y = part.shape
+    count = lax.axis_size("off")
+    off = lax.axis_index("off")
+    whole = jnp.zeros((count, depth, rows, size_y), part.dtype)
+    whole = lax.dynamic_update_slice(whole, part[None], (off, 0, 0, 0))
+    for step in range(1, count):
+        moves = [(i, i ^ step) for i in range(count)]
+        other = lax.ppermute(part, "off", moves)
+        whole = lax.dynamic_update_slice(whole, other[None], (off ^ step, 0, 0, 0))
+    return jnp.swapaxes(whole, 0, 1).reshape(depth, count * rows, size_y)
 
 
 def shards(volume, strength):
-    extended = with_halo(volume, (("gx", 1), ("gy", 2)), 3)
-    part = denoise(extended, strength)
-    return lax.all_gather(part, "off", axis=1, tiled=True)
+    return gathered(denoise(volume, strength))
 
 
 def solution(mesh):

time: 49.8 us -> 40.5 us (0.81)
  blocking collectives: 16.4 us -> 0 us
  waiting for transfers between devices: 7.46 us -> 12.3 us
  Pallas kernels: 12 us -> 15.2 us
  starting transfers between devices: 8.74 us -> 10.7 us
  other arithmetic: 1.56 us -> 0 us
  local copies, waits for them, and re-layouts: 3.21 us -> 1.97 us
    all_gather x1 -> x0, blocking collectives: 16.4 us -> none  [shards(): return lax.all_gather(part, 'off', axis=1, tiled=True)]
    ppermute x4 -> x8, waiting for transfers between devices: 7.46 us -> 12.3 us  [the longest x3 9.99 us: gathered(): other = lax.ppermute(part, 'off', moves)]
    ppermute x4 -> x8, starting transfers between devices: 8.74 us -> 10.7 us  [the longest x3 4.45 us: gathered(): other = lax.ppermute(part, 'off', moves)]
    pallas_call x0 -> x1, Pallas kernels: none -> 1.86 us  [denoise(): pl.pallas_call(pack_kernel(rows), out_shape=[jax.ShapeDtypeStruct((tall,...]
    slice x5 -> x0, local copies, waits for them, and re-layouts: 1.81 us -> none  [the longest x2 1.17 us: with_halo(): lax.slice_in_dim(cells, cells.shape[dim] - width, cells.shape[dim], axis=...]
    concatenate x2 -> x0, other arithmetic: 1.41 us -> none  [with_halo(): jnp.concatenate([lax.ppermute(tail, axis, [(i, (i + 1) % count) for i in...]
    pallas_call x1, Pallas kernels: 12 us -> 13.3 us  [denoise(): pl.pallas_call(make_kernel(depth, rows, blocks), out_shape=jax.ShapeDtype...]
    unnamed x5 -> x8, local copies, waits for them, and re-layouts: 0.8 us -> 1.83 us
  transfers between devices with their start and end apart: 4 -> 8, of which waited for: 3 -> 4; matrix products, arithmetic and copies ran while one was open for 1% -> 0% of each run, Pallas kernels for 0% -> 0%
where the time goes in v3:
time: 40.5 us; the launch traced here: 40.3 us
  Pallas kernels  15.2 us (38%)
  waiting for transfers between devices  12.3 us (30%)
  starting transfers between devices  10.7 us (26%)
  local copies, waits for them, and re-layouts  1.97 us (5%)
    pallas_call x1, Pallas kernels, denoise(): pl.pallas_call(make_kernel(depth, rows, blocks), out_shape=jax.ShapeDtype...  13.3 us
    ppermute x3, waiting for transfers between devices, gathered(): other = lax.ppermute(part, 'off', moves)  9.99 us
    ppermute x3, starting transfers between devices, gathered(): other = lax.ppermute(part, 'off', moves)  4.45 us
    ppermute x1, starting transfers between devices, denoise(): layer = lax.ppermute(layer, axes, across(list(range(gys))))  2.97 us
    pallas_call x1, Pallas kernels, denoise(): pl.pallas_call(pack_kernel(rows), out_shape=[jax.ShapeDtypeStruct((tall,...  1.86 us
    unnamed x8, local copies, waits for them, and re-layouts  1.83 us
    ppermute x1, starting transfers between devices, denoise(): far = lax.ppermute(strips, 'gy', list(enumerate(second)))  1.6 us
    ppermute x1, starting transfers between devices, denoise(): far_corner = lax.ppermute(corner, axes, across(second))  1.6 us
  transfers between devices with their start and end apart: 8, of which 4 were waited for; matrix products, arithmetic and copies ran while one was open for 0% of the time, Pallas kernels for 0%

profile of v3, /device:TPU:0, one launch (start us, length us, event | category | flops | bytes accessed | tf_op | source)
XLA Modules:
  0.0 40.3 jit_solution(10232303687806795803)
XLA Ops:
  0.0 0.0 copy-start
  0.0 1.9 %shard_map.28 = (f32[48,128]{1,0:T(8,128)}, f32[8,128]{1,0:T(8,128)}, f32[8,8,128]{2,1,0:T(8,128)}) custom-call(f32[8,128,128]{2,1,0:T(8,128)} %volume.3), custom_call_target="tpu_custom_call" | custom-call | tf_op jit(solution)/shard_map/pallas_call | solution.py:220
  1.9 0.0 copy-start.3
  1.9 3.0 %collective-permute-start = (f32[8,8,128]{2,1,0:T(8,128)}, f32[8,8,128]{2,1,0:T(8,128)S(1)}, u32[]{:S(2)}, u32[]{:S(2)}) collective-permute-start(f32[8,8,128]{2,1,0:T(8,128)} %get-tuple-element.8), channel_id=1, source_target_pairs={{0,16},{1,17},{2,18},{3,19},{4,20},{5,21},{6,22},{7,23},{8,24},{9,... | collective-permute-start | bytes 98312 | tf_op jit(solution)/shard_map/ppermute | solution.py:244
  4.8 0.0 collective-permute-start.1
  4.8 1.6 %collective-permute-start.2 = (f32[48,128]{1,0:T(8,128)}, f32[48,128]{1,0:T(8,128)S(1)}, u32[]{:S(2)}, u32[]{:S(2)}) collective-permute-start(f32[48,128]{1,0:T(8,128)} %get-tuple-element.9), channel_id=1, source_target_pairs={{0,12},{4,8},{8,4},{12,0},{1,13},{5,9},{9,5},{13,1},{2,14},{6,10},... | collective-permute-start | bytes 73736 | tf_op jit(solution)/shard_map/ppermute | solution.py:243
  6.4 0.0 copy-done.3
  6.4 0.1 collective-permute-start.3
  6.6 1.6 %collective-permute-start.4 = (f32[8,128]{1,0:T(8,128)S(1)}, f32[8,128]{1,0:T(8,128)S(1)}, u32[]{:S(2)}, u32[]{:S(2)}) collective-permute-start(f32[8,128]{1,0:T(8,128)S(1)} %copy-done.3), channel_id=1, source_target_pairs={{0,28},{1,29},{2,30},{3,31},{4,24},{5,25},{6,26},{7,27},{8,20},{9,... | collective-permute-start | bytes 12296 | tf_op jit(solution)/shard_map/ppermute | solution.py:246
  8.2 1.3 %collective-permute-done.3.near_corner = f32[8,128]{1,0:T(8,128)S(1)} collective-permute-done((f32[8,128]{1,0:T(8,128)S(1)}, f32[8,128]{1,0:T(8,128)S(1)}, u32[]{:S(2)}, u32[]{:S(2)}) %collective-permute-start.3) | collective-permute-done | bytes 4128 | tf_op jit(solution)/shard_map/ppermute | solution.py:245
  9.5 1.0 %collective-permute-done.4.far_corner = f32[8,128]{1,0:T(8,128)S(1)} collective-permute-done((f32[8,128]{1,0:T(8,128)S(1)}, f32[8,128]{1,0:T(8,128)S(1)}, u32[]{:S(2)}, u32[]{:S(2)}) %collective-permute-start.4) | collective-permute-done | bytes 4128 | tf_op jit(solution)/shard_map/ppermute | solution.py:246
  10.5 0.0 collective-permute-done.1.near
  10.5 0.0 collective-permute-done.2.far
  10.5 0.0 collective-permute-done.layer
  10.5 0.0 copy-done
  10.5 0.0 copy-start.1
  10.5 1.0 %copy-done.1 = f32[8,128,128]{2,1,0:T(8,128)S(1)} copy-done((f32[8,128,128]{2,1,0:T(8,128)S(1)}, f32[8,128,128]{2,1,0:T(8,128)}, u32[]{:S(2)}) %copy-start.1) | copy-done | bytes 524312
  11.6 13.3 %shard_map.29 = f32[8,32,128]{2,1,0:T(8,128)S(1)} custom-call(f32[8,128,128]{2,1,0:T(8,128)S(1)} %copy-done, f32[8,128,128]{2,1,0:T(8,128)S(1)} %copy-done.1, f32[8,8,128]{2,1,0:T(8,128)S(1)} %collective-permute-done.layer, f32[48,128]{1,0:T(8,128)S(1)} %collective-permute-done.1.near, f32[48,128]{1,0:T(8,128)S(1)} %collective-permute-done.2.far, ...), custom_call_target="tpu_custom_call" | custom-call | tf_op jit(solution)/shard_map/pallas_call | solution.py:247
  24.9 1.6 %collective-permute-start.5 = (f32[8,32,128]{2,1,0:T(8,128)S(1)}, f32[8,32,128]{2,1,0:T(8,128)S(1)}, u32[]{:S(2)}, u32[]{:S(2)}) collective-permute-start(f32[8,32,128]{2,1,0:T(8,128)S(1)} %shard_map.29), channel_id=1, source_target_pairs={{0,1},{1,0},{2,3},{3,2},{4,5},{5,4},{6,7},{7,6},{8,9},{9,8},{10,11... | collective-permute-start | bytes 393224 | tf_op jit(solution)/shard_map/ppermute | solution.py:274
  26.5 2.6 %collective-permute-start.6 = (f32[8,32,128]{2,1,0:T(8,128)S(1)}, f32[8,32,128]{2,1,0:T(8,128)S(1)}, u32[]{:S(2)}, u32[]{:S(2)}) collective-permute-start(f32[8,32,128]{2,1,0:T(8,128)S(1)} %shard_map.29), channel_id=1, source_target_pairs={{0,2},{1,3},{2,0},{3,1},{4,6},{5,7},{6,4},{7,5},{8,10},{9,11},{10,... | collective-permute-start | bytes 393224 | tf_op jit(solution)/shard_map/ppermute | solution.py:274
  29.1 0.2 collective-permute-start.7
  29.4 3.8 %collective-permute-done.5 = f32[8,32,128]{2,1,0:T(8,128)S(1)} collective-permute-done((f32[8,32,128]{2,1,0:T(8,128)S(1)}, f32[8,32,128]{2,1,0:T(8,128)S(1)}, u32[]{:S(2)}, u32[]{:S(2)}) %collective-permute-start.5) | collective-permute-done | bytes 131104 | tf_op jit(solution)/shard_map/ppermute | solution.py:274
  33.2 6.2 %collective-permute-done.6 = f32[8,32,128]{2,1,0:T(8,128)S(1)} collective-permute-done((f32[8,32,128]{2,1,0:T(8,128)S(1)}, f32[8,32,128]{2,1,0:T(8,128)S(1)}, u32[]{:S(2)}, u32[]{:S(2)}) %collective-permute-start.6) | collective-permute-done | bytes 131104 | tf_op jit(solution)/shard_map/ppermute | solution.py:274
  39.5 0.0 collective-permute-done.7
  39.5 0.0 copy-start.2
  39.5 0.8 %copy-done.2 = f32[4,8,32,128]{3,2,0,1:T(8,128)} copy-done((f32[4,8,32,128]{3,2,0,1:T(8,128)}, f32[4,8,32,128]{3,2,0,1:T(8,128)S(1)}, u32[]{:S(2)}) %copy-start.2) | copy-done | bytes 524312
  (6 shorter events, 0.1 us)
Async XLA Ops:
  0.0 10.5 %copy-start = (f32[8,128,128]{2,1,0:T(8,128)S(1)}, f32[8,128,128]{2,1,0:T(8,128)}, u32[]{:S(2)}) copy-start(f32[8,128,128]{2,1,0:T(8,128)} %volume.3) | copy-start | bytes 1572868
  1.9 4.6 %copy-start.3 = (f32[8,128]{1,0:T(8,128)S(1)}, f32[8,128]{1,0:T(8,128)}, u32[]{:S(2)}) copy-start(f32[8,128]{1,0:T(8,128)} %get-tuple-element.10) | copy-start | bytes 12292
  1.9 8.6 %collective-permute-start = (f32[8,8,128]{2,1,0:T(8,128)}, f32[8,8,128]{2,1,0:T(8,128)S(1)}, u32[]{:S(2)}, u32[]{:S(2)}) collective-permute-start(f32[8,8,128]{2,1,0:T(8,128)} %get-tuple-element.8), channel_id=1, source_target_pairs={{0,16},{1,17},{2,18},{3,19},{4,20},{5,21},{6,22},{7,23},{8,24},{9,... | collective-permute-start | bytes 98312 | tf_op jit(solution)/shard_map/ppermute | solution.py:244
  4.8 5.7 %collective-permute-start.1 = (f32[48,128]{1,0:T(8,128)}, f32[48,128]{1,0:T(8,128)S(1)}, u32[]{:S(2)}, u32[]{:S(2)}) collective-permute-start(f32[48,128]{1,0:T(8,128)} %get-tuple-element.9), channel_id=1, source_target_pairs={{0,4},{4,0},{8,12},{12,8},{1,5},{5,1},{9,13},{13,9},{2,6},{6,2},{1... | collective-permute-start | bytes 73736 | tf_op jit(solution)/shard_map/ppermute | solution.py:242
  4.8 5.7 %collective-permute-start.2 = (f32[48,128]{1,0:T(8,128)}, f32[48,128]{1,0:T(8,128)S(1)}, u32[]{:S(2)}, u32[]{:S(2)}) collective-permute-start(f32[48,128]{1,0:T(8,128)} %get-tuple-element.9), channel_id=1, source_target_pairs={{0,12},{4,8},{8,4},{12,0},{1,13},{5,9},{9,5},{13,1},{2,14},{6,10},... | collective-permute-start | bytes 73736 | tf_op jit(solution)/shard_map/ppermute | solution.py:243
  6.4 3.0 %collective-permute-start.3 = (f32[8,128]{1,0:T(8,128)S(1)}, f32[8,128]{1,0:T(8,128)S(1)}, u32[]{:S(2)}, u32[]{:S(2)}) collective-permute-start(f32[8,128]{1,0:T(8,128)S(1)} %copy-done.3), channel_id=1, source_target_pairs={{0,20},{1,21},{2,22},{3,23},{4,16},{5,17},{6,18},{7,19},{8,28},{9,... | collective-permute-start | bytes 12296 | tf_op jit(solution)/shard_map/ppermute | solution.py:245
  6.6 3.9 %collective-permute-start.4 = (f32[8,128]{1,0:T(8,128)S(1)}, f32[8,128]{1,0:T(8,128)S(1)}, u32[]{:S(2)}, u32[]{:S(2)}) collective-permute-start(f32[8,128]{1,0:T(8,128)S(1)} %copy-done.3), channel_id=1, source_target_pairs={{0,28},{1,29},{2,30},{3,31},{4,24},{5,25},{6,26},{7,27},{8,20},{9,... | collective-permute-start | bytes 12296 | tf_op jit(solution)/shard_map/ppermute | solution.py:246
  10.5 1.0 %copy-start.1 = (f32[8,128,128]{2,1,0:T(8,128)S(1)}, f32[8,128,128]{2,1,0:T(8,128)}, u32[]{:S(2)}) copy-start(f32[8,128,128]{2,1,0:T(8,128)} %strength.1) | copy-start | bytes 1572868
  24.9 8.3 %collective-permute-start.5 = (f32[8,32,128]{2,1,0:T(8,128)S(1)}, f32[8,32,128]{2,1,0:T(8,128)S(1)}, u32[]{:S(2)}, u32[]{:S(2)}) collective-permute-start(f32[8,32,128]{2,1,0:T(8,128)S(1)} %shard_map.29), channel_id=1, source_target_pairs={{0,1},{1,0},{2,3},{3,2},{4,5},{5,4},{6,7},{7,6},{8,9},{9,8},{10,11... | collective-permute-start | bytes 393224 | tf_op jit(solution)/shard_map/ppermute | solution.py:274
  26.5 12.9 %collective-permute-start.6 = (f32[8,32,128]{2,1,0:T(8,128)S(1)}, f32[8,32,128]{2,1,0:T(8,128)S(1)}, u32[]{:S(2)}, u32[]{:S(2)}) collective-permute-start(f32[8,32,128]{2,1,0:T(8,128)S(1)} %shard_map.29), channel_id=1, source_target_pairs={{0,2},{1,3},{2,0},{3,1},{4,6},{5,7},{6,4},{7,5},{8,10},{9,11},{10,... | collective-permute-start | bytes 393224 | tf_op jit(solution)/shard_map/ppermute | solution.py:274
  29.1 10.4 %collective-permute-start.7 = (f32[8,32,128]{2,1,0:T(8,128)S(1)}, f32[8,32,128]{2,1,0:T(8,128)S(1)}, u32[]{:S(2)}, u32[]{:S(2)}) collective-permute-start(f32[8,32,128]{2,1,0:T(8,128)S(1)} %shard_map.29), channel_id=1, source_target_pairs={{0,3},{1,2},{2,1},{3,0},{4,7},{5,6},{6,5},{7,4},{8,11},{9,10},{10,... | collective-permute-start | bytes 393224 | tf_op jit(solution)/shard_map/ppermute | solution.py:274
  39.5 0.8 %copy-start.2 = (f32[4,8,32,128]{3,2,0,1:T(8,128)}, f32[4,8,32,128]{3,2,0,1:T(8,128)S(1)}, u32[]{:S(2)}) copy-start(f32[4,8,32,128]{3,2,0,1:T(8,128)S(1)} %bitcast_dynamic-update-slice_fusion) | copy-start | bytes 1572868

commit v4 on v3

--- a/solution.py
+++ b/solution.py
@@ -50,20 +50,26 @@
     return kernel
 
 
-def make_kernel(depth, rows, blocks):
+def three(a, b, c):
+    return a + c + GAIN * b
+
+
+def prepare_kernel(depth, rows, blocks, slices):
     wide = blocks + 6
     tall = rows // SUBS + 2
 
     def kernel(
         volume, strength, layer, near, far, near_corner, far_corner,
-        out, flat, vals, cent, energy, scale, top, total, weighted,
+        out, vals, cent, energy, scale, flat, mine, arrived, *sums,
     ):
         lane = lax.broadcasted_iota(jnp.int32, (SUBS, LANES), 1)
         size_x = volume.shape[1]
         off, offs = lax.axis_index("off"), lax.axis_size("off")
         gx, gxs = lax.axis_index("gx"), lax.axis_size("gx")
         gy, gys = lax.axis_index("gy"), lax.axis_size("gy")
-        start = off * rows
+        start = pl.multiple_of(off * rows, rows)
+        fetch = pltpu.make_async_copy(strength.at[:, pl.ds(start, rows), :], mine, arrived)
+        fetch.start()
         odd = gy % 2 == 1
         outer = lane % 16 >= 13
         closed = (outer & (gy == 0)) | ((lane % 16 < 3) & (gy == gys - 1))
@@ -81,7 +87,7 @@
 
         lines = [side(j) for j in range(tall)]
 
-        def fill(z, _):
+        def fill(z):
             for r in range(tall):
                 at = pl.ds(SUBS * r, SUBS)
                 here = jnp.clip(start + SUBS * (r - 1), 0, size_x - SUBS)
@@ -99,19 +105,9 @@
                     vals[c, z, i] = v
                     if 2 <= c <= 4 and 2 <= i < wide - 2:
                         cent[c - 2, z, i - 2] = (-2.0 * GAIN if c == 3 else -2.0) * v
-            for i in range(blocks):
-                s = strength[z, pl.ds(start + i, SUBS, stride=blocks), :]
-                scale[z, i] = SCALE / s
-                top[z, i] = jnp.zeros((SUBS, LANES), jnp.float32)
-                total[z, i] = jnp.zeros((SUBS, LANES), jnp.float32)
-                weighted[z, i] = jnp.zeros((SUBS, LANES), jnp.float32)
-            return 0
 
         for z in range(depth):
-            fill(z, 0)
-
-        def three(a, b, c):
-            return a + c + GAIN * b
+            fill(z)
 
         def energies(c, _):
             count = blocks + 4
@@ -138,73 +134,86 @@
 
         lax.fori_loop(0, 5, energies, 0)
 
-        def offsets(a, b, group):
-            first, last = max(0, -a), min(depth, depth - a)
-            planes = sorted({c + k for c in group for k in range(3)})
-            filtered = {}
-
-            def emit(z):
-                if not first <= z < last:
-                    return
-                lines = {c: [] for c in group}
-                for i in range(blocks + 2):
-                    v = {k: vals[k, z + a, i + b] for k in planes}
-                    m = [cent[k, z, i] for k in range(3)]
+        fetch.wait()
+        for z in range(depth):
+            for i in range(blocks):
+                scale[z, i] = SCALE / mine[z, pl.ds(i, SUBS, stride=blocks), :]
+
+        weigh(depth, blocks, slices, vals, cent, energy, scale, out, *sums)
+
+    return kernel
+
+
+def weigh(depth, blocks, slices, vals, cent, energy, scale, out, top, total, weighted):
+    begin, end = slices
+    for z in range(end - begin):
+        for i in range(blocks):
+            for ref in (top, total, weighted):
+                ref[z, i] = jnp.zeros((SUBS, LANES), jnp.float32)
+
+    def offsets(a, b, group):
+        first, last = max(0, -a, begin - 1), min(depth, depth - a, end + 1)
+        planes = sorted({c + k for c in group for k in range(3)})
+        filtered = {}
+
+        def emit(z):
+            if not first <= z < last:
+                return
+            lines = {c: [] for c in group}
+            for i in range(blocks + 2):
+                v = {k: vals[k, z + a, i + b] for k in planes}
+                m = [cent[k, z, i] for k in range(3)]
+                for c in group:
+                    lines[c].append(m[0] * v[c] + m[2] * v[c + 2] + m[1] * v[c + 1])
+            filtered[z] = {
+                c: [three(*lines[c][i : i + 3]) for i in range(blocks)] for c in group
+            }
+
+        emit(begin - 1)
+        emit(begin)
+        for z in range(begin, end):
+            emit(z + 1)
+            for i in range(blocks):
+                weights = {}
+                for c in group:
+                    parts = [filtered[y][c][i] for y in (z - 1, z + 1) if y in filtered]
+                    if z in filtered:
+                        parts.append(GAIN * filtered[z][c][i])
+                    if -1 <= z + a <= depth:
+                        parts.append(energy[c, z + a + 1, i + b])
+                    if parts:
+                        weights[c] = jnp.exp2(scale[z, i] * sum(parts[1:], parts[0]))
+                    else:
+                        weights[c] = jnp.ones((SUBS, LANES), jnp.float32)
+                t = top[z - begin, i]
+                s = total[z - begin, i]
+                for c in group:
+                    t = jnp.maximum(t, weights[c])
+                    s = s + weights[c]
+                top[z - begin, i] = t
+                total[z - begin, i] = s
+                if 0 <= z + a < depth:
+                    w = weighted[z - begin, i]
                     for c in group:
-                        lines[c].append(m[0] * v[c] + m[2] * v[c + 2] + m[1] * v[c + 1])
-                filtered[z] = {
-                    c: [three(*lines[c][i : i + 3]) for i in range(blocks)] for c in group
-                }
-
-            emit(0)
-            for z in range(depth):
-                emit(z + 1)
-                for i in range(blocks):
-                    weights = {}
-                    for c in group:
-                        parts = [filtered[y][c][i] for y in (z - 1, z + 1) if y in filtered]
-                        if z in filtered:
-                            parts.append(GAIN * filtered[z][c][i])
-                        if -1 <= z + a <= depth:
-                            parts.append(energy[c, z + a + 1, i + b])
-                        if parts:
-                            weights[c] = jnp.exp2(scale[z, i] * sum(parts[1:], parts[0]))
-                        else:
-                            weights[c] = jnp.ones((SUBS, LANES), jnp.float32)
-                    t = top[z, i]
-                    s = total[z, i]
-                    for c in group:
-                        t = jnp.maximum(t, weights[c])
-                        s = s + weights[c]
-                    top[z, i] = t
-                    total[z, i] = s
-                    if 0 <= z + a < depth:
-                        w = weighted[z, i]
-                        for c in group:
-                            w = w + weights[c] * vals[c + 1, z + a, i + b + 1]
-                        weighted[z, i] = w
-
-        for a in range(-2, 3):
-
-            def one(n, _, a=a):
-                b = n + jnp.where(n >= 2, 1, 0) if a == 0 else n
-                offsets(a, b, range(5))
-                return 0
-
-            lax.fori_loop(0, 4 if a == 0 else 5, one, 0)
-        offsets(0, 2, (0, 1, 3, 4))
-
-        def finish(z, _):
-            for i in range(blocks):
-                t = top[z, i]
-                out[z, pl.ds(i, SUBS, stride=blocks), :] = (
-                    weighted[z, i] + t * vals[3, z, i + 3]
-                ) / (total[z, i] + t)
+                        w = w + weights[c] * vals[c + 1, z + a, i + b + 1]
+                    weighted[z - begin, i] = w
+
+    for a in range(-2, 3):
+
+        def one(n, _, a=a):
+            b = n + jnp.where(n >= 2, 1, 0) if a == 0 else n
+            offsets(a, b, range(5))
             return 0
 
-        lax.fori_loop(0, depth, finish, 0)
-
-    return kernel
+        lax.fori_loop(0, 4 if a == 0 else 5, one, 0)
+    offsets(0, 2, (0, 1, 3, 4))
+
+    for z in range(end - begin):
+        for i in range(blocks):
+            t = top[z, i]
+            out[z, pl.ds(i, SUBS, stride=blocks), :] = (
+                weighted[z, i] + t * vals[3, z + begin, i + 3]
+            ) / (total[z, i] + t)
 
 
 def denoise(volume, strength):
@@ -244,35 +253,62 @@
     layer = lax.ppermute(layer, axes, across(list(range(gys))))
     near_corner = lax.ppermute(corner, axes, across(first))
     far_corner = lax.ppermute(corner, axes, across(second))
-    return pl.pallas_call(
-        make_kernel(depth, rows, blocks),
-        out_shape=jax.ShapeDtypeStruct((depth, rows, size_y), f32),
-        in_specs=[VMEM] * 7,
-        out_specs=VMEM,
+    half = depth // 2
+    limit = 16 * 2**20
+    prepared = [
+        jax.ShapeDtypeStruct((7, depth, blocks + 6) + tile, f32),
+        jax.ShapeDtypeStruct((3, depth, blocks + 2) + tile, f32),
+        jax.ShapeDtypeStruct((5, depth + 2, blocks + 4) + tile, f32),
+        jax.ShapeDtypeStruct((depth, blocks) + tile, f32),
+    ]
+
+    def sums(slices):
+        return [pltpu.VMEM((slices, blocks) + tile, f32)] * 3
+
+    head, *prepared = pl.pallas_call(
+        prepare_kernel(depth, rows, blocks, (0, half)),
+        out_shape=[jax.ShapeDtypeStruct((half, rows, size_y), f32)] + prepared,
+        in_specs=[VMEM, pl.BlockSpec(memory_space=pl.ANY)] + [VMEM] * 5,
+        out_specs=[VMEM] * 5,
         scratch_shapes=[
             pltpu.VMEM((7, tall, LANES), f32),
-            pltpu.VMEM((7, depth, blocks + 6) + tile, f32),
-            pltpu.VMEM((3, depth, blocks + 2) + tile, f32),
-            pltpu.VMEM((5, depth + 2, blocks + 4) + tile, f32),
-            pltpu.VMEM((depth, blocks) + tile, f32),
-            pltpu.VMEM((depth, blocks) + tile, f32),
-            pltpu.VMEM((depth, blocks) + tile, f32),
-            pltpu.VMEM((depth, blocks) + tile, f32),
-        ],
-        compiler_params=pltpu.CompilerParams(vmem_limit_bytes=32 * 2**20),
+            pltpu.VMEM((depth, rows, LANES), f32),
+            pltpu.SemaphoreType.DMA,
+        ]
+        + sums(half),
+        compiler_params=pltpu.CompilerParams(vmem_limit_bytes=limit),
     )(volume, strength, layer, near, far, near_corner, far_corner)
 
-
-def gathered(part):
-    depth, rows, size_y = part.shape
+    def second_kernel(vals, cent, energy, scale, out, *sums):
+        weigh(depth, blocks, (half, depth), vals, cent, energy, scale, out, *sums)
+
+    work = 124 * 20 * (depth - half) * rows * size_y
+    tail = pl.pallas_call(
+        second_kernel,
+        out_shape=jax.ShapeDtypeStruct((depth - half, rows, size_y), f32),
+        in_specs=[VMEM] * 4,
+        out_specs=VMEM,
+        scratch_shapes=sums(depth - half),
+        compiler_params=pltpu.CompilerParams(vmem_limit_bytes=limit),
+        cost_estimate=pl.CostEstimate(flops=work, bytes_accessed=work // 2, transcendentals=0),
+    )(*prepared)
+    return head, tail
+
+
+def gathered(parts):
     count = lax.axis_size("off")
     off = lax.axis_index("off")
-    whole = jnp.zeros((count, depth, rows, size_y), part.dtype)
-    whole = lax.dynamic_update_slice(whole, part[None], (off, 0, 0, 0))
-    for step in range(1, count):
-        moves = [(i, i ^ step) for i in range(count)]
-        other = lax.ppermute(part, "off", moves)
-        whole = lax.dynamic_update_slice(whole, other[None], (off ^ step, 0, 0, 0))
+    rows, size_y = parts[0].shape[1:]
+    depth = sum(part.shape[0] for part in parts)
+    whole = jnp.zeros((count, depth, rows, size_y), parts[0].dtype)
+    z = 0
+    for part in parts:
+        whole = lax.dynamic_update_slice(whole, part[None], (off, z, 0, 0))
+        for step in range(1, count):
+            moves = [(i, i ^ step) for i in range(count)]
+            other = lax.ppermute(part, "off", moves)
+            whole = lax.dynamic_update_slice(whole, other[None], (off ^ step, z, 0, 0))
+        z += part.shape[0]
     return jnp.swapaxes(whole, 0, 1).reshape(depth, count * rows, size_y)
 
 

time: 40.5 us -> 43.7 us (1.079)
  starting transfers between devices: 10.7 us -> 15.3 us
  waiting for transfers between devices: 12.3 us -> 8.22 us
  Pallas kernels: 15.2 us -> 16.8 us
  local copies, waits for them, and re-layouts: 1.97 us -> 3.03 us
    ppermute x3 -> x6, starting transfers between devices: 4.45 us -> 8.97 us  [gathered(): other = lax.ppermute(part, 'off', moves)]
    ppermute x3 -> x6, waiting for transfers between devices: 9.99 us -> 5.68 us  [gathered(): other = lax.ppermute(part, 'off', moves)]
    pallas_call x1 -> x2, Pallas kernels: 13.3 us -> 15.1 us  [the longest x1 9.03 us: denoise(): pl.pallas_call(prepare_kernel(depth, rows, blocks, (0, half)), out_shape=...]
    unnamed x8 -> x6, local copies, waits for them, and re-layouts: 1.83 us -> 2.87 us
  transfers between devices with their start and end apart: 8 -> 11, of which waited for: 4 -> 4; matrix products, arithmetic and copies ran while one was open for 0% -> 0% of each run, Pallas kernels for 0% -> 14%
where the time goes in v4:
time: 43.7 us; the launch traced here: 43.5 us
  Pallas kernels  16.8 us (38%)
  starting transfers between devices  15.3 us (35%)
  waiting for transfers between devices  8.22 us (19%)
  local copies, waits for them, and re-layouts  3.03 us (7%)
    pallas_call x1, Pallas kernels, denoise(): pl.pallas_call(prepare_kernel(depth, rows, blocks, (0, half)), out_shape=...  9.03 us
    ppermute x6, starting transfers between devices, gathered(): other = lax.ppermute(part, 'off', moves)  8.97 us
    pallas_call x1, Pallas kernels, denoise(): pl.pallas_call(second_kernel, out_shape=jax.ShapeDtypeStruct((depth - hal...  6.03 us
    ppermute x6, waiting for transfers between devices, gathered(): other = lax.ppermute(part, 'off', moves)  5.68 us
    ppermute x1, starting transfers between devices, denoise(): layer = lax.ppermute(layer, axes, across(list(range(gys))))  2.97 us
    unnamed x6, local copies, waits for them, and re-layouts  2.87 us
    pallas_call x1, Pallas kernels, denoise(): pl.pallas_call(pack_kernel(rows), out_shape=[jax.ShapeDtypeStruct((tall,...  1.78 us
    ppermute x1, starting transfers between devices, denoise(): far = lax.ppermute(strips, 'gy', list(enumerate(second)))  1.6 us
  transfers between devices with their start and end apart: 11, of which 4 were waited for; matrix products, arithmetic and copies ran while one was open for 0% of the time, Pallas kernels for 14%

profile of v4, /device:TPU:0, one launch (start us, length us, event | category | flops | bytes accessed | tf_op | source)
XLA Modules:
  0.0 43.5 jit_solution(4901152204459409249)
XLA Ops:
  0.0 1.8 %shard_map.28 = (f32[48,128]{1,0:T(8,128)}, f32[8,128]{1,0:T(8,128)}, f32[8,8,128]{2,1,0:T(8,128)}) custom-call(f32[8,128,128]{2,1,0:T(8,128)} %volume.3), custom_call_target="tpu_custom_call" | custom-call | tf_op jit(solution)/shard_map/pallas_call | solution.py:229
  1.8 3.0 %collective-permute-start = (f32[8,8,128]{2,1,0:T(8,128)}, f32[8,8,128]{2,1,0:T(8,128)S(1)}, u32[]{:S(2)}, u32[]{:S(2)}) collective-permute-start(f32[8,8,128]{2,1,0:T(8,128)} %get-tuple-element.13), channel_id=1, source_target_pairs={{0,16},{1,17},{2,18},{3,19},{4,20},{5,21},{6,22},{7,23},{8,24},{9,... | collective-permute-start | bytes 98312 | tf_op jit(solution)/shard_map/ppermute | solution.py:253
  4.8 0.0 collective-permute-start.1
  4.8 1.6 %collective-permute-start.2 = (f32[48,128]{1,0:T(8,128)}, f32[48,128]{1,0:T(8,128)S(1)}, u32[]{:S(2)}, u32[]{:S(2)}) collective-permute-start(f32[48,128]{1,0:T(8,128)} %get-tuple-element.14), channel_id=1, source_target_pairs={{0,12},{4,8},{8,4},{12,0},{1,13},{5,9},{9,5},{13,1},{2,14},{6,10},... | collective-permute-start | bytes 73736 | tf_op jit(solution)/shard_map/ppermute | solution.py:252
  6.4 0.1 collective-permute-start.3
  6.5 1.6 %collective-permute-start.4 = (f32[8,128]{1,0:T(8,128)}, f32[8,128]{1,0:T(8,128)S(1)}, u32[]{:S(2)}, u32[]{:S(2)}) collective-permute-start(f32[8,128]{1,0:T(8,128)} %get-tuple-element.15), channel_id=1, source_target_pairs={{0,28},{1,29},{2,30},{3,31},{4,24},{5,25},{6,26},{7,27},{8,20},{9,... | collective-permute-start | bytes 12296 | tf_op jit(solution)/shard_map/ppermute | solution.py:255
  8.1 1.5 %collective-permute-done.3.near_corner = f32[8,128]{1,0:T(8,128)S(1)} collective-permute-done((f32[8,128]{1,0:T(8,128)}, f32[8,128]{1,0:T(8,128)S(1)}, u32[]{:S(2)}, u32[]{:S(2)}) %collective-permute-start.3) | collective-permute-done | bytes 4128 | tf_op jit(solution)/shard_map/ppermute | solution.py:254
  9.6 1.0 %collective-permute-done.4.far_corner = f32[8,128]{1,0:T(8,128)S(1)} collective-permute-done((f32[8,128]{1,0:T(8,128)}, f32[8,128]{1,0:T(8,128)S(1)}, u32[]{:S(2)}, u32[]{:S(2)}) %collective-permute-start.4) | collective-permute-done | bytes 4128 | tf_op jit(solution)/shard_map/ppermute | solution.py:255
  10.6 0.0 collective-permute-done.1.near
  10.6 0.0 collective-permute-done.2.far
  10.6 0.0 collective-permute-done.layer
  10.6 0.0 copy-start
  10.6 1.0 %copy-done = f32[8,128,128]{2,1,0:T(8,128)S(1)} copy-done((f32[8,128,128]{2,1,0:T(8,128)S(1)}, f32[8,128,128]{2,1,0:T(8,128)}, u32[]{:S(2)}) %copy-start) | copy-done | bytes 524312
  11.7 0.0 copy-start.1
  11.7 1.0 %copy-done.1 = f32[8,128,128]{2,1,0:T(8,128)S(1)} copy-done((f32[8,128,128]{2,1,0:T(8,128)S(1)}, f32[8,128,128]{2,1,0:T(8,128)}, u32[]{:S(2)}) %copy-start.1) | copy-done | bytes 524312
  12.7 9.0 %shard_map.29 = (f32[4,32,128]{2,1,0:T(8,128)S(1)}, f32[7,8,10,8,128]{4,3,2,1,0:T(8,128)S(1)}, f32[3,8,6,8,128]{4,3,2,1,0:T(8,128)S(1)}, f32[5,10,8,8,128]{4,3,2,1,0:T(8,128)S(1)}, f32[8,4,8,128]{3,2,1,0:T(8,128)S(1)}) custom-call(f32[8,128,128]{2,1,0:T(8,128)S(1)} %copy-done, f32[8,128,128]{2,1,0:T(8,128)S(1)} %copy-done.1, ...), custom_call_target="tpu_custom_call" | custom-call | tf_op jit(solution)/shard_map/pallas_call | solution.py:268
  21.8 1.6 %collective-permute-start.5 = (f32[4,32,128]{2,1,0:T(8,128)S(1)}, f32[4,32,128]{2,1,0:T(8,128)S(1)}, u32[]{:S(2)}, u32[]{:S(2)}) collective-permute-start(f32[4,32,128]{2,1,0:T(8,128)S(1)} %get-tuple-element.16), channel_id=1, source_target_pairs={{0,1},{1,0},{2,3},{3,2},{4,5},{5,4},{6,7},{7,6},{8,9},{9,8},{10,11... | collective-permute-start | bytes 196616 | tf_op jit(solution)/shard_map/ppermute | solution.py:309
  23.4 2.6 %collective-permute-start.6 = (f32[4,32,128]{2,1,0:T(8,128)S(1)}, f32[4,32,128]{2,1,0:T(8,128)S(1)}, u32[]{:S(2)}, u32[]{:S(2)}) collective-permute-start(f32[4,32,128]{2,1,0:T(8,128)S(1)} %get-tuple-element.16), channel_id=1, source_target_pairs={{0,2},{1,3},{2,0},{3,1},{4,6},{5,7},{6,4},{7,5},{8,10},{9,11},{10,... | collective-permute-start | bytes 196616 | tf_op jit(solution)/shard_map/ppermute | solution.py:309
  26.0 0.2 collective-permute-start.7
  26.2 6.0 %shard_map.30 = f32[4,32,128]{2,1,0:T(8,128)S(1)} custom-call(f32[7,8,10,8,128]{4,3,2,1,0:T(8,128)S(1)} %get-tuple-element.17.vals, f32[3,8,6,8,128]{4,3,2,1,0:T(8,128)S(1)} %get-tuple-element.18.cent, f32[5,10,8,8,128]{4,3,2,1,0:T(8,128)S(1)} %get-tuple-element.19.energy, f32[8,4,8,128]{3,2,1,0:T(8,128)S(1)} %get-tuple-element.20.scale), custom_call_target="tpu_custom_call" | custom-call | flops 40632320 | bytes 20316160 | tf_op jit(solution)/shard_map/pallas_call | solution.py:286
  32.2 0.7 %collective-permute-start.8 = (f32[4,32,128]{2,1,0:T(8,128)S(1)}, f32[4,32,128]{2,1,0:T(8,128)S(1)}, u32[]{:S(2)}, u32[]{:S(2)}) collective-permute-start(f32[4,32,128]{2,1,0:T(8,128)S(1)} %shard_map.30), channel_id=1, source_target_pairs={{0,1},{1,0},{2,3},{3,2},{4,5},{5,4},{6,7},{7,6},{8,9},{9,8},{10,11... | collective-permute-start | bytes 196616 | tf_op jit(solution)/shard_map/ppermute | solution.py:309
  33.0 3.5 %collective-permute-start.9 = (f32[4,32,128]{2,1,0:T(8,128)S(1)}, f32[4,32,128]{2,1,0:T(8,128)S(1)}, u32[]{:S(2)}, u32[]{:S(2)}) collective-permute-start(f32[4,32,128]{2,1,0:T(8,128)S(1)} %shard_map.30), channel_id=1, source_target_pairs={{0,2},{1,3},{2,0},{3,1},{4,6},{5,7},{6,4},{7,5},{8,10},{9,11},{10,... | collective-permute-start | bytes 196616 | tf_op jit(solution)/shard_map/ppermute | solution.py:309
  36.5 0.0 collective-permute-done.5
  36.6 0.3 collective-permute-start.10
  36.9 0.0 collective-permute-done.6
  36.9 0.0 collective-permute-done.7
  36.9 0.0 collective-permute-done.8
  37.0 3.2 %collective-permute-done.9 = f32[4,32,128]{2,1,0:T(8,128)S(1)} collective-permute-done((f32[4,32,128]{2,1,0:T(8,128)S(1)}, f32[4,32,128]{2,1,0:T(8,128)S(1)}, u32[]{:S(2)}, u32[]{:S(2)}) %collective-permute-start.9) | collective-permute-done | bytes 65568 | tf_op jit(solution)/shard_map/ppermute | solution.py:309
  40.2 2.5 %collective-permute-done.10 = f32[4,32,128]{2,1,0:T(8,128)S(1)} collective-permute-done((f32[4,32,128]{2,1,0:T(8,128)S(1)}, f32[4,32,128]{2,1,0:T(8,128)S(1)}, u32[]{:S(2)}, u32[]{:S(2)}) %collective-permute-start.10) | collective-permute-done | bytes 65568 | tf_op jit(solution)/shard_map/ppermute | solution.py:309
  42.7 0.0 copy-start.2
  42.7 0.8 %copy-done.2 = f32[4,8,32,128]{3,2,0,1:T(8,128)} copy-done((f32[4,8,32,128]{3,2,0,1:T(8,128)}, f32[4,8,32,128]{3,2,0,1:T(8,128)S(1)}, u32[]{:S(2)}) %copy-start.2) | copy-done | bytes 524312
  (10 shorter events, 0.2 us)
Async XLA Ops:
  1.8 8.8 %collective-permute-start = (f32[8,8,128]{2,1,0:T(8,128)}, f32[8,8,128]{2,1,0:T(8,128)S(1)}, u32[]{:S(2)}, u32[]{:S(2)}) collective-permute-start(f32[8,8,128]{2,1,0:T(8,128)} %get-tuple-element.13), channel_id=1, source_target_pairs={{0,16},{1,17},{2,18},{3,19},{4,20},{5,21},{6,22},{7,23},{8,24},{9,... | collective-permute-start | bytes 98312 | tf_op jit(solution)/shard_map/ppermute | solution.py:253
  4.8 5.9 %collective-permute-start.1 = (f32[48,128]{1,0:T(8,128)}, f32[48,128]{1,0:T(8,128)S(1)}, u32[]{:S(2)}, u32[]{:S(2)}) collective-permute-start(f32[48,128]{1,0:T(8,128)} %get-tuple-element.14), channel_id=1, source_target_pairs={{0,4},{4,0},{8,12},{12,8},{1,5},{5,1},{9,13},{13,9},{2,6},{6,2},{1... | collective-permute-start | bytes 73736 | tf_op jit(solution)/shard_map/ppermute | solution.py:251
  4.8 5.9 %collective-permute-start.2 = (f32[48,128]{1,0:T(8,128)}, f32[48,128]{1,0:T(8,128)S(1)}, u32[]{:S(2)}, u32[]{:S(2)}) collective-permute-start(f32[48,128]{1,0:T(8,128)} %get-tuple-element.14), channel_id=1, source_target_pairs={{0,12},{4,8},{8,4},{12,0},{1,13},{5,9},{9,5},{13,1},{2,14},{6,10},... | collective-permute-start | bytes 73736 | tf_op jit(solution)/shard_map/ppermute | solution.py:252
  6.4 3.2 %collective-permute-start.3 = (f32[8,128]{1,0:T(8,128)}, f32[8,128]{1,0:T(8,128)S(1)}, u32[]{:S(2)}, u32[]{:S(2)}) collective-permute-start(f32[8,128]{1,0:T(8,128)} %get-tuple-element.15), channel_id=1, source_target_pairs={{0,20},{1,21},{2,22},{3,23},{4,16},{5,17},{6,18},{7,19},{8,28},{9,... | collective-permute-start | bytes 12296 | tf_op jit(solution)/shard_map/ppermute | solution.py:254
  6.5 4.1 %collective-permute-start.4 = (f32[8,128]{1,0:T(8,128)}, f32[8,128]{1,0:T(8,128)S(1)}, u32[]{:S(2)}, u32[]{:S(2)}) collective-permute-start(f32[8,128]{1,0:T(8,128)} %get-tuple-element.15), channel_id=1, source_target_pairs={{0,28},{1,29},{2,30},{3,31},{4,24},{5,25},{6,26},{7,27},{8,20},{9,... | collective-permute-start | bytes 12296 | tf_op jit(solution)/shard_map/ppermute | solution.py:255
  10.6 1.0 %copy-start = (f32[8,128,128]{2,1,0:T(8,128)S(1)}, f32[8,128,128]{2,1,0:T(8,128)}, u32[]{:S(2)}) copy-start(f32[8,128,128]{2,1,0:T(8,128)} %volume.3) | copy-start | bytes 1572868
  11.7 1.0 %copy-start.1 = (f32[8,128,128]{2,1,0:T(8,128)S(1)}, f32[8,128,128]{2,1,0:T(8,128)}, u32[]{:S(2)}) copy-start(f32[8,128,128]{2,1,0:T(8,128)} %strength.1) | copy-start | bytes 1572868
  21.8 14.8 %collective-permute-start.5 = (f32[4,32,128]{2,1,0:T(8,128)S(1)}, f32[4,32,128]{2,1,0:T(8,128)S(1)}, u32[]{:S(2)}, u32[]{:S(2)}) collective-permute-start(f32[4,32,128]{2,1,0:T(8,128)S(1)} %get-tuple-element.16), channel_id=1, source_target_pairs={{0,1},{1,0},{2,3},{3,2},{4,5},{5,4},{6,7},{7,6},{8,9},{9,8},{10,11... | collective-permute-start | bytes 196616 | tf_op jit(solution)/shard_map/ppermute | solution.py:309
  23.4 13.5 %collective-permute-start.6 = (f32[4,32,128]{2,1,0:T(8,128)S(1)}, f32[4,32,128]{2,1,0:T(8,128)S(1)}, u32[]{:S(2)}, u32[]{:S(2)}) collective-permute-start(f32[4,32,128]{2,1,0:T(8,128)S(1)} %get-tuple-element.16), channel_id=1, source_target_pairs={{0,2},{1,3},{2,0},{3,1},{4,6},{5,7},{6,4},{7,5},{8,10},{9,11},{10,... | collective-permute-start | bytes 196616 | tf_op jit(solution)/shard_map/ppermute | solution.py:309
  26.0 10.9 %collective-permute-start.7 = (f32[4,32,128]{2,1,0:T(8,128)S(1)}, f32[4,32,128]{2,1,0:T(8,128)S(1)}, u32[]{:S(2)}, u32[]{:S(2)}) collective-permute-start(f32[4,32,128]{2,1,0:T(8,128)S(1)} %get-tuple-element.16), channel_id=1, source_target_pairs={{0,3},{1,2},{2,1},{3,0},{4,7},{5,6},{6,5},{7,4},{8,11},{9,10},{10,... | collective-permute-start | bytes 196616 | tf_op jit(solution)/shard_map/ppermute | solution.py:309
  32.2 4.7 %collective-permute-start.8 = (f32[4,32,128]{2,1,0:T(8,128)S(1)}, f32[4,32,128]{2,1,0:T(8,128)S(1)}, u32[]{:S(2)}, u32[]{:S(2)}) collective-permute-start(f32[4,32,128]{2,1,0:T(8,128)S(1)} %shard_map.30), channel_id=1, source_target_pairs={{0,1},{1,0},{2,3},{3,2},{4,5},{5,4},{6,7},{7,6},{8,9},{9,8},{10,11... | collective-permute-start | bytes 196616 | tf_op jit(solution)/shard_map/ppermute | solution.py:309
  33.0 7.2 %collective-permute-start.9 = (f32[4,32,128]{2,1,0:T(8,128)S(1)}, f32[4,32,128]{2,1,0:T(8,128)S(1)}, u32[]{:S(2)}, u32[]{:S(2)}) collective-permute-start(f32[4,32,128]{2,1,0:T(8,128)S(1)} %shard_map.30), channel_id=1, source_target_pairs={{0,2},{1,3},{2,0},{3,1},{4,6},{5,7},{6,4},{7,5},{8,10},{9,11},{10,... | collective-permute-start | bytes 196616 | tf_op jit(solution)/shard_map/ppermute | solution.py:309
  36.6 6.1 %collective-permute-start.10 = (f32[4,32,128]{2,1,0:T(8,128)S(1)}, f32[4,32,128]{2,1,0:T(8,128)S(1)}, u32[]{:S(2)}, u32[]{:S(2)}) collective-permute-start(f32[4,32,128]{2,1,0:T(8,128)S(1)} %shard_map.30), channel_id=1, source_target_pairs={{0,3},{1,2},{2,1},{3,0},{4,7},{5,6},{6,5},{7,4},{8,11},{9,10},{10,... | collective-permute-start | bytes 196616 | tf_op jit(solution)/shard_map/ppermute | solution.py:309
  42.7 0.8 %copy-start.2 = (f32[4,8,32,128]{3,2,0,1:T(8,128)}, f32[4,8,32,128]{3,2,0,1:T(8,128)S(1)}, u32[]{:S(2)}) copy-start(f32[4,8,32,128]{3,2,0,1:T(8,128)S(1)} %bitcast_dynamic-update-slice_fusion) | copy-start | bytes 1572868

commit v5 on v4

v5 whole, which is shorter than its diff:
```python
import math

import jax
import jax.numpy as jnp
from jax import lax
from jax.experimental import pallas as pl
from jax.experimental.pallas import tpu as pltpu
from jax.sharding import PartitionSpec as P

EDGE = math.exp(-0.5) / (1.0 + 2.0 * math.exp(-0.5))
GAIN = math.exp(0.5)
SCALE = -(EDGE**3) * math.log2(math.e)
LANES = 128
SUBS = 8
VMEM = pl.BlockSpec(memory_space=pltpu.VMEM)


def partners(count):
    assert count % 2 == 0
    first = [i ^ 1 for i in range(count)]
    second = [(((i + 1) ^ 1) - 1) % count for i in range(count)]
    return first, second


def packed(slices, lane):
    place = (lane + 3) % LANES
    line = jnp.zeros((SUBS, LANES), jnp.float32)
    for z, v in enumerate(slices):
        v = pltpu.roll(v, 16 * z, 1) if z else v
        line = jnp.where((place >= 16 * z) & (place < 16 * z + 6), v, line)
    return line


def lanes():
    return lax.broadcasted_iota(jnp.int32, (SUBS, LANES), 1)


def layer_kernel(volume, layer, arrived):
    off, size_x = lax.axis_index("off"), volume.shape[1]
    at = pl.multiple_of(jnp.where(off == 0, size_x - SUBS, 0), SUBS)
    copy = pltpu.make_async_copy(volume.at[:, pl.ds(at, SUBS), :], layer, arrived)
    copy.start()
    copy.wait()


def window(off, rows, size_x):
    begin = pl.multiple_of(jnp.clip(off * rows - SUBS, 0, size_x - rows - 2 * SUBS), SUBS)

    def block(j):
        at = jnp.clip(off * rows + SUBS * (j - 1), 0, size_x - SUBS) - begin
        return pl.ds(pl.multiple_of(at, SUBS), SUBS)

    return begin, block


def pack_kernel(rows, size_x):
    blocks = rows // SUBS

    def kernel(volume, strength, strips, mine, scale, local, arrived):
        depth = volume.shape[0]
        off = lax.axis_index("off")
        begin, block = window(off, rows, size_x)
        first = pltpu.make_async_copy(
            volume.at[:, pl.ds(begin, rows + 2 * SUBS), :], mine, arrived.at[0]
        )
        start = pl.multiple_of(off * rows, SUBS)
        second = pltpu.make_async_copy(
            strength.at[:, pl.ds(start, rows), :], local, arrived.at[1]
        )
        first.start()
        second.start()
        lane = lanes()
        first.wait()
        for j in range(blocks + 2):
            strips[pl.ds(SUBS * j, SUBS), :] = packed(
                [mine[z, block(j), :] for z in range(depth)], lane
            )
        second.wait()
        for z in range(depth):
            for i in range(blocks):
                scale[z, i] = SCALE / local[z, pl.ds(i, SUBS, stride=blocks), :]

    return kernel


def edges(tall):
    off, offs = lax.axis_index("off"), lax.axis_size("off")
    gx, gxs = lax.axis_index("gx"), lax.axis_size("gx")
    return {0: (off == 0, gx == 0), tall - 1: (off == offs - 1, gx == gxs - 1)}


def join_kernel(strips, layer, joined):
    depth, tall = layer.shape[0], strips.shape[0] // SUBS
    line = packed([layer[z] for z in range(depth)], lanes())
    for j in range(tall):
        at = pl.ds(SUBS * j, SUBS)
        value = strips[at, :]
        for end, (outside, beyond) in edges(tall).items():
            if j == end:
                value = jnp.where(outside, jnp.where(beyond, 0.0, line), value)
        joined[at, :] = value


def three(a, b, c):
    return a + c + GAIN * b


def main_kernel(depth, rows, blocks, size_x):
    wide = blocks + 6
    tall = rows // SUBS + 2

    def kernel(mine, scale, layer, near, far, out, flat, vals, cent, energy, *sums):
        lane = lanes()
        _, block = window(lax.axis_index("off"), rows, size_x)
        gy, gys = lax.axis_index("gy"), lax.axis_size("gy")
        outer = lane % 16 >= 13
        closed = (outer & (gy == 0)) | ((lane % 16 < 3) & (gy == gys - 1))
        from_near = outer == (gy % 2 == 1)
        ends = edges(tall)

        def side(j):
            at = pl.ds(SUBS * j, SUBS)
            return jnp.where(closed, 0.0, jnp.where(from_near, near[at, :], far[at, :]))

        lines = [side(j) for j in range(tall)]

        def fill(z):
            for r in range(tall):
                at = pl.ds(SUBS * r, SUBS)
                v = mine[z, block(r), :]
                if r in ends:
                    v = jnp.where(ends[r][0], jnp.where(ends[r][1], 0.0, layer[z]), v)
                h = pltpu.roll(lines[r], LANES - 16 * z, 1)
                flat[3, at, :] = v
                for c in range(1, 4):
                    flat[3 + c, at, :] = pltpu.roll(jnp.where(lane < c, h, v), LANES - c, 1)
                    flat[3 - c, at, :] = pltpu.roll(jnp.where(lane >= LANES - c, h, v), c, 1)
            for i in range(wide):
                for c in range(7):
                    v = flat[c, pl.ds(SUBS - 3 + i, SUBS, stride=blocks), :]
                    vals[c, z, i] = v
                    if 2 <= c <= 4 and 2 <= i < wide - 2:
                        cent[c - 2, z, i - 2] = (-2.0 * GAIN if c == 3 else -2.0) * v

        for z in range(depth):
            fill(z)

        def energies(c, _):
            count = blocks + 4
            filtered = []

            def store(z):
                for i in range(count):
                    e = GAIN * filtered[z][i] if 0 <= z < depth else None
                    for y in (z - 1, z + 1):
                        if 0 <= y < depth:
                            e = filtered[y][i] if e is None else e + filtered[y][i]
                    energy[c, z + 1, i] = e

            for z in range(depth):
                line = []
                for i in range(wide):
                    u, v, w = (vals[c + k, z, i] for k in range(3))
                    line.append(three(u * u, v * v, w * w))
                filtered.append([three(*line[i : i + 3]) for i in range(count)])
                store(z - 1)
            store(depth - 1)
            store(depth)
            return 0

        lax.fori_loop(0, 5, energies, 0)

        weigh(depth, blocks, vals, cent, energy, scale, out, *sums)

    return kernel


def weigh(depth, blocks, vals, cent, energy, scale, out, top, total, weighted):
    begin, end = 0, depth
    for z in range(end - begin):
        for i in range(blocks):
            for ref in (top, total, weighted):
                ref[z, i] = jnp.zeros((SUBS, LANES), jnp.float32)

    def offsets(a, b, group):
        first, last = max(0, -a, begin - 1), min(depth, depth - a, end + 1)
        planes = sorted({c + k for c in group for k in range(3)})
        filtered = {}

        def emit(z):
            if not first <= z < last:
                return
            lines = {c: [] for c in group}
            for i in range(blocks + 2):
                v = {k: vals[k, z + a, i + b] for k in planes}
                m = [cent[k, z, i] for k in range(3)]
                for c in group:
                    lines[c].append(m[0] * v[c] + m[2] * v[c + 2] + m[1] * v[c + 1])
            filtered[z] = {
                c: [three(*lines[c][i : i + 3]) for i in range(blocks)] for c in group
            }

        emit(begin - 1)
        emit(begin)
        for z in range(begin, end):
            emit(z + 1)
            for i in range(blocks):
                weights = {}
                for c in group:
                    parts = [filtered[y][c][i] for y in (z - 1, z + 1) if y in filtered]
                    if z in filtered:
                        parts.append(GAIN * filtered[z][c][i])
                    if -1 <= z + a <= depth:
                        parts.append(energy[c, z + a + 1, i + b])
                    if parts:
                        weights[c] = jnp.exp2(scale[z, i] * sum(parts[1:], parts[0]))
                    else:
                        weights[c] = jnp.ones((SUBS, LANES), jnp.float32)
                t = top[z - begin, i]
                s = total[z - begin, i]
                for c in group:
                    t = jnp.maximum(t, weights[c])
                    s = s + weights[c]
                top[z - begin, i] = t
                total[z - begin, i] = s
                if 0 <= z + a < depth:
                    w = weighted[z - begin, i]
                    for c in group:
                        w = w + weights[c] * vals[c + 1, z + a, i + b + 1]
                    weighted[z - begin, i] = w

    for a in range(-2, 3):

        def one(n, _, a=a):
            b = n + jnp.where(n >= 2, 1, 0) if a == 0 else n
            offsets(a, b, range(5))
            return 0

        lax.fori_loop(0, 4 if a == 0 else 5, one, 0)
    offsets(0, 2, (0, 1, 3, 4))

    for z in range(end - begin):
        for i in range(blocks):
            t = top[z, i]
            out[z, pl.ds(i, SUBS, stride=blocks), :] = (
                weighted[z, i] + t * vals[3, z + begin, i + 3]
            ) / (total[z, i] + t)


def place_kernel(part, off, *refs):
    *_, out, done = refs
    rows = part.shape[1]
    at = pl.ds(pl.multiple_of(off[0] * rows, SUBS), rows)
    copy = pltpu.make_async_copy(part, out.at[:, at, :], done)
    copy.start()
    copy.wait()


def shards(volume, strength):
    depth, size_x, size_y = strength.shape
    gxs, gys, offs = (lax.axis_size(axis) for axis in ("gx", "gy", "off"))
    rows = size_x // offs
    blocks = rows // SUBS
    tall = rows + 2 * SUBS
    assert size_y == LANES and offs > 1
    tile = (SUBS, LANES)
    f32 = jnp.float32
    HBM = pl.BlockSpec(memory_space=pltpu.HBM)

    small = pltpu.CompilerParams(vmem_limit_bytes=4 * 2**20)

    def shape(*sizes):
        return jax.ShapeDtypeStruct(sizes, f32)

    layer = pl.pallas_call(
        layer_kernel,
        out_shape=shape(depth, *tile),
        in_specs=[HBM],
        out_specs=VMEM,
        scratch_shapes=[pltpu.SemaphoreType.DMA],
    )(volume)
    moves = []
    for x in range(gxs):
        for k in range(offs):
            to = (x + (1 if k == 0 else -1)) % gxs
            moves.append((x * offs + k, to * offs + k))
    layer = lax.ppermute(layer, ("gx", "off"), moves)
    strips, mine, scale = pl.pallas_call(
        pack_kernel(rows, size_x),
        out_shape=[shape(tall, LANES), shape(depth, tall, LANES), shape(depth, blocks, *tile)],
        in_specs=[HBM, HBM],
        out_specs=[VMEM] * 3,
        scratch_shapes=[pltpu.VMEM((depth, rows, LANES), f32), pltpu.SemaphoreType.DMA((2,))],
        cost_estimate=pl.CostEstimate(flops=4_000_000, bytes_accessed=4_000_000, transcendentals=0),
        compiler_params=small,
    )(volume, strength)
    strips = pl.pallas_call(
        join_kernel,
        out_shape=shape(tall, LANES),
        in_specs=[VMEM] * 2,
        out_specs=VMEM,
        compiler_params=small,
    )(strips, layer)
    first, second = partners(gys)
    near = lax.ppermute(strips, "gy", list(enumerate(first)))
    far = lax.ppermute(strips, "gy", list(enumerate(second)))
    part = pl.pallas_call(
        main_kernel(depth, rows, blocks, size_x),
        out_shape=shape(depth, rows, size_y),
        in_specs=[VMEM] * 5,
        out_specs=VMEM,
        scratch_shapes=[
            pltpu.VMEM((7, tall, LANES), f32),
            pltpu.VMEM((7, depth, blocks + 6) + tile, f32),
            pltpu.VMEM((3, depth, blocks + 2) + tile, f32),
            pltpu.VMEM((5, depth + 2, blocks + 4) + tile, f32),
        ]
        + [pltpu.VMEM((depth, blocks) + tile, f32)] * 3,
        compiler_params=pltpu.CompilerParams(vmem_limit_bytes=16 * 2**20),
    )(mine, scale, layer, near, far)

    off = lax.axis_index("off")
    SMEM = pl.BlockSpec(memory_space=pltpu.SMEM)

    def place(block, source, whole):
        held = [] if whole is None else [whole]
        return pl.pallas_call(
            place_kernel,
            out_shape=shape(depth, size_x, size_y),
            in_specs=[VMEM, SMEM] + [HBM] * len(held),
            out_specs=HBM,
            scratch_shapes=[pltpu.SemaphoreType.DMA],
            input_output_aliases={2: 0} if held else {},
            compiler_params=small,
        )(block, source[None].astype(jnp.int32), *held)

    whole = place(part, off, None)
    for step in range(1, offs):
        other = lax.ppermute(part, "off", [(i, i ^ step) for i in range(offs)])
        whole = place(other, off ^ step, whole)
    return whole


def solution(mesh):
    return jax.shard_map(
        shards,
        mesh=mesh,
        in_specs=(P(None, "gx", "gy"), P(None, "gx", "gy")),
        out_specs=P(None, "gx", "gy"),
        check_vma=False,
    )
```

time: 43.7 us -> 39.8 us (0.911)
  starting transfers between devices: 15.3 us -> 9.66 us
  waiting for transfers between devices: 8.22 us -> 11.3 us
  local copies, waits for them, and re-layouts: 3.03 us -> 1.05 us
  Pallas kernels: 16.8 us -> 17.6 us
    ppermute x11 -> x6, starting transfers between devices: 15.3 us -> 9.66 us  [the longest x3 4.45 us: shards(): other = lax.ppermute(part, 'off', [(i, i ^ step) for i in range(offs)])]
    ppermute x11 -> x6, waiting for transfers between devices: 8.22 us -> 11.3 us  [the longest x3 8.95 us: shards(): other = lax.ppermute(part, 'off', [(i, i ^ step) for i in range(offs)])]
    unnamed x6 -> x4, local copies, waits for them, and re-layouts: 2.87 us -> 1.05 us
    pallas_call x3 -> x8, Pallas kernels: 16.8 us -> 17.6 us  [the longest x1 13.2 us: shards(): pl.pallas_call(main_kernel(depth, rows, blocks, size_x), out_shape=shape(...]
  transfers between devices with their start and end apart: 11 -> 6, of which waited for: 4 -> 4; matrix products, arithmetic and copies ran while one was open for 0% -> 0% of each run, Pallas kernels for 14% -> 6%
where the time goes in v5:
time: 39.8 us; the launch traced here: 39.7 us
  Pallas kernels  17.6 us (44%)
  waiting for transfers between devices  11.3 us (28%)
  starting transfers between devices  9.66 us (24%)
  local copies, waits for them, and re-layouts  1.05 us (3%)
    pallas_call x1, Pallas kernels, shards(): pl.pallas_call(main_kernel(depth, rows, blocks, size_x), out_shape=shape(...  13.2 us
    ppermute x3, waiting for transfers between devices, shards(): other = lax.ppermute(part, 'off', [(i, i ^ step) for i in range(offs)])  8.95 us
    ppermute x3, starting transfers between devices, shards(): other = lax.ppermute(part, 'off', [(i, i ^ step) for i in range(offs)])  4.45 us
    ppermute x1, starting transfers between devices, shards(): layer = lax.ppermute(layer, ('gx', 'off'), moves)  3.03 us
    pallas_call x4, Pallas kernels, place(): pl.pallas_call(place_kernel, out_shape=shape(depth, size_x, size_y), in_s...  2.66 us
    ppermute x1, starting transfers between devices, shards(): far = lax.ppermute(strips, 'gy', list(enumerate(second)))  2.11 us
    ppermute x1, waiting for transfers between devices, shards(): far = lax.ppermute(strips, 'gy', list(enumerate(second)))  1.52 us
    pallas_call x1, Pallas kernels, shards(): pl.pallas_call(layer_kernel, out_shape=shape(depth, *tile), in_specs=[HBM...  1.45 us
  transfers between devices with their start and end apart: 6, of which 4 were waited for; matrix products, arithmetic and copies ran while one was open for 0% of the time, Pallas kernels for 6%

profile of v5, /device:TPU:0, one launch (start us, length us, event | category | flops | bytes accessed | tf_op | source)
XLA Modules:
  0.0 39.7 jit_solution(1273749082884253486)
XLA Ops:
  0.0 0.0 copy-start
  0.0 1.5 %shard_map.29 = f32[8,8,128]{2,1,0:T(8,128)} custom-call(f32[8,128,128]{2,1,0:T(8,128)} %volume.3), custom_call_target="tpu_custom_call" | custom-call | tf_op jit(solution)/shard_map/pallas_call | solution.py:275
  1.5 3.0 %collective-permute-start = (f32[8,8,128]{2,1,0:T(8,128)}, f32[8,8,128]{2,1,0:T(8,128)S(1)}, u32[]{:S(2)}, u32[]{:S(2)}) collective-permute-start(f32[8,8,128]{2,1,0:T(8,128)} %shard_map.29), channel_id=1, source_target_pairs={{0,16},{1,17},{2,18},{3,19},{16,0},{17,1},{18,2},{19,3},{4,20},{5,... | collective-permute-start | bytes 98312 | tf_op jit(solution)/shard_map/ppermute | solution.py:287
  4.5 0.0 copy-done
  4.5 0.0 copy-start.1
  4.5 1.0 %copy-done.1 = f32[8,128,128]{2,1,0:T(8,128)S(1)} copy-done((f32[8,128,128]{2,1,0:T(8,128)S(1)}, f32[8,128,128]{2,1,0:T(8,128)}, u32[]{:S(2)}) %copy-start.1) | copy-done | bytes 524312
  5.5 0.2 shard_map.28
  5.8 0.8 %collective-permute-done.layer = f32[8,8,128]{2,1,0:T(8,128)S(1)} collective-permute-done((f32[8,8,128]{2,1,0:T(8,128)}, f32[8,8,128]{2,1,0:T(8,128)S(1)}, u32[]{:S(2)}, u32[]{:S(2)}) %collective-permute-start) | collective-permute-done | bytes 32800 | tf_op jit(solution)/shard_map/ppermute | solution.py:287
  6.6 0.1 shard_map.30
  6.7 0.1 collective-permute-start.1
  6.8 2.1 %collective-permute-start.2 = (f32[48,128]{1,0:T(8,128)S(1)}, f32[48,128]{1,0:T(8,128)S(1)}, u32[]{:S(2)}, u32[]{:S(2)}) collective-permute-start(f32[48,128]{1,0:T(8,128)S(1)} %shard_map.30), channel_id=1, source_target_pairs={{0,12},{4,8},{8,4},{12,0},{1,13},{5,9},{9,5},{13,1},{2,14},{6,10},... | collective-permute-start | bytes 73736 | tf_op jit(solution)/shard_map/ppermute | solution.py:306
  8.9 0.0 collective-permute-done.1.near
  8.9 1.5 %collective-permute-done.2.far = f32[48,128]{1,0:T(8,128)S(1)} collective-permute-done((f32[48,128]{1,0:T(8,128)S(1)}, f32[48,128]{1,0:T(8,128)S(1)}, u32[]{:S(2)}, u32[]{:S(2)}) %collective-permute-start.2) | collective-permute-done | bytes 24608 | tf_op jit(solution)/shard_map/ppermute | solution.py:306
  10.4 13.2 %shard_map.31.part = f32[8,32,128]{2,1,0:T(8,128)S(1)} custom-call(f32[8,48,128]{2,1,0:T(8,128)S(1)} %get-tuple-element.8.mine, f32[8,4,8,128]{3,2,1,0:T(8,128)S(1)} %get-tuple-element.9.scale, f32[8,8,128]{2,1,0:T(8,128)S(1)} %collective-permute-done.layer, f32[48,128]{1,0:T(8,128)S(1)} %collective-permute-done.1.near, f32[48,128]{1,0:T(8,128)S(1)} %collective-permute-done.2.far), custom_call_target="tpu_custom_call" | custom-call | tf_op jit(solution)/shard_map/pallas_call | solution.py:307
  23.6 1.8 %collective-permute-start.5 = (f32[8,32,128]{2,1,0:T(8,128)S(1)}, f32[8,32,128]{2,1,0:T(8,128)S(1)}, u32[]{:S(2)}, u32[]{:S(2)}) collective-permute-start(f32[8,32,128]{2,1,0:T(8,128)S(1)} %shard_map.31.part), channel_id=1, source_target_pairs={{0,1},{1,0},{2,3},{3,2},{4,5},{5,4},{6,7},{7,6},{8,9},{9,8},{10,11... | collective-permute-start | bytes 393224 | tf_op jit(solution)/shard_map/ppermute | solution.py:339
  25.4 2.6 %collective-permute-start.4 = (f32[8,32,128]{2,1,0:T(8,128)S(1)}, f32[8,32,128]{2,1,0:T(8,128)S(1)}, u32[]{:S(2)}, u32[]{:S(2)}) collective-permute-start(f32[8,32,128]{2,1,0:T(8,128)S(1)} %shard_map.31.part), channel_id=1, source_target_pairs={{0,2},{1,3},{2,0},{3,1},{4,6},{5,7},{6,4},{7,5},{8,10},{9,11},{10,... | collective-permute-start | bytes 393224 | tf_op jit(solution)/shard_map/ppermute | solution.py:339
  28.0 0.0 collective-permute-start.3
  28.0 0.7 %shard_map.32.refs_0_ = f32[8,128,128]{2,1,0:T(8,128)} custom-call(f32[8,32,128]{2,1,0:T(8,128)S(1)} %shard_map.31.part, s32[1]{0:T(128)} %bitcast.3.off), custom_call_target="tpu_custom_call" | custom-call | tf_op jit(solution)/shard_map/pallas_call | solution.py:327
  28.7 3.0 %collective-permute-done.5.part = f32[8,32,128]{2,1,0:T(8,128)S(1)} collective-permute-done((f32[8,32,128]{2,1,0:T(8,128)S(1)}, f32[8,32,128]{2,1,0:T(8,128)S(1)}, u32[]{:S(2)}, u32[]{:S(2)}) %collective-permute-start.5) | collective-permute-done | bytes 131104 | tf_op jit(solution)/shard_map/ppermute | solution.py:339
  31.7 0.7 %shard_map.33.refs_0_ = f32[8,128,128]{2,1,0:T(8,128)} custom-call(f32[8,32,128]{2,1,0:T(8,128)S(1)} %collective-permute-done.5.part, s32[1]{0:T(128)} %bitcast.2.off, f32[8,128,128]{2,1,0:T(8,128)} %shard_map.32.refs_0_), custom_call_target="tpu_custom_call", output_to_operand_aliasing={{}: (2, {})} | custom-call | tf_op jit(solution)/shard_map/pallas_call | solution.py:327
  32.4 5.9 %collective-permute-done.4.part = f32[8,32,128]{2,1,0:T(8,128)S(1)} collective-permute-done((f32[8,32,128]{2,1,0:T(8,128)S(1)}, f32[8,32,128]{2,1,0:T(8,128)S(1)}, u32[]{:S(2)}, u32[]{:S(2)}) %collective-permute-start.4) | collective-permute-done | bytes 131104 | tf_op jit(solution)/shard_map/ppermute | solution.py:339
  38.3 0.7 %shard_map.34.refs_0_ = f32[8,128,128]{2,1,0:T(8,128)} custom-call(f32[8,32,128]{2,1,0:T(8,128)S(1)} %collective-permute-done.4.part, s32[1]{0:T(128)} %bitcast.1.off, f32[8,128,128]{2,1,0:T(8,128)} %shard_map.33.refs_0_), custom_call_target="tpu_custom_call", output_to_operand_aliasing={{}: (2, {})} | custom-call | tf_op jit(solution)/shard_map/pallas_call | solution.py:327
  39.0 0.0 collective-permute-done.3.part
  39.0 0.7 %shard_map.35 = f32[8,128,128]{2,1,0:T(8,128)} custom-call(f32[8,32,128]{2,1,0:T(8,128)S(1)} %collective-permute-done.3.part, s32[1]{0:T(128)} %bitcast.off, f32[8,128,128]{2,1,0:T(8,128)} %shard_map.34.refs_0_), custom_call_target="tpu_custom_call", output_to_operand_aliasing={{}: (2, {})} | custom-call | tf_op jit(solution)/shard_map/pallas_call | solution.py:327
Async XLA Ops:
  0.0 4.5 %copy-start = (f32[8,128,128]{2,1,0:T(8,128)S(1)}, f32[8,128,128]{2,1,0:T(8,128)}, u32[]{:S(2)}) copy-start(f32[8,128,128]{2,1,0:T(8,128)} %volume.3) | copy-start | bytes 1572868
  1.5 5.1 %collective-permute-start = (f32[8,8,128]{2,1,0:T(8,128)}, f32[8,8,128]{2,1,0:T(8,128)S(1)}, u32[]{:S(2)}, u32[]{:S(2)}) collective-permute-start(f32[8,8,128]{2,1,0:T(8,128)} %shard_map.29), channel_id=1, source_target_pairs={{0,16},{1,17},{2,18},{3,19},{16,0},{17,1},{18,2},{19,3},{4,20},{5,... | collective-permute-start | bytes 98312 | tf_op jit(solution)/shard_map/ppermute | solution.py:287
  4.5 1.0 %copy-start.1 = (f32[8,128,128]{2,1,0:T(8,128)S(1)}, f32[8,128,128]{2,1,0:T(8,128)}, u32[]{:S(2)}) copy-start(f32[8,128,128]{2,1,0:T(8,128)} %strength.1) | copy-start | bytes 1572868
  6.7 2.2 %collective-permute-start.1 = (f32[48,128]{1,0:T(8,128)S(1)}, f32[48,128]{1,0:T(8,128)S(1)}, u32[]{:S(2)}, u32[]{:S(2)}) collective-permute-start(f32[48,128]{1,0:T(8,128)S(1)} %shard_map.30), channel_id=1, source_target_pairs={{0,4},{4,0},{8,12},{12,8},{1,5},{5,1},{9,13},{13,9},{2,6},{6,2},{1... | collective-permute-start | bytes 73736 | tf_op jit(solution)/shard_map/ppermute | solution.py:305
  6.8 3.6 %collective-permute-start.2 = (f32[48,128]{1,0:T(8,128)S(1)}, f32[48,128]{1,0:T(8,128)S(1)}, u32[]{:S(2)}, u32[]{:S(2)}) collective-permute-start(f32[48,128]{1,0:T(8,128)S(1)} %shard_map.30), channel_id=1, source_target_pairs={{0,12},{4,8},{8,4},{12,0},{1,13},{5,9},{9,5},{13,1},{2,14},{6,10},... | collective-permute-start | bytes 73736 | tf_op jit(solution)/shard_map/ppermute | solution.py:306
  23.6 8.1 %collective-permute-start.5 = (f32[8,32,128]{2,1,0:T(8,128)S(1)}, f32[8,32,128]{2,1,0:T(8,128)S(1)}, u32[]{:S(2)}, u32[]{:S(2)}) collective-permute-start(f32[8,32,128]{2,1,0:T(8,128)S(1)} %shard_map.31.part), channel_id=1, source_target_pairs={{0,1},{1,0},{2,3},{3,2},{4,5},{5,4},{6,7},{7,6},{8,9},{9,8},{10,11... | collective-permute-start | bytes 393224 | tf_op jit(solution)/shard_map/ppermute | solution.py:339
  25.4 12.9 %collective-permute-start.4 = (f32[8,32,128]{2,1,0:T(8,128)S(1)}, f32[8,32,128]{2,1,0:T(8,128)S(1)}, u32[]{:S(2)}, u32[]{:S(2)}) collective-permute-start(f32[8,32,128]{2,1,0:T(8,128)S(1)} %shard_map.31.part), channel_id=1, source_target_pairs={{0,2},{1,3},{2,0},{3,1},{4,6},{5,7},{6,4},{7,5},{8,10},{9,11},{10,... | collective-permute-start | bytes 393224 | tf_op jit(solution)/shard_map/ppermute | solution.py:339
  28.0 11.0 %collective-permute-start.3 = (f32[8,32,128]{2,1,0:T(8,128)S(1)}, f32[8,32,128]{2,1,0:T(8,128)S(1)}, u32[]{:S(2)}, u32[]{:S(2)}) collective-permute-start(f32[8,32,128]{2,1,0:T(8,128)S(1)} %shard_map.31.part), channel_id=1, source_target_pairs={{0,3},{1,2},{2,1},{3,0},{4,7},{5,6},{6,5},{7,4},{8,11},{9,10},{10,... | collective-permute-start | bytes 393224 | tf_op jit(solution)/shard_map/ppermute | solution.py:339

commit v6 on v5

--- a/solution.py
+++ b/solution.py
@@ -247,13 +247,18 @@
             ) / (total[z, i] + t)
 
 
-def place_kernel(part, off, *refs):
-    *_, out, done = refs
-    rows = part.shape[1]
-    at = pl.ds(pl.multiple_of(off[0] * rows, SUBS), rows)
-    copy = pltpu.make_async_copy(part, out.at[:, at, :], done)
-    copy.start()
-    copy.wait()
+def place_kernel(count, rows):
+    def kernel(*refs):
+        parts, sources, (*_, out, done) = refs[:count], refs[count], refs[count + 1 :]
+        copies = []
+        for n, part in enumerate(parts):
+            at = pl.ds(pl.multiple_of(sources[n] * rows, SUBS), rows)
+            copies.append(pltpu.make_async_copy(part, out.at[:, at, :], done.at[n]))
+            copies[n].start()
+        for copy in copies:
+            copy.wait()
+
+    return kernel
 
 
 def shards(volume, strength):
@@ -278,6 +283,7 @@
         in_specs=[HBM],
         out_specs=VMEM,
         scratch_shapes=[pltpu.SemaphoreType.DMA],
+        compiler_params=small,
     )(volume)
     moves = []
     for x in range(gxs):
@@ -322,23 +328,27 @@
     off = lax.axis_index("off")
     SMEM = pl.BlockSpec(memory_space=pltpu.SMEM)
 
-    def place(block, source, whole):
+    def place(blocks, whole):
+        count = len(blocks)
         held = [] if whole is None else [whole]
+        sources = jnp.stack([off ^ step for step, _ in blocks]).astype(jnp.int32)
         return pl.pallas_call(
-            place_kernel,
+            place_kernel(count, rows),
             out_shape=shape(depth, size_x, size_y),
-            in_specs=[VMEM, SMEM] + [HBM] * len(held),
+            in_specs=[VMEM] * count + [SMEM] + [HBM] * len(held),
             out_specs=HBM,
-            scratch_shapes=[pltpu.SemaphoreType.DMA],
-            input_output_aliases={2: 0} if held else {},
+            scratch_shapes=[pltpu.SemaphoreType.DMA((count,))],
+            input_output_aliases={count + 1: 0} if held else {},
             compiler_params=small,
-        )(block, source[None].astype(jnp.int32), *held)
-
-    whole = place(part, off, None)
-    for step in range(1, offs):
-        other = lax.ppermute(part, "off", [(i, i ^ step) for i in range(offs)])
-        whole = place(other, off ^ step, whole)
-    return whole
+        )(*(block for _, block in blocks), sources, *held)
+
+    assert offs & (offs - 1) == 0
+    blocks, bit = [(0, part)], offs // 2
+    while bit:
+        swap = [(i, i ^ bit) for i in range(offs)]
+        blocks += [(step ^ bit, lax.ppermute(block, "off", swap)) for step, block in blocks]
+        bit //= 2
+    return place(blocks[-1:], place(blocks[:-1], None))
 
 
 def solution(mesh):

time: 39.8 us -> 38.4 us (0.965)
  Pallas kernels: 17.6 us -> 15.5 us
  starting transfers between devices: 9.66 us -> 10.8 us
  waiting for transfers between devices: 11.3 us -> 10.9 us
    ppermute x1, starting transfers between devices: 2.11 us -> 0.35 us  [shards(): far = lax.ppermute(strips, 'gy', list(enumerate(second)))]
    ppermute x1, starting transfers between devices: 0.07 us -> 1.83 us  [shards(): near = lax.ppermute(strips, 'gy', list(enumerate(first)))]
    pallas_call x1, Pallas kernels: 1.45 us -> 0.02 us  [shards(): pl.pallas_call(layer_kernel, out_shape=shape(depth, *tile), in_specs=[HBM...]
    ppermute x3, starting transfers between devices: 4.45 us -> 5.56 us  [shards(): lax.ppermute(block, 'off', swap)]
    ppermute x3, waiting for transfers between devices: 8.95 us -> 8.07 us  [shards(): lax.ppermute(block, 'off', swap)]
    ppermute x1, waiting for transfers between devices: 0.84 us -> 1.67 us  [shards(): layer = lax.ppermute(layer, ('gx', 'off'), moves)]
    pallas_call x4 -> x2, Pallas kernels: 2.66 us -> 1.97 us  [place(): pl.pallas_call(place_kernel(count, rows), out_shape=shape(depth, size_x,...]
  transfers between devices with their start and end apart: 6 -> 6, of which waited for: 4 -> 4; matrix products, arithmetic and copies ran while one was open for 0% -> 0% of each run, Pallas kernels for 6% -> 4%
where the time goes in v6:
time: 38.4 us; the launch traced here: 38.3 us
  Pallas kernels  15.5 us (40%)
  waiting for transfers between devices  10.9 us (28%)
  starting transfers between devices  10.8 us (28%)
  local copies, waits for them, and re-layouts  1.04 us (3%)
    pallas_call x1, Pallas kernels, shards(): pl.pallas_call(main_kernel(depth, rows, blocks, size_x), out_shape=shape(...  13.2 us
    ppermute x3, waiting for transfers between devices, shards(): lax.ppermute(block, 'off', swap)  8.07 us
    ppermute x3, starting transfers between devices, shards(): lax.ppermute(block, 'off', swap)  5.56 us
    ppermute x1, starting transfers between devices, shards(): layer = lax.ppermute(layer, ('gx', 'off'), moves)  3.03 us
    pallas_call x2, Pallas kernels, place(): pl.pallas_call(place_kernel(count, rows), out_shape=shape(depth, size_x,...  1.97 us
    ppermute x1, starting transfers between devices, shards(): near = lax.ppermute(strips, 'gy', list(enumerate(first)))  1.83 us
    ppermute x1, waiting for transfers between devices, shards(): layer = lax.ppermute(layer, ('gx', 'off'), moves)  1.67 us
    ppermute x1, waiting for transfers between devices, shards(): far = lax.ppermute(strips, 'gy', list(enumerate(second)))  1.14 us
  transfers between devices with their start and end apart: 6, of which 4 were waited for; matrix products, arithmetic and copies ran while one was open for 0% of the time, Pallas kernels for 4%

profile of v6, /device:TPU:0, one launch (start us, length us, event | category | flops | bytes accessed | tf_op | source)
XLA Modules:
  0.0 38.3 jit_solution(9139077340619757149)
XLA Ops:
  0.0 0.0 copy-start
  0.0 1.0 %copy-done = f32[8,128,128]{2,1,0:T(8,128)S(1)} copy-done((f32[8,128,128]{2,1,0:T(8,128)S(1)}, f32[8,128,128]{2,1,0:T(8,128)}, u32[]{:S(2)}) %copy-start) | copy-done | bytes 524312
  1.0 0.0 copy-start.1
  1.1 3.0 %collective-permute-start = (f32[8,8,128]{2,1,0:T(8,128)S(1)}, f32[8,8,128]{2,1,0:T(8,128)S(1)}, u32[]{:S(2)}, u32[]{:S(2)}) collective-permute-start(f32[8,8,128]{2,1,0:T(8,128)S(1)} %shard_map.29), channel_id=1, source_target_pairs={{0,16},{1,17},{2,18},{3,19},{16,0},{17,1},{18,2},{19,3},{4,20},{5,... | collective-permute-start | bytes 98312 | tf_op jit(solution)/shard_map/ppermute | solution.py:293
  4.1 0.0 copy-done.1
  4.1 0.2 shard_map.28
  4.3 1.7 %collective-permute-done.layer = f32[8,8,128]{2,1,0:T(8,128)S(1)} collective-permute-done((f32[8,8,128]{2,1,0:T(8,128)S(1)}, f32[8,8,128]{2,1,0:T(8,128)S(1)}, u32[]{:S(2)}, u32[]{:S(2)}) %collective-permute-start) | collective-permute-done | bytes 32800 | tf_op jit(solution)/shard_map/ppermute | solution.py:293
  6.0 0.1 shard_map.30
  6.1 0.3 collective-permute-start.2
  6.4 1.8 %collective-permute-start.1 = (f32[48,128]{1,0:T(8,128)S(1)}, f32[48,128]{1,0:T(8,128)S(1)}, u32[]{:S(2)}, u32[]{:S(2)}) collective-permute-start(f32[48,128]{1,0:T(8,128)S(1)} %shard_map.30), channel_id=1, source_target_pairs={{0,4},{4,0},{8,12},{12,8},{1,5},{5,1},{9,13},{13,9},{2,6},{6,2},{1... | collective-permute-start | bytes 73736 | tf_op jit(solution)/shard_map/ppermute | solution.py:311
  8.3 1.1 %collective-permute-done.2.far = f32[48,128]{1,0:T(8,128)S(1)} collective-permute-done((f32[48,128]{1,0:T(8,128)S(1)}, f32[48,128]{1,0:T(8,128)S(1)}, u32[]{:S(2)}, u32[]{:S(2)}) %collective-permute-start.2) | collective-permute-done | bytes 24608 | tf_op jit(solution)/shard_map/ppermute | solution.py:312
  9.4 0.0 collective-permute-done.1.near
  9.4 13.2 %shard_map.31.refs_0_ = f32[8,32,128]{2,1,0:T(8,128)S(1)} custom-call(f32[8,48,128]{2,1,0:T(8,128)S(1)} %get-tuple-element.8.mine, f32[8,4,8,128]{3,2,1,0:T(8,128)S(1)} %get-tuple-element.9.scale, f32[8,8,128]{2,1,0:T(8,128)S(1)} %collective-permute-done.layer, f32[48,128]{1,0:T(8,128)S(1)} %collective-permute-done.1.near, ...), custom_call_target="tpu_custom_call" | custom-call | tf_op jit(solution)/shard_map/pallas_call | solution.py:313
  22.6 3.4 %collective-permute-start.3 = (f32[8,32,128]{2,1,0:T(8,128)S(1)}, f32[8,32,128]{2,1,0:T(8,128)S(1)}, u32[]{:S(2)}, u32[]{:S(2)}) collective-permute-start(f32[8,32,128]{2,1,0:T(8,128)S(1)} %shard_map.31.refs_0_), channel_id=1, source_target_pairs={{0,2},{1,3},{2,0},{3,1},{4,6},{5,7},{6,4},{7,5},{8,10},{9,11},{10,... | collective-permute-start | bytes 393224 | tf_op jit(solution)/shard_map/ppermute | solution.py:349
  26.0 1.6 %collective-permute-start.5 = (f32[8,32,128]{2,1,0:T(8,128)S(1)}, f32[8,32,128]{2,1,0:T(8,128)S(1)}, u32[]{:S(2)}, u32[]{:S(2)}) collective-permute-start(f32[8,32,128]{2,1,0:T(8,128)S(1)} %shard_map.31.refs_0_), channel_id=1, source_target_pairs={{0,1},{1,0},{2,3},{3,2},{4,5},{5,4},{6,7},{7,6},{8,9},{9,8},{10,11... | collective-permute-start | bytes 393224 | tf_op jit(solution)/shard_map/ppermute | solution.py:349
  27.5 5.1 %collective-permute-done.3.refs_1_ = f32[8,32,128]{2,1,0:T(8,128)S(1)} collective-permute-done((f32[8,32,128]{2,1,0:T(8,128)S(1)}, f32[8,32,128]{2,1,0:T(8,128)S(1)}, u32[]{:S(2)}, u32[]{:S(2)}) %collective-permute-start.3) | collective-permute-done | bytes 131104 | tf_op jit(solution)/shard_map/ppermute | solution.py:349
  32.6 0.6 %collective-permute-start.4 = (f32[8,32,128]{2,1,0:T(8,128)S(1)}, f32[8,32,128]{2,1,0:T(8,128)S(1)}, u32[]{:S(2)}, u32[]{:S(2)}) collective-permute-start(f32[8,32,128]{2,1,0:T(8,128)S(1)} %collective-permute-done.3.refs_1_), channel_id=1, source_target_pairs={{0,1},{1,0},{2,3},{3,2},{4,5},{5,4},{6,7},{7,6},{8,9},{9,8},{10,11... | collective-permute-start | bytes 393224 | tf_op jit(solution)/shard_map/ppermute | solution.py:349
  33.3 0.1 pad_add_fusion.refs_3_
  33.3 0.0 collective-permute-done.5.refs_2_
  33.3 1.3 %shard_map.32.refs_2_ = f32[8,128,128]{2,1,0:T(8,128)} custom-call(f32[8,32,128]{2,1,0:T(8,128)S(1)} %shard_map.31.refs_0_, f32[8,32,128]{2,1,0:T(8,128)S(1)} %collective-permute-done.3.refs_1_, f32[8,32,128]{2,1,0:T(8,128)S(1)} %collective-permute-done.5.refs_2_, s32[3]{0:T(128)S(1)} %pad_add_fusion.refs_3_), custom_call_target="tpu_custom_call" | custom-call | tf_op jit(solution)/shard_map/pallas_call | solution.py:335
  34.7 3.0 %collective-permute-done.4.refs_0_ = f32[8,32,128]{2,1,0:T(8,128)S(1)} collective-permute-done((f32[8,32,128]{2,1,0:T(8,128)S(1)}, f32[8,32,128]{2,1,0:T(8,128)S(1)}, u32[]{:S(2)}, u32[]{:S(2)}) %collective-permute-start.4) | collective-permute-done | bytes 131104 | tf_op jit(solution)/shard_map/ppermute | solution.py:349
  37.6 0.7 %shard_map.33 = f32[8,128,128]{2,1,0:T(8,128)} custom-call(f32[8,32,128]{2,1,0:T(8,128)S(1)} %collective-permute-done.4.refs_0_, s32[1]{0:T(128)} %bitcast.refs_1_, f32[8,128,128]{2,1,0:T(8,128)} %shard_map.32.refs_2_), custom_call_target="tpu_custom_call", output_to_operand_aliasing={{}: (2, {})} | custom-call | tf_op jit(solution)/shard_map/pallas_call | solution.py:335
  (1 shorter events, 0.0 us)
Async XLA Ops:
  0.0 1.0 %copy-start = (f32[8,128,128]{2,1,0:T(8,128)S(1)}, f32[8,128,128]{2,1,0:T(8,128)}, u32[]{:S(2)}) copy-start(f32[8,128,128]{2,1,0:T(8,128)} %volume.3) | copy-start | bytes 1572868
  1.0 3.1 %copy-start.1 = (f32[8,128,128]{2,1,0:T(8,128)S(1)}, f32[8,128,128]{2,1,0:T(8,128)}, u32[]{:S(2)}) copy-start(f32[8,128,128]{2,1,0:T(8,128)} %strength.1) | copy-start | bytes 1572868
  1.1 4.9 %collective-permute-start = (f32[8,8,128]{2,1,0:T(8,128)S(1)}, f32[8,8,128]{2,1,0:T(8,128)S(1)}, u32[]{:S(2)}, u32[]{:S(2)}) collective-permute-start(f32[8,8,128]{2,1,0:T(8,128)S(1)} %shard_map.29), channel_id=1, source_target_pairs={{0,16},{1,17},{2,18},{3,19},{16,0},{17,1},{18,2},{19,3},{4,20},{5,... | collective-permute-start | bytes 98312 | tf_op jit(solution)/shard_map/ppermute | solution.py:293
  6.1 3.3 %collective-permute-start.2 = (f32[48,128]{1,0:T(8,128)S(1)}, f32[48,128]{1,0:T(8,128)S(1)}, u32[]{:S(2)}, u32[]{:S(2)}) collective-permute-start(f32[48,128]{1,0:T(8,128)S(1)} %shard_map.30), channel_id=1, source_target_pairs={{0,12},{4,8},{8,4},{12,0},{1,13},{5,9},{9,5},{13,1},{2,14},{6,10},... | collective-permute-start | bytes 73736 | tf_op jit(solution)/shard_map/ppermute | solution.py:312
  6.4 3.0 %collective-permute-start.1 = (f32[48,128]{1,0:T(8,128)S(1)}, f32[48,128]{1,0:T(8,128)S(1)}, u32[]{:S(2)}, u32[]{:S(2)}) collective-permute-start(f32[48,128]{1,0:T(8,128)S(1)} %shard_map.30), channel_id=1, source_target_pairs={{0,4},{4,0},{8,12},{12,8},{1,5},{5,1},{9,13},{13,9},{2,6},{6,2},{1... | collective-permute-start | bytes 73736 | tf_op jit(solution)/shard_map/ppermute | solution.py:311
  22.6 10.1 %collective-permute-start.3 = (f32[8,32,128]{2,1,0:T(8,128)S(1)}, f32[8,32,128]{2,1,0:T(8,128)S(1)}, u32[]{:S(2)}, u32[]{:S(2)}) collective-permute-start(f32[8,32,128]{2,1,0:T(8,128)S(1)} %shard_map.31.refs_0_), channel_id=1, source_target_pairs={{0,2},{1,3},{2,0},{3,1},{4,6},{5,7},{6,4},{7,5},{8,10},{9,11},{10,... | collective-permute-start | bytes 393224 | tf_op jit(solution)/shard_map/ppermute | solution.py:349
  26.0 7.4 %collective-permute-start.5 = (f32[8,32,128]{2,1,0:T(8,128)S(1)}, f32[8,32,128]{2,1,0:T(8,128)S(1)}, u32[]{:S(2)}, u32[]{:S(2)}) collective-permute-start(f32[8,32,128]{2,1,0:T(8,128)S(1)} %shard_map.31.refs_0_), channel_id=1, source_target_pairs={{0,1},{1,0},{2,3},{3,2},{4,5},{5,4},{6,7},{7,6},{8,9},{9,8},{10,11... | collective-permute-start | bytes 393224 | tf_op jit(solution)/shard_map/ppermute | solution.py:349
  32.6 5.0 %collective-permute-start.4 = (f32[8,32,128]{2,1,0:T(8,128)S(1)}, f32[8,32,128]{2,1,0:T(8,128)S(1)}, u32[]{:S(2)}, u32[]{:S(2)}) collective-permute-start(f32[8,32,128]{2,1,0:T(8,128)S(1)} %collective-permute-done.3.refs_1_), channel_id=1, source_target_pairs={{0,1},{1,0},{2,3},{3,2},{4,5},{5,4},{6,7},{7,6},{8,9},{9,8},{10,11... | collective-permute-start | bytes 393224 | tf_op jit(solution)/shard_map/ppermute | solution.py:349

commit v7 on v6

--- a/solution.py
+++ b/solution.py
@@ -109,7 +109,7 @@
     wide = blocks + 6
     tall = rows // SUBS + 2
 
-    def kernel(mine, scale, layer, near, far, out, flat, vals, cent, energy, *sums):
+    def kernel(mine, scale, layer, near, far, out, low, high, flat, vals, cent, energy, *sums):
         lane = lanes()
         _, block = window(lax.axis_index("off"), rows, size_x)
         gy, gys = lax.axis_index("gy"), lax.axis_size("gy")
@@ -170,12 +170,12 @@
 
         lax.fori_loop(0, 5, energies, 0)
 
-        weigh(depth, blocks, vals, cent, energy, scale, out, *sums)
+        weigh(depth, blocks, vals, cent, energy, scale, (out, low, high), *sums)
 
     return kernel
 
 
-def weigh(depth, blocks, vals, cent, energy, scale, out, top, total, weighted):
+def weigh(depth, blocks, vals, cent, energy, scale, outs, top, total, weighted):
     begin, end = 0, depth
     for z in range(end - begin):
         for i in range(blocks):
@@ -242,9 +242,10 @@
     for z in range(end - begin):
         for i in range(blocks):
             t = top[z, i]
-            out[z, pl.ds(i, SUBS, stride=blocks), :] = (
-                weighted[z, i] + t * vals[3, z + begin, i + 3]
-            ) / (total[z, i] + t)
+            value = (weighted[z, i] + t * vals[3, z + begin, i + 3]) / (total[z, i] + t)
+            part = outs[1] if z < depth // 2 else outs[2]
+            for ref, at in ((outs[0], z), (part, z % (depth // 2))):
+                ref[at, pl.ds(i, SUBS, stride=blocks), :] = value
 
 
 def place_kernel(count, rows):
@@ -252,8 +253,9 @@
         parts, sources, (*_, out, done) = refs[:count], refs[count], refs[count + 1 :]
         copies = []
         for n, part in enumerate(parts):
-            at = pl.ds(pl.multiple_of(sources[n] * rows, SUBS), rows)
-            copies.append(pltpu.make_async_copy(part, out.at[:, at, :], done.at[n]))
+            at = pl.ds(pl.multiple_of(sources[n, 0] * rows, SUBS), rows)
+            slices = pl.ds(sources[n, 1], part.shape[0])
+            copies.append(pltpu.make_async_copy(part, out.at[slices, at, :], done.at[n]))
             copies[n].start()
         for copy in copies:
             copy.wait()
@@ -310,11 +312,12 @@
     first, second = partners(gys)
     near = lax.ppermute(strips, "gy", list(enumerate(first)))
     far = lax.ppermute(strips, "gy", list(enumerate(second)))
-    part = pl.pallas_call(
+    half = depth // 2
+    part, *halves = pl.pallas_call(
         main_kernel(depth, rows, blocks, size_x),
-        out_shape=shape(depth, rows, size_y),
+        out_shape=[shape(depth, rows, size_y)] + [shape(half, rows, size_y)] * 2,
         in_specs=[VMEM] * 5,
-        out_specs=VMEM,
+        out_specs=[VMEM] * 3,
         scratch_shapes=[
             pltpu.VMEM((7, tall, LANES), f32),
             pltpu.VMEM((7, depth, blocks + 6) + tile, f32),
@@ -331,7 +334,7 @@
     def place(blocks, whole):
         count = len(blocks)
         held = [] if whole is None else [whole]
-        sources = jnp.stack([off ^ step for step, _ in blocks]).astype(jnp.int32)
+        sources = jnp.stack([jnp.stack([off ^ step, z]) for step, z, _ in blocks]).astype(jnp.int32)
         return pl.pallas_call(
             place_kernel(count, rows),
             out_shape=shape(depth, size_x, size_y),
@@ -340,14 +343,19 @@
             scratch_shapes=[pltpu.SemaphoreType.DMA((count,))],
             input_output_aliases={count + 1: 0} if held else {},
             compiler_params=small,
-        )(*(block for _, block in blocks), sources, *held)
+        )(*(block for *_, block in blocks), sources, *held)
+
+    def swapped(block, bit):
+        return lax.ppermute(block, "off", [(i, i ^ bit) for i in range(offs)])
 
     assert offs & (offs - 1) == 0
-    blocks, bit = [(0, part)], offs // 2
-    while bit:
-        swap = [(i, i ^ bit) for i in range(offs)]
-        blocks += [(step ^ bit, lax.ppermute(block, "off", swap)) for step, block in blocks]
+    zero = jnp.int32(0)
+    bit = offs // 2
+    blocks = [(0, zero, part)]
+    blocks += [(bit, zero + half * n, swapped(halves[n], bit)) for n in range(2)]
+    while bit > 1:
         bit //= 2
+        blocks += [(step ^ bit, z, swapped(block, bit)) for step, z, block in blocks]
     return place(blocks[-1:], place(blocks[:-1], None))
 
 

time: 38.4 us -> 39.3 us (1.023)
  waiting for transfers between devices: 10.9 us -> 6.97 us
  starting transfers between devices: 10.8 us -> 13.6 us
  local copies, waits for them, and re-layouts: 1.04 us -> 2.11 us
  Pallas kernels: 15.5 us -> 16.1 us
    ppermute x3 -> x5, starting transfers between devices: 5.56 us -> 8.39 us  [swapped(): return lax.ppermute(block, 'off', [(i, i ^ bit) for i in range(offs)])]
    ppermute x3 -> x5, waiting for transfers between devices: 8.07 us -> 5.34 us  [swapped(): return lax.ppermute(block, 'off', [(i, i ^ bit) for i in range(offs)])]
    ppermute x1, waiting for transfers between devices: 1.67 us -> 0.56 us  [shards(): layer = lax.ppermute(layer, ('gx', 'off'), moves)]
    unnamed x4 -> x6, local copies, waits for them, and re-layouts: 1.04 us -> 2.09 us
    pallas_call x2, Pallas kernels: 1.97 us -> 2.59 us  [place(): pl.pallas_call(place_kernel(count, rows), out_shape=shape(depth, size_x,...]
  transfers between devices with their start and end apart: 6 -> 8, of which waited for: 4 -> 5; matrix products, arithmetic and copies ran while one was open for 0% -> 1% of each run, Pallas kernels for 4% -> 4%
where the time goes in v7:
time: 39.3 us; the launch traced here: 39.1 us
  Pallas kernels  16.1 us (41%)
  starting transfers between devices  13.6 us (35%)
  waiting for transfers between devices  6.97 us (18%)
  local copies, waits for them, and re-layouts  2.11 us (5%)
    pallas_call x1, Pallas kernels, shards(): pl.pallas_call(main_kernel(depth, rows, blocks, size_x), out_shape=[shape...  13.2 us
    ppermute x5, starting transfers between devices, swapped(): return lax.ppermute(block, 'off', [(i, i ^ bit) for i in range(offs)])  8.39 us
    ppermute x5, waiting for transfers between devices, swapped(): return lax.ppermute(block, 'off', [(i, i ^ bit) for i in range(offs)])  5.34 us
    ppermute x1, starting transfers between devices, shards(): layer = lax.ppermute(layer, ('gx', 'off'), moves)  3.03 us
    pallas_call x2, Pallas kernels, place(): pl.pallas_call(place_kernel(count, rows), out_shape=shape(depth, size_x,...  2.59 us
    unnamed x6, local copies, waits for them, and re-layouts  2.09 us
    ppermute x1, starting transfers between devices, shards(): near = lax.ppermute(strips, 'gy', list(enumerate(first)))  1.83 us
    ppermute x1, waiting for transfers between devices, shards(): far = lax.ppermute(strips, 'gy', list(enumerate(second)))  1.07 us
  transfers between devices with their start and end apart: 8, of which 5 were waited for; matrix products, arithmetic and copies ran while one was open for 1% of the time, Pallas kernels for 4%

profile of v7, /device:TPU:0, one launch (start us, length us, event | category | flops | bytes accessed | tf_op | source)
XLA Modules:
  0.0 39.1 jit_solution(1246341389347262692)
XLA Ops:
  0.0 0.0 copy-start
  0.0 1.0 %copy-done = f32[8,128,128]{2,1,0:T(8,128)S(1)} copy-done((f32[8,128,128]{2,1,0:T(8,128)S(1)}, f32[8,128,128]{2,1,0:T(8,128)}, u32[]{:S(2)}) %copy-start) | copy-done | bytes 524312
  1.0 0.0 copy-start.1
  1.1 3.0 %collective-permute-start = (f32[8,8,128]{2,1,0:T(8,128)S(1)}, f32[8,8,128]{2,1,0:T(8,128)S(1)}, u32[]{:S(2)}, u32[]{:S(2)}) collective-permute-start(f32[8,8,128]{2,1,0:T(8,128)S(1)} %shard_map.29), channel_id=1, source_target_pairs={{0,16},{1,17},{2,18},{3,19},{16,0},{17,1},{18,2},{19,3},{4,20},{5,... | collective-permute-start | bytes 98312 | tf_op jit(solution)/shard_map/ppermute | solution.py:295
  4.1 0.1 fusion.4
  4.2 0.0 copy-done.1
  4.2 0.0 copy-start.2
  4.2 1.0 %copy-done.2 = f32[8,128,128]{2,1,0:T(8,128)S(1)} copy-done((f32[8,128,128]{2,1,0:T(8,128)S(1)}, f32[8,128,128]{2,1,0:T(8,128)}, u32[]{:S(2)}) %copy-start.2) | copy-done | bytes 524312
  5.2 0.2 shard_map.28
  5.4 0.6 %collective-permute-done.layer = f32[8,8,128]{2,1,0:T(8,128)S(1)} collective-permute-done((f32[8,8,128]{2,1,0:T(8,128)S(1)}, f32[8,8,128]{2,1,0:T(8,128)S(1)}, u32[]{:S(2)}, u32[]{:S(2)}) %collective-permute-start) | collective-permute-done | bytes 32800 | tf_op jit(solution)/shard_map/ppermute | solution.py:295
  6.0 0.1 shard_map.30
  6.1 0.3 collective-permute-start.2
  6.4 1.8 %collective-permute-start.1 = (f32[48,128]{1,0:T(8,128)S(1)}, f32[48,128]{1,0:T(8,128)S(1)}, u32[]{:S(2)}, u32[]{:S(2)}) collective-permute-start(f32[48,128]{1,0:T(8,128)S(1)} %shard_map.30), channel_id=1, source_target_pairs={{0,4},{4,0},{8,12},{12,8},{1,5},{5,1},{9,13},{13,9},{2,6},{6,2},{1... | collective-permute-start | bytes 73736 | tf_op jit(solution)/shard_map/ppermute | solution.py:313
  8.3 0.1 fusion.2
  8.3 1.1 %collective-permute-done.2.far = f32[48,128]{1,0:T(8,128)S(1)} collective-permute-done((f32[48,128]{1,0:T(8,128)S(1)}, f32[48,128]{1,0:T(8,128)S(1)}, u32[]{:S(2)}, u32[]{:S(2)}) %collective-permute-start.2) | collective-permute-done | bytes 24608 | tf_op jit(solution)/shard_map/ppermute | solution.py:314
  9.4 0.0 collective-permute-done.1.near
  9.4 13.2 %shard_map.31 = (f32[8,32,128]{2,1,0:T(8,128)S(1)}, f32[4,32,128]{2,1,0:T(8,128)S(1)}, f32[4,32,128]{2,1,0:T(8,128)S(1)}) custom-call(f32[8,48,128]{2,1,0:T(8,128)S(1)} %get-tuple-element.11.mine, f32[8,4,8,128]{3,2,1,0:T(8,128)S(1)} %get-tuple-element.12.scale, f32[8,8,128]{2,1,0:T(8,128)S(1)} %collective-permute-done.layer, ...), custom_call_target="tpu_custom_call" | custom-call | tf_op jit(solution)/shard_map/pallas_call | solution.py:316
  22.6 3.4 %collective-permute-start.3 = (f32[4,32,128]{2,1,0:T(8,128)S(1)}, f32[4,32,128]{2,1,0:T(8,128)S(1)}, u32[]{:S(2)}, u32[]{:S(2)}) collective-permute-start(f32[4,32,128]{2,1,0:T(8,128)S(1)} %get-tuple-element.14), channel_id=1, source_target_pairs={{0,2},{1,3},{2,0},{3,1},{4,6},{5,7},{6,4},{7,5},{8,10},{9,11},{10,... | collective-permute-start | bytes 196616 | tf_op jit(solution)/shard_map/ppermute | solution.py:349
  26.0 0.1 collective-permute-start.5
  26.0 1.8 %collective-permute-start.6 = (f32[8,32,128]{2,1,0:T(8,128)S(1)}, f32[8,32,128]{2,1,0:T(8,128)S(1)}, u32[]{:S(2)}, u32[]{:S(2)}) collective-permute-start(f32[8,32,128]{2,1,0:T(8,128)S(1)} %get-tuple-element.15.refs_0_), channel_id=1, source_target_pairs={{0,1},{1,0},{2,3},{3,2},{4,5},{5,4},{6,7},{7,6},{8,9},{9,8},{10,11... | collective-permute-start | bytes 393224 | tf_op jit(solution)/shard_map/ppermute | solution.py:349
  27.9 0.1 fusion.1
  28.0 2.0 %collective-permute-done.3.refs_2_ = f32[4,32,128]{2,1,0:T(8,128)S(1)} collective-permute-done((f32[4,32,128]{2,1,0:T(8,128)S(1)}, f32[4,32,128]{2,1,0:T(8,128)S(1)}, u32[]{:S(2)}, u32[]{:S(2)}) %collective-permute-start.3) | collective-permute-done | bytes 65568 | tf_op jit(solution)/shard_map/ppermute | solution.py:349
  30.0 1.9 %collective-permute-start.4 = (f32[4,32,128]{2,1,0:T(8,128)S(1)}, f32[4,32,128]{2,1,0:T(8,128)S(1)}, u32[]{:S(2)}, u32[]{:S(2)}) collective-permute-start(f32[4,32,128]{2,1,0:T(8,128)S(1)} %collective-permute-done.3.refs_2_), channel_id=1, source_target_pairs={{0,1},{1,0},{2,3},{3,2},{4,5},{5,4},{6,7},{7,6},{8,9},{9,8},{10,11... | collective-permute-start | bytes 196616 | tf_op jit(solution)/shard_map/ppermute | solution.py:349
  31.9 0.3 collective-permute-done.5.refs_1_
  32.2 1.2 %collective-permute-start.7 = (f32[4,32,128]{2,1,0:T(8,128)S(1)}, f32[4,32,128]{2,1,0:T(8,128)S(1)}, u32[]{:S(2)}, u32[]{:S(2)}) collective-permute-start(f32[4,32,128]{2,1,0:T(8,128)S(1)} %collective-permute-done.5.refs_1_), channel_id=1, source_target_pairs={{0,1},{1,0},{2,3},{3,2},{4,5},{5,4},{6,7},{7,6},{8,9},{9,8},{10,11... | collective-permute-start | bytes 196616 | tf_op jit(solution)/shard_map/ppermute | solution.py:349
  33.4 0.1 fusion.refs_1_
  33.5 0.0 collective-permute-done.6.refs_3_
  33.5 3.0 %collective-permute-done.7.refs_4_ = f32[4,32,128]{2,1,0:T(8,128)S(1)} collective-permute-done((f32[4,32,128]{2,1,0:T(8,128)S(1)}, f32[4,32,128]{2,1,0:T(8,128)S(1)}, u32[]{:S(2)}, u32[]{:S(2)}) %collective-permute-start.7) | collective-permute-done | bytes 65568 | tf_op jit(solution)/shard_map/ppermute | solution.py:349
  36.5 1.4 %shard_map.32.refs_2_ = f32[8,128,128]{2,1,0:T(8,128)} custom-call(f32[8,32,128]{2,1,0:T(8,128)S(1)} %get-tuple-element.15.refs_0_, f32[4,32,128]{2,1,0:T(8,128)S(1)} %collective-permute-done.5.refs_1_, f32[4,32,128]{2,1,0:T(8,128)S(1)} %collective-permute-done.3.refs_2_, f32[8,32,128]{2,1,0:T(8,128)S(1)} %collective-permute-done.6.refs_3_, ...), custom_call_target="tpu_custom_call" | custom-call | tf_op jit(solution)/shard_map/pallas_call | solution.py:338
  37.9 0.0 collective-permute-done.4.refs_0_
  37.9 1.2 %shard_map.33 = f32[8,128,128]{2,1,0:T(8,128)} custom-call(f32[4,32,128]{2,1,0:T(8,128)S(1)} %collective-permute-done.4.refs_0_, s32[1,2]{1,0:T(1,128)S(1)} %fusion.refs_1_, f32[8,128,128]{2,1,0:T(8,128)} %shard_map.32.refs_2_), custom_call_target="tpu_custom_call", output_to_operand_aliasing={{}: (2, {})} | custom-call | tf_op jit(solution)/shard_map/pallas_call | solution.py:338
  (2 shorter events, 0.0 us)
Async XLA Ops:
  0.0 1.0 %copy-start = (f32[8,128,128]{2,1,0:T(8,128)S(1)}, f32[8,128,128]{2,1,0:T(8,128)}, u32[]{:S(2)}) copy-start(f32[8,128,128]{2,1,0:T(8,128)} %volume.3) | copy-start | bytes 1572868
  1.0 3.1 %copy-start.1 = (f32[8,128,128]{2,1,0:T(8,128)S(1)}, f32[8,128,128]{2,1,0:T(8,128)}, u32[]{:S(2)}) copy-start(f32[8,128,128]{2,1,0:T(8,128)} %volume.3) | copy-start | bytes 1572868
  1.1 4.9 %collective-permute-start = (f32[8,8,128]{2,1,0:T(8,128)S(1)}, f32[8,8,128]{2,1,0:T(8,128)S(1)}, u32[]{:S(2)}, u32[]{:S(2)}) collective-permute-start(f32[8,8,128]{2,1,0:T(8,128)S(1)} %shard_map.29), channel_id=1, source_target_pairs={{0,16},{1,17},{2,18},{3,19},{16,0},{17,1},{18,2},{19,3},{4,20},{5,... | collective-permute-start | bytes 98312 | tf_op jit(solution)/shard_map/ppermute | solution.py:295
  4.2 1.0 %copy-start.2 = (f32[8,128,128]{2,1,0:T(8,128)S(1)}, f32[8,128,128]{2,1,0:T(8,128)}, u32[]{:S(2)}) copy-start(f32[8,128,128]{2,1,0:T(8,128)} %strength.1) | copy-start | bytes 1572868
  6.1 3.3 %collective-permute-start.2 = (f32[48,128]{1,0:T(8,128)S(1)}, f32[48,128]{1,0:T(8,128)S(1)}, u32[]{:S(2)}, u32[]{:S(2)}) collective-permute-start(f32[48,128]{1,0:T(8,128)S(1)} %shard_map.30), channel_id=1, source_target_pairs={{0,12},{4,8},{8,4},{12,0},{1,13},{5,9},{9,5},{13,1},{2,14},{6,10},... | collective-permute-start | bytes 73736 | tf_op jit(solution)/shard_map/ppermute | solution.py:314
  6.4 3.0 %collective-permute-start.1 = (f32[48,128]{1,0:T(8,128)S(1)}, f32[48,128]{1,0:T(8,128)S(1)}, u32[]{:S(2)}, u32[]{:S(2)}) collective-permute-start(f32[48,128]{1,0:T(8,128)S(1)} %shard_map.30), channel_id=1, source_target_pairs={{0,4},{4,0},{8,12},{12,8},{1,5},{5,1},{9,13},{13,9},{2,6},{6,2},{1... | collective-permute-start | bytes 73736 | tf_op jit(solution)/shard_map/ppermute | solution.py:313
  22.6 7.4 %collective-permute-start.3 = (f32[4,32,128]{2,1,0:T(8,128)S(1)}, f32[4,32,128]{2,1,0:T(8,128)S(1)}, u32[]{:S(2)}, u32[]{:S(2)}) collective-permute-start(f32[4,32,128]{2,1,0:T(8,128)S(1)} %get-tuple-element.14), channel_id=1, source_target_pairs={{0,2},{1,3},{2,0},{3,1},{4,6},{5,7},{6,4},{7,5},{8,10},{9,11},{10,... | collective-permute-start | bytes 196616 | tf_op jit(solution)/shard_map/ppermute | solution.py:349
  26.0 6.3 %collective-permute-start.5 = (f32[4,32,128]{2,1,0:T(8,128)S(1)}, f32[4,32,128]{2,1,0:T(8,128)S(1)}, u32[]{:S(2)}, u32[]{:S(2)}) collective-permute-start(f32[4,32,128]{2,1,0:T(8,128)S(1)} %get-tuple-element.16), channel_id=1, source_target_pairs={{0,2},{1,3},{2,0},{3,1},{4,6},{5,7},{6,4},{7,5},{8,10},{9,11},{10,... | collective-permute-start | bytes 196616 | tf_op jit(solution)/shard_map/ppermute | solution.py:349
  26.0 7.5 %collective-permute-start.6 = (f32[8,32,128]{2,1,0:T(8,128)S(1)}, f32[8,32,128]{2,1,0:T(8,128)S(1)}, u32[]{:S(2)}, u32[]{:S(2)}) collective-permute-start(f32[8,32,128]{2,1,0:T(8,128)S(1)} %get-tuple-element.15.refs_0_), channel_id=1, source_target_pairs={{0,1},{1,0},{2,3},{3,2},{4,5},{5,4},{6,7},{7,6},{8,9},{9,8},{10,11... | collective-permute-start | bytes 393224 | tf_op jit(solution)/shard_map/ppermute | solution.py:349
  30.0 8.0 %collective-permute-start.4 = (f32[4,32,128]{2,1,0:T(8,128)S(1)}, f32[4,32,128]{2,1,0:T(8,128)S(1)}, u32[]{:S(2)}, u32[]{:S(2)}) collective-permute-start(f32[4,32,128]{2,1,0:T(8,128)S(1)} %collective-permute-done.3.refs_2_), channel_id=1, source_target_pairs={{0,1},{1,0},{2,3},{3,2},{4,5},{5,4},{6,7},{7,6},{8,9},{9,8},{10,11... | collective-permute-start | bytes 196616 | tf_op jit(solution)/shard_map/ppermute | solution.py:349
  32.2 4.3 %collective-permute-start.7 = (f32[4,32,128]{2,1,0:T(8,128)S(1)}, f32[4,32,128]{2,1,0:T(8,128)S(1)}, u32[]{:S(2)}, u32[]{:S(2)}) collective-permute-start(f32[4,32,128]{2,1,0:T(8,128)S(1)} %collective-permute-done.5.refs_1_), channel_id=1, source_target_pairs={{0,1},{1,0},{2,3},{3,2},{4,5},{5,4},{6,7},{7,6},{8,9},{9,8},{10,11... | collective-permute-start | bytes 196616 | tf_op jit(solution)/shard_map/ppermute | solution.py:349

commit v8 on v7

--- a/solution.py
+++ b/solution.py
@@ -254,9 +254,10 @@
         copies = []
         for n, part in enumerate(parts):
             at = pl.ds(pl.multiple_of(sources[n, 0] * rows, SUBS), rows)
-            slices = pl.ds(sources[n, 1], part.shape[0])
-            copies.append(pltpu.make_async_copy(part, out.at[slices, at, :], done.at[n]))
-            copies[n].start()
+            for z in range(part.shape[0]):
+                target = out.at[sources[n, 1] + z, at, :]
+                copies.append(pltpu.make_async_copy(part.at[z], target, done.at[len(copies)]))
+                copies[-1].start()
         for copy in copies:
             copy.wait()
 
@@ -340,7 +341,7 @@
             out_shape=shape(depth, size_x, size_y),
             in_specs=[VMEM] * count + [SMEM] + [HBM] * len(held),
             out_specs=HBM,
-            scratch_shapes=[pltpu.SemaphoreType.DMA((count,))],
+            scratch_shapes=[pltpu.SemaphoreType.DMA((sum(len(b) for *_, b in blocks),))],
             input_output_aliases={count + 1: 0} if held else {},
             compiler_params=small,
         )(*(block for *_, block in blocks), sources, *held)
@@ -356,7 +357,7 @@
     while bit > 1:
         bit //= 2
         blocks += [(step ^ bit, z, swapped(block, bit)) for step, z, block in blocks]
-    return place(blocks[-1:], place(blocks[:-1], None))
+    return place(blocks[-2:], place(blocks[:-2], None))
 
 
 def solution(mesh):

time: 39.3 us -> 38 us (0.967)
  waiting for transfers between devices: 6.97 us -> 5.51 us
    ppermute x5, waiting for transfers between devices: 5.34 us -> 3.9 us  [swapped(): return lax.ppermute(block, 'off', [(i, i ^ bit) for i in range(offs)])]
  transfers between devices with their start and end apart: 8 -> 8, of which waited for: 5 -> 5; matrix products, arithmetic and copies ran while one was open for 1% -> 1% of each run, Pallas kernels for 4% -> 5%
where the time goes in v8:
time: 38 us; the launch traced here: 37.8 us
  Pallas kernels  16.3 us (43%)
  starting transfers between devices  13.6 us (36%)
  waiting for transfers between devices  5.51 us (14%)
  local copies, waits for them, and re-layouts  2.09 us (6%)
    pallas_call x1, Pallas kernels, shards(): pl.pallas_call(main_kernel(depth, rows, blocks, size_x), out_shape=[shape...  13.2 us
    ppermute x5, starting transfers between devices, swapped(): return lax.ppermute(block, 'off', [(i, i ^ bit) for i in range(offs)])  8.39 us
    ppermute x5, waiting for transfers between devices, swapped(): return lax.ppermute(block, 'off', [(i, i ^ bit) for i in range(offs)])  3.9 us
    ppermute x1, starting transfers between devices, shards(): layer = lax.ppermute(layer, ('gx', 'off'), moves)  3.03 us
    pallas_call x2, Pallas kernels, place(): pl.pallas_call(place_kernel(count, rows), out_shape=shape(depth, size_x,...  2.78 us
    unnamed x6, local copies, waits for them, and re-layouts  2.09 us
    ppermute x1, starting transfers between devices, shards(): near = lax.ppermute(strips, 'gy', list(enumerate(first)))  1.83 us
    ppermute x1, waiting for transfers between devices, shards(): far = lax.ppermute(strips, 'gy', list(enumerate(second)))  1.13 us
  transfers between devices with their start and end apart: 8, of which 5 were waited for; matrix products, arithmetic and copies ran while one was open for 1% of the time, Pallas kernels for 5%

profile of v8, /device:TPU:0, one launch (start us, length us, event | category | flops | bytes accessed | tf_op | source)
XLA Modules:
  0.0 37.8 jit_solution(8445077414664979254)
XLA Ops:
  0.0 0.0 copy-start
  0.0 1.0 %copy-done = f32[8,128,128]{2,1,0:T(8,128)S(1)} copy-done((f32[8,128,128]{2,1,0:T(8,128)S(1)}, f32[8,128,128]{2,1,0:T(8,128)}, u32[]{:S(2)}) %copy-start) | copy-done | bytes 524312
  1.0 0.0 copy-start.1
  1.1 3.0 %collective-permute-start = (f32[8,8,128]{2,1,0:T(8,128)S(1)}, f32[8,8,128]{2,1,0:T(8,128)S(1)}, u32[]{:S(2)}, u32[]{:S(2)}) collective-permute-start(f32[8,8,128]{2,1,0:T(8,128)S(1)} %shard_map.29), channel_id=1, source_target_pairs={{0,16},{1,17},{2,18},{3,19},{16,0},{17,1},{18,2},{19,3},{4,20},{5,... | collective-permute-start | bytes 98312 | tf_op jit(solution)/shard_map/ppermute | solution.py:296
  4.1 0.1 fusion.3
  4.2 0.1 fusion.1
  4.3 0.0 copy-done.1
  4.3 0.0 copy-start.2
  4.3 1.0 %copy-done.2 = f32[8,128,128]{2,1,0:T(8,128)S(1)} copy-done((f32[8,128,128]{2,1,0:T(8,128)S(1)}, f32[8,128,128]{2,1,0:T(8,128)}, u32[]{:S(2)}) %copy-start.2) | copy-done | bytes 524312
  5.3 0.2 shard_map.28
  5.5 0.5 %collective-permute-done.layer = f32[8,8,128]{2,1,0:T(8,128)S(1)} collective-permute-done((f32[8,8,128]{2,1,0:T(8,128)S(1)}, f32[8,8,128]{2,1,0:T(8,128)S(1)}, u32[]{:S(2)}, u32[]{:S(2)}) %collective-permute-start) | collective-permute-done | bytes 32800 | tf_op jit(solution)/shard_map/ppermute | solution.py:296
  6.0 0.1 shard_map.30
  6.1 0.3 collective-permute-start.2
  6.4 1.8 %collective-permute-start.1 = (f32[48,128]{1,0:T(8,128)S(1)}, f32[48,128]{1,0:T(8,128)S(1)}, u32[]{:S(2)}, u32[]{:S(2)}) collective-permute-start(f32[48,128]{1,0:T(8,128)S(1)} %shard_map.30), channel_id=1, source_target_pairs={{0,4},{4,0},{8,12},{12,8},{1,5},{5,1},{9,13},{13,9},{2,6},{6,2},{1... | collective-permute-start | bytes 73736 | tf_op jit(solution)/shard_map/ppermute | solution.py:314
  8.3 1.1 %collective-permute-done.2.far = f32[48,128]{1,0:T(8,128)S(1)} collective-permute-done((f32[48,128]{1,0:T(8,128)S(1)}, f32[48,128]{1,0:T(8,128)S(1)}, u32[]{:S(2)}, u32[]{:S(2)}) %collective-permute-start.2) | collective-permute-done | bytes 24608 | tf_op jit(solution)/shard_map/ppermute | solution.py:315
  9.4 0.0 collective-permute-done.1.near
  9.4 13.2 %shard_map.31 = (f32[8,32,128]{2,1,0:T(8,128)S(1)}, f32[4,32,128]{2,1,0:T(8,128)S(1)}, f32[4,32,128]{2,1,0:T(8,128)S(1)}) custom-call(f32[8,48,128]{2,1,0:T(8,128)S(1)} %get-tuple-element.11.mine, f32[8,4,8,128]{3,2,1,0:T(8,128)S(1)} %get-tuple-element.12.scale, f32[8,8,128]{2,1,0:T(8,128)S(1)} %collective-permute-done.layer, ...), custom_call_target="tpu_custom_call" | custom-call | tf_op jit(solution)/shard_map/pallas_call | solution.py:317
  22.6 3.4 %collective-permute-start.3 = (f32[4,32,128]{2,1,0:T(8,128)S(1)}, f32[4,32,128]{2,1,0:T(8,128)S(1)}, u32[]{:S(2)}, u32[]{:S(2)}) collective-permute-start(f32[4,32,128]{2,1,0:T(8,128)S(1)} %get-tuple-element.14), channel_id=1, source_target_pairs={{0,2},{1,3},{2,0},{3,1},{4,6},{5,7},{6,4},{7,5},{8,10},{9,11},{10,... | collective-permute-start | bytes 196616 | tf_op jit(solution)/shard_map/ppermute | solution.py:350
  26.0 0.1 collective-permute-start.5
  26.0 1.8 %collective-permute-start.7 = (f32[8,32,128]{2,1,0:T(8,128)S(1)}, f32[8,32,128]{2,1,0:T(8,128)S(1)}, u32[]{:S(2)}, u32[]{:S(2)}) collective-permute-start(f32[8,32,128]{2,1,0:T(8,128)S(1)} %get-tuple-element.16.refs_0_), channel_id=1, source_target_pairs={{0,1},{1,0},{2,3},{3,2},{4,5},{5,4},{6,7},{7,6},{8,9},{9,8},{10,11... | collective-permute-start | bytes 393224 | tf_op jit(solution)/shard_map/ppermute | solution.py:350
  27.9 0.1 fusion
  27.9 2.0 %collective-permute-done.3.refs_1_ = f32[4,32,128]{2,1,0:T(8,128)S(1)} collective-permute-done((f32[4,32,128]{2,1,0:T(8,128)S(1)}, f32[4,32,128]{2,1,0:T(8,128)S(1)}, u32[]{:S(2)}, u32[]{:S(2)}) %collective-permute-start.3) | collective-permute-done | bytes 65568 | tf_op jit(solution)/shard_map/ppermute | solution.py:350
  30.0 1.9 %collective-permute-start.4 = (f32[4,32,128]{2,1,0:T(8,128)S(1)}, f32[4,32,128]{2,1,0:T(8,128)S(1)}, u32[]{:S(2)}, u32[]{:S(2)}) collective-permute-start(f32[4,32,128]{2,1,0:T(8,128)S(1)} %collective-permute-done.3.refs_1_), channel_id=1, source_target_pairs={{0,1},{1,0},{2,3},{3,2},{4,5},{5,4},{6,7},{7,6},{8,9},{9,8},{10,11... | collective-permute-start | bytes 196616 | tf_op jit(solution)/shard_map/ppermute | solution.py:350
  31.9 0.3 collective-permute-done.5.refs_2_
  32.2 1.2 %collective-permute-start.6 = (f32[4,32,128]{2,1,0:T(8,128)S(1)}, f32[4,32,128]{2,1,0:T(8,128)S(1)}, u32[]{:S(2)}, u32[]{:S(2)}) collective-permute-start(f32[4,32,128]{2,1,0:T(8,128)S(1)} %collective-permute-done.5.refs_2_), channel_id=1, source_target_pairs={{0,1},{1,0},{2,3},{3,2},{4,5},{5,4},{6,7},{7,6},{8,9},{9,8},{10,11... | collective-permute-start | bytes 196616 | tf_op jit(solution)/shard_map/ppermute | solution.py:350
  33.4 0.0 collective-permute-done.7.refs_3_
  33.4 1.5 %shard_map.32.refs_3_ = f32[8,128,128]{2,1,0:T(8,128)} custom-call(f32[8,32,128]{2,1,0:T(8,128)S(1)} %get-tuple-element.16.refs_0_, f32[4,32,128]{2,1,0:T(8,128)S(1)} %collective-permute-done.3.refs_1_, f32[4,32,128]{2,1,0:T(8,128)S(1)} %collective-permute-done.5.refs_2_, f32[8,32,128]{2,1,0:T(8,128)S(1)} %collective-permute-done.7.refs_3_, ...), custom_call_target="tpu_custom_call" | custom-call | tf_op jit(solution)/shard_map/pallas_call | solution.py:339
  34.9 0.0 collective-permute-done.4.refs_0_
  35.0 1.5 %collective-permute-done.6.refs_1_ = f32[4,32,128]{2,1,0:T(8,128)S(1)} collective-permute-done((f32[4,32,128]{2,1,0:T(8,128)S(1)}, f32[4,32,128]{2,1,0:T(8,128)S(1)}, u32[]{:S(2)}, u32[]{:S(2)}) %collective-permute-start.6) | collective-permute-done | bytes 65568 | tf_op jit(solution)/shard_map/ppermute | solution.py:350
  36.5 1.3 %shard_map.33 = f32[8,128,128]{2,1,0:T(8,128)} custom-call(f32[4,32,128]{2,1,0:T(8,128)S(1)} %collective-permute-done.4.refs_0_, f32[4,32,128]{2,1,0:T(8,128)S(1)} %collective-permute-done.6.refs_1_, s32[2,2]{1,0:T(2,128)S(1)} %pad_add_fusion.1.refs_2_, f32[8,128,128]{2,1,0:T(8,128)} %shard_map.32.refs_3_), custom_call_target="tpu_custom_call", output_to_operand_aliasing={{}: (3, {})} | custom-call | tf_op jit(solution)/shard_map/pallas_call | solution.py:339
  (3 shorter events, 0.0 us)
Async XLA Ops:
  0.0 1.0 %copy-start = (f32[8,128,128]{2,1,0:T(8,128)S(1)}, f32[8,128,128]{2,1,0:T(8,128)}, u32[]{:S(2)}) copy-start(f32[8,128,128]{2,1,0:T(8,128)} %volume.3) | copy-start | bytes 1572868
  1.0 3.2 %copy-start.1 = (f32[8,128,128]{2,1,0:T(8,128)S(1)}, f32[8,128,128]{2,1,0:T(8,128)}, u32[]{:S(2)}) copy-start(f32[8,128,128]{2,1,0:T(8,128)} %volume.3) | copy-start | bytes 1572868
  1.1 4.9 %collective-permute-start = (f32[8,8,128]{2,1,0:T(8,128)S(1)}, f32[8,8,128]{2,1,0:T(8,128)S(1)}, u32[]{:S(2)}, u32[]{:S(2)}) collective-permute-start(f32[8,8,128]{2,1,0:T(8,128)S(1)} %shard_map.29), channel_id=1, source_target_pairs={{0,16},{1,17},{2,18},{3,19},{16,0},{17,1},{18,2},{19,3},{4,20},{5,... | collective-permute-start | bytes 98312 | tf_op jit(solution)/shard_map/ppermute | solution.py:296
  4.3 1.0 %copy-start.2 = (f32[8,128,128]{2,1,0:T(8,128)S(1)}, f32[8,128,128]{2,1,0:T(8,128)}, u32[]{:S(2)}) copy-start(f32[8,128,128]{2,1,0:T(8,128)} %strength.1) | copy-start | bytes 1572868
  6.1 3.3 %collective-permute-start.2 = (f32[48,128]{1,0:T(8,128)S(1)}, f32[48,128]{1,0:T(8,128)S(1)}, u32[]{:S(2)}, u32[]{:S(2)}) collective-permute-start(f32[48,128]{1,0:T(8,128)S(1)} %shard_map.30), channel_id=1, source_target_pairs={{0,12},{4,8},{8,4},{12,0},{1,13},{5,9},{9,5},{13,1},{2,14},{6,10},... | collective-permute-start | bytes 73736 | tf_op jit(solution)/shard_map/ppermute | solution.py:315
  6.4 3.0 %collective-permute-start.1 = (f32[48,128]{1,0:T(8,128)S(1)}, f32[48,128]{1,0:T(8,128)S(1)}, u32[]{:S(2)}, u32[]{:S(2)}) collective-permute-start(f32[48,128]{1,0:T(8,128)S(1)} %shard_map.30), channel_id=1, source_target_pairs={{0,4},{4,0},{8,12},{12,8},{1,5},{5,1},{9,13},{13,9},{2,6},{6,2},{1... | collective-permute-start | bytes 73736 | tf_op jit(solution)/shard_map/ppermute | solution.py:314
  22.6 7.4 %collective-permute-start.3 = (f32[4,32,128]{2,1,0:T(8,128)S(1)}, f32[4,32,128]{2,1,0:T(8,128)S(1)}, u32[]{:S(2)}, u32[]{:S(2)}) collective-permute-start(f32[4,32,128]{2,1,0:T(8,128)S(1)} %get-tuple-element.14), channel_id=1, source_target_pairs={{0,2},{1,3},{2,0},{3,1},{4,6},{5,7},{6,4},{7,5},{8,10},{9,11},{10,... | collective-permute-start | bytes 196616 | tf_op jit(solution)/shard_map/ppermute | solution.py:350
  26.0 6.3 %collective-permute-start.5 = (f32[4,32,128]{2,1,0:T(8,128)S(1)}, f32[4,32,128]{2,1,0:T(8,128)S(1)}, u32[]{:S(2)}, u32[]{:S(2)}) collective-permute-start(f32[4,32,128]{2,1,0:T(8,128)S(1)} %get-tuple-element.15), channel_id=1, source_target_pairs={{0,2},{1,3},{2,0},{3,1},{4,6},{5,7},{6,4},{7,5},{8,10},{9,11},{10,... | collective-permute-start | bytes 196616 | tf_op jit(solution)/shard_map/ppermute | solution.py:350
  26.0 7.4 %collective-permute-start.7 = (f32[8,32,128]{2,1,0:T(8,128)S(1)}, f32[8,32,128]{2,1,0:T(8,128)S(1)}, u32[]{:S(2)}, u32[]{:S(2)}) collective-permute-start(f32[8,32,128]{2,1,0:T(8,128)S(1)} %get-tuple-element.16.refs_0_), channel_id=1, source_target_pairs={{0,1},{1,0},{2,3},{3,2},{4,5},{5,4},{6,7},{7,6},{8,9},{9,8},{10,11... | collective-permute-start | bytes 393224 | tf_op jit(solution)/shard_map/ppermute | solution.py:350
  30.0 5.0 %collective-permute-start.4 = (f32[4,32,128]{2,1,0:T(8,128)S(1)}, f32[4,32,128]{2,1,0:T(8,128)S(1)}, u32[]{:S(2)}, u32[]{:S(2)}) collective-permute-start(f32[4,32,128]{2,1,0:T(8,128)S(1)} %collective-permute-done.3.refs_1_), channel_id=1, source_target_pairs={{0,1},{1,0},{2,3},{3,2},{4,5},{5,4},{6,7},{7,6},{8,9},{9,8},{10,11... | collective-permute-start | bytes 196616 | tf_op jit(solution)/shard_map/ppermute | solution.py:350
  32.2 4.3 %collective-permute-start.6 = (f32[4,32,128]{2,1,0:T(8,128)S(1)}, f32[4,32,128]{2,1,0:T(8,128)S(1)}, u32[]{:S(2)}, u32[]{:S(2)}) collective-permute-start(f32[4,32,128]{2,1,0:T(8,128)S(1)} %collective-permute-done.5.refs_2_), channel_id=1, source_target_pairs={{0,1},{1,0},{2,3},{3,2},{4,5},{5,4},{6,7},{7,6},{8,9},{9,8},{10,11... | collective-permute-start | bytes 196616 | tf_op jit(solution)/shard_map/ppermute | solution.py:350

commit v9 on v7

--- a/solution.py
+++ b/solution.py
@@ -131,13 +131,13 @@
                 if r in ends:
                     v = jnp.where(ends[r][0], jnp.where(ends[r][1], 0.0, layer[z]), v)
                 h = pltpu.roll(lines[r], LANES - 16 * z, 1)
-                flat[3, at, :] = v
+                flat[z, 3, at, :] = v
                 for c in range(1, 4):
-                    flat[3 + c, at, :] = pltpu.roll(jnp.where(lane < c, h, v), LANES - c, 1)
-                    flat[3 - c, at, :] = pltpu.roll(jnp.where(lane >= LANES - c, h, v), c, 1)
+                    flat[z, 3 + c, at, :] = pltpu.roll(jnp.where(lane < c, h, v), LANES - c, 1)
+                    flat[z, 3 - c, at, :] = pltpu.roll(jnp.where(lane >= LANES - c, h, v), c, 1)
             for i in range(wide):
                 for c in range(7):
-                    v = flat[c, pl.ds(SUBS - 3 + i, SUBS, stride=blocks), :]
+                    v = flat[z, c, pl.ds(SUBS - 3 + i, SUBS, stride=blocks), :]
                     vals[c, z, i] = v
                     if 2 <= c <= 4 and 2 <= i < wide - 2:
                         cent[c - 2, z, i - 2] = (-2.0 * GAIN if c == 3 else -2.0) * v
@@ -248,14 +248,15 @@
                 ref[at, pl.ds(i, SUBS, stride=blocks), :] = value
 
 
-def place_kernel(count, rows):
+def place_kernel(sources, rows):
     def kernel(*refs):
-        parts, sources, (*_, out, done) = refs[:count], refs[count], refs[count + 1 :]
+        parts, (*_, out, done) = refs[: len(sources)], refs[len(sources) :]
+        off = lax.axis_index("off")
         copies = []
-        for n, part in enumerate(parts):
-            at = pl.ds(pl.multiple_of(sources[n, 0] * rows, SUBS), rows)
-            slices = pl.ds(sources[n, 1], part.shape[0])
-            copies.append(pltpu.make_async_copy(part, out.at[slices, at, :], done.at[n]))
+        for n, (part, (step, z)) in enumerate(zip(parts, sources)):
+            at = pl.ds(pl.multiple_of((off ^ step) * rows, SUBS), rows)
+            target = out.at[z : z + part.shape[0], at, :]
+            copies.append(pltpu.make_async_copy(part, target, done.at[n]))
             copies[n].start()
         for copy in copies:
             copy.wait()
@@ -319,7 +320,7 @@
         in_specs=[VMEM] * 5,
         out_specs=[VMEM] * 3,
         scratch_shapes=[
-            pltpu.VMEM((7, tall, LANES), f32),
+            pltpu.VMEM((depth, 7, tall, LANES), f32),
             pltpu.VMEM((7, depth, blocks + 6) + tile, f32),
             pltpu.VMEM((3, depth, blocks + 2) + tile, f32),
             pltpu.VMEM((5, depth + 2, blocks + 4) + tile, f32),
@@ -328,35 +329,30 @@
         compiler_params=pltpu.CompilerParams(vmem_limit_bytes=16 * 2**20),
     )(mine, scale, layer, near, far)
 
-    off = lax.axis_index("off")
-    SMEM = pl.BlockSpec(memory_space=pltpu.SMEM)
-
     def place(blocks, whole):
         count = len(blocks)
         held = [] if whole is None else [whole]
-        sources = jnp.stack([jnp.stack([off ^ step, z]) for step, z, _ in blocks]).astype(jnp.int32)
         return pl.pallas_call(
-            place_kernel(count, rows),
+            place_kernel([source for source, _ in blocks], rows),
             out_shape=shape(depth, size_x, size_y),
-            in_specs=[VMEM] * count + [SMEM] + [HBM] * len(held),
+            in_specs=[VMEM] * count + [HBM] * len(held),
             out_specs=HBM,
             scratch_shapes=[pltpu.SemaphoreType.DMA((count,))],
-            input_output_aliases={count + 1: 0} if held else {},
+            input_output_aliases={count: 0} if held else {},
             compiler_params=small,
-        )(*(block for *_, block in blocks), sources, *held)
+        )(*(block for _, block in blocks), *held)
 
     def swapped(block, bit):
         return lax.ppermute(block, "off", [(i, i ^ bit) for i in range(offs)])
 
     assert offs & (offs - 1) == 0
-    zero = jnp.int32(0)
     bit = offs // 2
-    blocks = [(0, zero, part)]
-    blocks += [(bit, zero + half * n, swapped(halves[n], bit)) for n in range(2)]
+    blocks = [((0, 0), part)]
+    blocks += [((bit, half * n), swapped(halves[n], bit)) for n in range(2)]
     while bit > 1:
         bit //= 2
-        blocks += [(step ^ bit, z, swapped(block, bit)) for step, z, block in blocks]
-    return place(blocks[-1:], place(blocks[:-1], None))
+        blocks += [((step ^ bit, z), swapped(block, bit)) for (step, z), block in blocks]
+    return place(blocks[-2:], place(blocks[:-2], None))
 
 
 def solution(mesh):

time: 39.3 us -> 38.7 us (0.985)
  waiting for transfers between devices: 6.97 us -> 10.4 us
  Pallas kernels: 16.1 us -> 14.7 us
  starting transfers between devices: 13.6 us -> 12.4 us
  local copies, waits for them, and re-layouts: 2.11 us -> 1.04 us
    ppermute x5, waiting for transfers between devices: 5.34 us -> 7.6 us  [swapped(): return lax.ppermute(block, 'off', [(i, i ^ bit) for i in range(offs)])]
    ppermute x5, starting transfers between devices: 8.39 us -> 7.19 us  [swapped(): return lax.ppermute(block, 'off', [(i, i ^ bit) for i in range(offs)])]
    pallas_call x2, Pallas kernels: 2.59 us -> 1.44 us  [place(): pl.pallas_call(place_kernel([source for source, _ in blocks], rows), out_...]
    ppermute x1, waiting for transfers between devices: 0.56 us -> 1.67 us  [shards(): layer = lax.ppermute(layer, ('gx', 'off'), moves)]
    unnamed x6 -> x4, local copies, waits for them, and re-layouts: 2.09 us -> 1.04 us
  transfers between devices with their start and end apart: 8 -> 8, of which waited for: 5 -> 5; matrix products, arithmetic and copies ran while one was open for 1% -> 0% of each run, Pallas kernels for 4% -> 3%
where the time goes in v9:
time: 38.7 us; the launch traced here: 38.6 us
  Pallas kernels  14.7 us (38%)
  starting transfers between devices  12.4 us (32%)
  waiting for transfers between devices  10.4 us (27%)
  local copies, waits for them, and re-layouts  1.04 us (3%)
    pallas_call x1, Pallas kernels, shards(): pl.pallas_call(main_kernel(depth, rows, blocks, size_x), out_shape=[shape...  12.9 us
    ppermute x5, waiting for transfers between devices, swapped(): return lax.ppermute(block, 'off', [(i, i ^ bit) for i in range(offs)])  7.6 us
    ppermute x5, starting transfers between devices, swapped(): return lax.ppermute(block, 'off', [(i, i ^ bit) for i in range(offs)])  7.19 us
    ppermute x1, starting transfers between devices, shards(): layer = lax.ppermute(layer, ('gx', 'off'), moves)  3.03 us
    ppermute x1, starting transfers between devices, shards(): near = lax.ppermute(strips, 'gy', list(enumerate(first)))  1.83 us
    ppermute x1, waiting for transfers between devices, shards(): layer = lax.ppermute(layer, ('gx', 'off'), moves)  1.67 us
    pallas_call x2, Pallas kernels, place(): pl.pallas_call(place_kernel([source for source, _ in blocks], rows), out_...  1.44 us
    ppermute x1, waiting for transfers between devices, shards(): far = lax.ppermute(strips, 'gy', list(enumerate(second)))  1.14 us
  transfers between devices with their start and end apart: 8, of which 5 were waited for; matrix products, arithmetic and copies ran while one was open for 0% of the time, Pallas kernels for 3%

profile of v9, /device:TPU:0, one launch (start us, length us, event | category | flops | bytes accessed | tf_op | source)
XLA Modules:
  0.0 38.6 jit_solution(5323874659449248960)
XLA Ops:
  0.0 0.0 copy-start
  0.0 1.0 %copy-done = f32[8,128,128]{2,1,0:T(8,128)S(1)} copy-done((f32[8,128,128]{2,1,0:T(8,128)S(1)}, f32[8,128,128]{2,1,0:T(8,128)}, u32[]{:S(2)}) %copy-start) | copy-done | bytes 524312
  1.0 0.0 copy-start.1
  1.1 3.0 %collective-permute-start = (f32[8,8,128]{2,1,0:T(8,128)S(1)}, f32[8,8,128]{2,1,0:T(8,128)S(1)}, u32[]{:S(2)}, u32[]{:S(2)}) collective-permute-start(f32[8,8,128]{2,1,0:T(8,128)S(1)} %shard_map.29), channel_id=1, source_target_pairs={{0,16},{1,17},{2,18},{3,19},{16,0},{17,1},{18,2},{19,3},{4,20},{5,... | collective-permute-start | bytes 98312 | tf_op jit(solution)/shard_map/ppermute | solution.py:296
  4.1 0.0 copy-done.1
  4.1 0.2 shard_map.28
  4.3 1.7 %collective-permute-done.layer = f32[8,8,128]{2,1,0:T(8,128)S(1)} collective-permute-done((f32[8,8,128]{2,1,0:T(8,128)S(1)}, f32[8,8,128]{2,1,0:T(8,128)S(1)}, u32[]{:S(2)}, u32[]{:S(2)}) %collective-permute-start) | collective-permute-done | bytes 32800 | tf_op jit(solution)/shard_map/ppermute | solution.py:296
  6.0 0.1 shard_map.30
  6.1 0.3 collective-permute-start.2
  6.4 1.8 %collective-permute-start.1 = (f32[48,128]{1,0:T(8,128)S(1)}, f32[48,128]{1,0:T(8,128)S(1)}, u32[]{:S(2)}, u32[]{:S(2)}) collective-permute-start(f32[48,128]{1,0:T(8,128)S(1)} %shard_map.30), channel_id=1, source_target_pairs={{0,4},{4,0},{8,12},{12,8},{1,5},{5,1},{9,13},{13,9},{2,6},{6,2},{1... | collective-permute-start | bytes 73736 | tf_op jit(solution)/shard_map/ppermute | solution.py:314
  8.3 1.1 %collective-permute-done.2.far = f32[48,128]{1,0:T(8,128)S(1)} collective-permute-done((f32[48,128]{1,0:T(8,128)S(1)}, f32[48,128]{1,0:T(8,128)S(1)}, u32[]{:S(2)}, u32[]{:S(2)}) %collective-permute-start.2) | collective-permute-done | bytes 24608 | tf_op jit(solution)/shard_map/ppermute | solution.py:315
  9.4 0.0 collective-permute-done.1.near
  9.4 12.9 %shard_map.31 = (f32[8,32,128]{2,1,0:T(8,128)S(1)}, f32[4,32,128]{2,1,0:T(8,128)S(1)}, f32[4,32,128]{2,1,0:T(8,128)S(1)}) custom-call(f32[8,48,128]{2,1,0:T(8,128)S(1)} %get-tuple-element.11.mine, f32[8,4,8,128]{3,2,1,0:T(8,128)S(1)} %get-tuple-element.12.scale, f32[8,8,128]{2,1,0:T(8,128)S(1)} %collective-permute-done.layer, ...), custom_call_target="tpu_custom_call" | custom-call | tf_op jit(solution)/shard_map/pallas_call | solution.py:317
  22.3 3.4 %collective-permute-start.3 = (f32[4,32,128]{2,1,0:T(8,128)S(1)}, f32[4,32,128]{2,1,0:T(8,128)S(1)}, u32[]{:S(2)}, u32[]{:S(2)}) collective-permute-start(f32[4,32,128]{2,1,0:T(8,128)S(1)} %get-tuple-element.14), channel_id=1, source_target_pairs={{0,2},{1,3},{2,0},{3,1},{4,6},{5,7},{6,4},{7,5},{8,10},{9,11},{10,... | collective-permute-start | bytes 196616 | tf_op jit(solution)/shard_map/ppermute | solution.py:346
  25.7 1.6 %collective-permute-start.7 = (f32[8,32,128]{2,1,0:T(8,128)S(1)}, f32[8,32,128]{2,1,0:T(8,128)S(1)}, u32[]{:S(2)}, u32[]{:S(2)}) collective-permute-start(f32[8,32,128]{2,1,0:T(8,128)S(1)} %get-tuple-element.16.refs_0_), channel_id=1, source_target_pairs={{0,1},{1,0},{2,3},{3,2},{4,5},{5,4},{6,7},{7,6},{8,9},{9,8},{10,11... | collective-permute-start | bytes 393224 | tf_op jit(solution)/shard_map/ppermute | solution.py:346
  27.3 0.3 collective-permute-start.5
  27.6 1.4 %collective-permute-done.3.refs_1_ = f32[4,32,128]{2,1,0:T(8,128)S(1)} collective-permute-done((f32[4,32,128]{2,1,0:T(8,128)S(1)}, f32[4,32,128]{2,1,0:T(8,128)S(1)}, u32[]{:S(2)}, u32[]{:S(2)}) %collective-permute-start.3) | collective-permute-done | bytes 65568 | tf_op jit(solution)/shard_map/ppermute | solution.py:346
  29.0 1.5 %collective-permute-start.4 = (f32[4,32,128]{2,1,0:T(8,128)S(1)}, f32[4,32,128]{2,1,0:T(8,128)S(1)}, u32[]{:S(2)}, u32[]{:S(2)}) collective-permute-start(f32[4,32,128]{2,1,0:T(8,128)S(1)} %collective-permute-done.3.refs_1_), channel_id=1, source_target_pairs={{0,1},{1,0},{2,3},{3,2},{4,5},{5,4},{6,7},{7,6},{8,9},{9,8},{10,11... | collective-permute-start | bytes 196616 | tf_op jit(solution)/shard_map/ppermute | solution.py:346
  30.5 3.1 %collective-permute-done.5.refs_2_ = f32[4,32,128]{2,1,0:T(8,128)S(1)} collective-permute-done((f32[4,32,128]{2,1,0:T(8,128)S(1)}, f32[4,32,128]{2,1,0:T(8,128)S(1)}, u32[]{:S(2)}, u32[]{:S(2)}) %collective-permute-start.5) | collective-permute-done | bytes 65568 | tf_op jit(solution)/shard_map/ppermute | solution.py:346
  33.6 0.4 collective-permute-start.6
  34.0 0.0 collective-permute-done.7.refs_3_
  34.0 0.8 %shard_map.32.refs_2_ = f32[8,128,128]{2,1,0:T(8,128)} custom-call(f32[8,32,128]{2,1,0:T(8,128)S(1)} %get-tuple-element.16.refs_0_, f32[4,32,128]{2,1,0:T(8,128)S(1)} %collective-permute-done.3.refs_1_, f32[4,32,128]{2,1,0:T(8,128)S(1)} %collective-permute-done.5.refs_2_, f32[8,32,128]{2,1,0:T(8,128)S(1)} %collective-permute-done.7.refs_3_), custom_call_target="tpu_custom_call" | custom-call | tf_op jit(solution)/shard_map/pallas_call | solution.py:335
  34.8 0.0 collective-permute-done.4.refs_0_
  34.8 3.1 %collective-permute-done.6.refs_1_ = f32[4,32,128]{2,1,0:T(8,128)S(1)} collective-permute-done((f32[4,32,128]{2,1,0:T(8,128)S(1)}, f32[4,32,128]{2,1,0:T(8,128)S(1)}, u32[]{:S(2)}, u32[]{:S(2)}) %collective-permute-start.6) | collective-permute-done | bytes 65568 | tf_op jit(solution)/shard_map/ppermute | solution.py:346
  37.9 0.7 %shard_map.33 = f32[8,128,128]{2,1,0:T(8,128)} custom-call(f32[4,32,128]{2,1,0:T(8,128)S(1)} %collective-permute-done.4.refs_0_, f32[4,32,128]{2,1,0:T(8,128)S(1)} %collective-permute-done.6.refs_1_, f32[8,128,128]{2,1,0:T(8,128)} %shard_map.32.refs_2_), custom_call_target="tpu_custom_call", output_to_operand_aliasing={{}: (2, {})} | custom-call | tf_op jit(solution)/shard_map/pallas_call | solution.py:335
  (1 shorter events, 0.0 us)
Async XLA Ops:
  0.0 1.0 %copy-start = (f32[8,128,128]{2,1,0:T(8,128)S(1)}, f32[8,128,128]{2,1,0:T(8,128)}, u32[]{:S(2)}) copy-start(f32[8,128,128]{2,1,0:T(8,128)} %volume.3) | copy-start | bytes 1572868
  1.0 3.1 %copy-start.1 = (f32[8,128,128]{2,1,0:T(8,128)S(1)}, f32[8,128,128]{2,1,0:T(8,128)}, u32[]{:S(2)}) copy-start(f32[8,128,128]{2,1,0:T(8,128)} %strength.1) | copy-start | bytes 1572868
  1.1 4.9 %collective-permute-start = (f32[8,8,128]{2,1,0:T(8,128)S(1)}, f32[8,8,128]{2,1,0:T(8,128)S(1)}, u32[]{:S(2)}, u32[]{:S(2)}) collective-permute-start(f32[8,8,128]{2,1,0:T(8,128)S(1)} %shard_map.29), channel_id=1, source_target_pairs={{0,16},{1,17},{2,18},{3,19},{16,0},{17,1},{18,2},{19,3},{4,20},{5,... | collective-permute-start | bytes 98312 | tf_op jit(solution)/shard_map/ppermute | solution.py:296
  6.1 3.3 %collective-permute-start.2 = (f32[48,128]{1,0:T(8,128)S(1)}, f32[48,128]{1,0:T(8,128)S(1)}, u32[]{:S(2)}, u32[]{:S(2)}) collective-permute-start(f32[48,128]{1,0:T(8,128)S(1)} %shard_map.30), channel_id=1, source_target_pairs={{0,12},{4,8},{8,4},{12,0},{1,13},{5,9},{9,5},{13,1},{2,14},{6,10},... | collective-permute-start | bytes 73736 | tf_op jit(solution)/shard_map/ppermute | solution.py:315
  6.4 3.0 %collective-permute-start.1 = (f32[48,128]{1,0:T(8,128)S(1)}, f32[48,128]{1,0:T(8,128)S(1)}, u32[]{:S(2)}, u32[]{:S(2)}) collective-permute-start(f32[48,128]{1,0:T(8,128)S(1)} %shard_map.30), channel_id=1, source_target_pairs={{0,4},{4,0},{8,12},{12,8},{1,5},{5,1},{9,13},{13,9},{2,6},{6,2},{1... | collective-permute-start | bytes 73736 | tf_op jit(solution)/shard_map/ppermute | solution.py:314
  22.3 6.7 %collective-permute-start.3 = (f32[4,32,128]{2,1,0:T(8,128)S(1)}, f32[4,32,128]{2,1,0:T(8,128)S(1)}, u32[]{:S(2)}, u32[]{:S(2)}) collective-permute-start(f32[4,32,128]{2,1,0:T(8,128)S(1)} %get-tuple-element.14), channel_id=1, source_target_pairs={{0,2},{1,3},{2,0},{3,1},{4,6},{5,7},{6,4},{7,5},{8,10},{9,11},{10,... | collective-permute-start | bytes 196616 | tf_op jit(solution)/shard_map/ppermute | solution.py:346
  25.7 8.3 %collective-permute-start.7 = (f32[8,32,128]{2,1,0:T(8,128)S(1)}, f32[8,32,128]{2,1,0:T(8,128)S(1)}, u32[]{:S(2)}, u32[]{:S(2)}) collective-permute-start(f32[8,32,128]{2,1,0:T(8,128)S(1)} %get-tuple-element.16.refs_0_), channel_id=1, source_target_pairs={{0,1},{1,0},{2,3},{3,2},{4,5},{5,4},{6,7},{7,6},{8,9},{9,8},{10,11... | collective-permute-start | bytes 393224 | tf_op jit(solution)/shard_map/ppermute | solution.py:346
  27.3 6.4 %collective-permute-start.5 = (f32[4,32,128]{2,1,0:T(8,128)S(1)}, f32[4,32,128]{2,1,0:T(8,128)S(1)}, u32[]{:S(2)}, u32[]{:S(2)}) collective-permute-start(f32[4,32,128]{2,1,0:T(8,128)S(1)} %get-tuple-element.15), channel_id=1, source_target_pairs={{0,2},{1,3},{2,0},{3,1},{4,6},{5,7},{6,4},{7,5},{8,10},{9,11},{10,... | collective-permute-start | bytes 196616 | tf_op jit(solution)/shard_map/ppermute | solution.py:346
  29.0 5.8 %collective-permute-start.4 = (f32[4,32,128]{2,1,0:T(8,128)S(1)}, f32[4,32,128]{2,1,0:T(8,128)S(1)}, u32[]{:S(2)}, u32[]{:S(2)}) collective-permute-start(f32[4,32,128]{2,1,0:T(8,128)S(1)} %collective-permute-done.3.refs_1_), channel_id=1, source_target_pairs={{0,1},{1,0},{2,3},{3,2},{4,5},{5,4},{6,7},{7,6},{8,9},{9,8},{10,11... | collective-permute-start | bytes 196616 | tf_op jit(solution)/shard_map/ppermute | solution.py:346
  33.6 4.3 %collective-permute-start.6 = (f32[4,32,128]{2,1,0:T(8,128)S(1)}, f32[4,32,128]{2,1,0:T(8,128)S(1)}, u32[]{:S(2)}, u32[]{:S(2)}) collective-permute-start(f32[4,32,128]{2,1,0:T(8,128)S(1)} %collective-permute-done.5.refs_2_), channel_id=1, source_target_pairs={{0,1},{1,0},{2,3},{3,2},{4,5},{5,4},{6,7},{7,6},{8,9},{9,8},{10,11... | collective-permute-start | bytes 196616 | tf_op jit(solution)/shard_map/ppermute | solution.py:346

commit v10 on v9

--- a/solution.py
+++ b/solution.py
@@ -105,36 +105,52 @@
     return a + c + GAIN * b
 
 
-def main_kernel(depth, rows, blocks, size_x):
+def shift_kernel(rows, size_x):
+    def kernel(mine, layer, moved):
+        depth, tall = mine.shape[0], mine.shape[1] // SUBS
+        _, block = window(lax.axis_index("off"), rows, size_x)
+        ends = edges(tall)
+        for z in range(depth):
+            for r in range(tall):
+                v = mine[z, block(r), :]
+                if r in ends:
+                    v = jnp.where(ends[r][0], jnp.where(ends[r][1], 0.0, layer[z]), v)
+                for c in range(7):
+                    shift = (3 - c) % LANES
+                    moved[z, c, pl.ds(SUBS * r, SUBS), :] = pltpu.roll(v, shift, 1) if shift else v
+
+    return kernel
+
+
+def main_kernel(depth, rows, blocks):
     wide = blocks + 6
     tall = rows // SUBS + 2
 
-    def kernel(mine, scale, layer, near, far, out, low, high, flat, vals, cent, energy, *sums):
+    def kernel(moved, scale, near, far, low, high, flat, vals, cent, energy, *sums):
         lane = lanes()
-        _, block = window(lax.axis_index("off"), rows, size_x)
         gy, gys = lax.axis_index("gy"), lax.axis_size("gy")
         outer = lane % 16 >= 13
         closed = (outer & (gy == 0)) | ((lane % 16 < 3) & (gy == gys - 1))
         from_near = outer == (gy % 2 == 1)
-        ends = edges(tall)
 
         def side(j):
             at = pl.ds(SUBS * j, SUBS)
-            return jnp.where(closed, 0.0, jnp.where(from_near, near[at, :], far[at, :]))
+            line = jnp.where(closed, 0.0, jnp.where(from_near, near[at, :], far[at, :]))
+            return [
+                jnp.where(outer, pltpu.roll(line, LANES - c, 1), pltpu.roll(line, c, 1))
+                for c in range(1, 4)
+            ]
 
         lines = [side(j) for j in range(tall)]
 
         def fill(z):
             for r in range(tall):
                 at = pl.ds(SUBS * r, SUBS)
-                v = mine[z, block(r), :]
-                if r in ends:
-                    v = jnp.where(ends[r][0], jnp.where(ends[r][1], 0.0, layer[z]), v)
-                h = pltpu.roll(lines[r], LANES - 16 * z, 1)
-                flat[z, 3, at, :] = v
+                flat[z, 3, at, :] = moved[z, 3, at, :]
                 for c in range(1, 4):
-                    flat[z, 3 + c, at, :] = pltpu.roll(jnp.where(lane < c, h, v), LANES - c, 1)
-                    flat[z, 3 - c, at, :] = pltpu.roll(jnp.where(lane >= LANES - c, h, v), c, 1)
+                    h = pltpu.roll(lines[r][c - 1], LANES - 16 * z, 1) if z else lines[r][c - 1]
+                    flat[z, 3 + c, at, :] = jnp.where(lane >= LANES - c, h, moved[z, 3 + c, at, :])
+                    flat[z, 3 - c, at, :] = jnp.where(lane < c, h, moved[z, 3 - c, at, :])
             for i in range(wide):
                 for c in range(7):
                     v = flat[z, c, pl.ds(SUBS - 3 + i, SUBS, stride=blocks), :]
@@ -145,7 +161,7 @@
         for z in range(depth):
             fill(z)
 
-        def energies(c, _):
+        def energies(c):
             count = blocks + 4
             filtered = []
 
@@ -166,11 +182,11 @@
                 store(z - 1)
             store(depth - 1)
             store(depth)
-            return 0
-
-        lax.fori_loop(0, 5, energies, 0)
-
-        weigh(depth, blocks, vals, cent, energy, scale, (out, low, high), *sums)
+
+        for c in range(5):
+            energies(c)
+
+        weigh(depth, blocks, vals, cent, energy, scale, (low, high), *sums)
 
     return kernel
 
@@ -243,9 +259,8 @@
         for i in range(blocks):
             t = top[z, i]
             value = (weighted[z, i] + t * vals[3, z + begin, i + 3]) / (total[z, i] + t)
-            part = outs[1] if z < depth // 2 else outs[2]
-            for ref, at in ((outs[0], z), (part, z % (depth // 2))):
-                ref[at, pl.ds(i, SUBS, stride=blocks), :] = value
+            part = outs[z // (depth // 2)]
+            part[z % (depth // 2), pl.ds(i, SUBS, stride=blocks), :] = value
 
 
 def place_kernel(sources, rows):
@@ -313,12 +328,20 @@
     first, second = partners(gys)
     near = lax.ppermute(strips, "gy", list(enumerate(first)))
     far = lax.ppermute(strips, "gy", list(enumerate(second)))
+    moved = pl.pallas_call(
+        shift_kernel(rows, size_x),
+        out_shape=shape(depth, 7, tall, LANES),
+        in_specs=[VMEM] * 2,
+        out_specs=VMEM,
+        cost_estimate=pl.CostEstimate(flops=4_000_000, bytes_accessed=4_000_000, transcendentals=0),
+        compiler_params=small,
+    )(mine, layer)
     half = depth // 2
-    part, *halves = pl.pallas_call(
-        main_kernel(depth, rows, blocks, size_x),
-        out_shape=[shape(depth, rows, size_y)] + [shape(half, rows, size_y)] * 2,
-        in_specs=[VMEM] * 5,
-        out_specs=[VMEM] * 3,
+    halves = pl.pallas_call(
+        main_kernel(depth, rows, blocks),
+        out_shape=[shape(half, rows, size_y)] * 2,
+        in_specs=[VMEM] * 4,
+        out_specs=[VMEM] * 2,
         scratch_shapes=[
             pltpu.VMEM((depth, 7, tall, LANES), f32),
             pltpu.VMEM((7, depth, blocks + 6) + tile, f32),
@@ -327,7 +350,7 @@
         ]
         + [pltpu.VMEM((depth, blocks) + tile, f32)] * 3,
         compiler_params=pltpu.CompilerParams(vmem_limit_bytes=16 * 2**20),
-    )(mine, scale, layer, near, far)
+    )(moved, scale, near, far)
 
     def place(blocks, whole):
         count = len(blocks)
@@ -347,7 +370,7 @@
 
     assert offs & (offs - 1) == 0
     bit = offs // 2
-    blocks = [((0, 0), part)]
+    blocks = [((0, half * n), halves[n]) for n in range(2)]
     blocks += [((bit, half * n), swapped(halves[n], bit)) for n in range(2)]
     while bit > 1:
         bit //= 2

time: 38.7 us -> 35.8 us (0.925)
  waiting for transfers between devices: 10.4 us -> 7.52 us
  Pallas kernels: 14.7 us -> 13.1 us
  local copies, waits for them, and re-layouts: 1.04 us -> 2.08 us
  starting transfers between devices: 12.4 us -> 12.8 us
    ppermute x5 -> x6, waiting for transfers between devices: 7.6 us -> 5.73 us  [swapped(): return lax.ppermute(block, 'off', [(i, i ^ bit) for i in range(offs)])]
    ppermute x1, starting transfers between devices: 0.35 us -> 2.11 us  [shards(): far = lax.ppermute(strips, 'gy', list(enumerate(second)))]
    ppermute x1, starting transfers between devices: 1.83 us -> 0.07 us  [shards(): near = lax.ppermute(strips, 'gy', list(enumerate(first)))]
    pallas_call x1 -> x2, Pallas kernels: 12.9 us -> 11.3 us  [the longest x1 11 us: shards(): pl.pallas_call(main_kernel(depth, rows, blocks), out_shape=[shape(half, r...]
    ppermute x1, waiting for transfers between devices: 1.67 us -> 0.64 us  [shards(): layer = lax.ppermute(layer, ('gx', 'off'), moves)]
    unnamed x4, local copies, waits for them, and re-layouts: 1.04 us -> 2.08 us
    ppermute x5 -> x6, starting transfers between devices: 7.19 us -> 7.6 us  [swapped(): return lax.ppermute(block, 'off', [(i, i ^ bit) for i in range(offs)])]
  transfers between devices with their start and end apart: 8 -> 9, of which waited for: 5 -> 6; matrix products, arithmetic and copies ran while one was open for 0% -> 0% of each run, Pallas kernels for 3% -> 4%
where the time goes in v10:
time: 35.8 us; the launch traced here: 35.6 us
  Pallas kernels  13.1 us (37%)
  starting transfers between devices  12.8 us (36%)
  waiting for transfers between devices  7.52 us (21%)
  local copies, waits for them, and re-layouts  2.08 us (6%)
    pallas_call x1, Pallas kernels, shards(): pl.pallas_call(main_kernel(depth, rows, blocks), out_shape=[shape(half, r...  11 us
    ppermute x6, starting transfers between devices, swapped(): return lax.ppermute(block, 'off', [(i, i ^ bit) for i in range(offs)])  7.6 us
    ppermute x6, waiting for transfers between devices, swapped(): return lax.ppermute(block, 'off', [(i, i ^ bit) for i in range(offs)])  5.73 us
    ppermute x1, starting transfers between devices, shards(): layer = lax.ppermute(layer, ('gx', 'off'), moves)  3.03 us
    ppermute x1, starting transfers between devices, shards(): far = lax.ppermute(strips, 'gy', list(enumerate(second)))  2.11 us
    unnamed x4, local copies, waits for them, and re-layouts  2.08 us
    pallas_call x2, Pallas kernels, place(): pl.pallas_call(place_kernel([source for source, _ in blocks], rows), out_...  1.45 us
    ppermute x1, waiting for transfers between devices, shards(): far = lax.ppermute(strips, 'gy', list(enumerate(second)))  1.15 us
  transfers between devices with their start and end apart: 9, of which 6 were waited for; matrix products, arithmetic and copies ran while one was open for 0% of the time, Pallas kernels for 4%

profile of v10, /device:TPU:0, one launch (start us, length us, event | category | flops | bytes accessed | tf_op | source)
XLA Modules:
  0.0 35.6 jit_solution(5167071192718925858)
XLA Ops:
  0.0 0.0 copy-start
  0.0 1.0 %copy-done = f32[8,128,128]{2,1,0:T(8,128)S(1)} copy-done((f32[8,128,128]{2,1,0:T(8,128)S(1)}, f32[8,128,128]{2,1,0:T(8,128)}, u32[]{:S(2)}) %copy-start) | copy-done | bytes 524312
  1.1 3.0 %collective-permute-start = (f32[8,8,128]{2,1,0:T(8,128)S(1)}, f32[8,8,128]{2,1,0:T(8,128)S(1)}, u32[]{:S(2)}, u32[]{:S(2)}) collective-permute-start(f32[8,8,128]{2,1,0:T(8,128)S(1)} %shard_map.29), channel_id=1, source_target_pairs={{0,16},{1,17},{2,18},{3,19},{16,0},{17,1},{18,2},{19,3},{4,20},{5,... | collective-permute-start | bytes 98312 | tf_op jit(solution)/shard_map/ppermute | solution.py:311
  4.1 0.0 copy-start.1
  4.1 1.0 %copy-done.1 = f32[8,128,128]{2,1,0:T(8,128)S(1)} copy-done((f32[8,128,128]{2,1,0:T(8,128)S(1)}, f32[8,128,128]{2,1,0:T(8,128)}, u32[]{:S(2)}) %copy-start.1) | copy-done | bytes 524312
  5.1 0.2 shard_map.28
  5.4 0.6 %collective-permute-done.layer = f32[8,8,128]{2,1,0:T(8,128)S(1)} collective-permute-done((f32[8,8,128]{2,1,0:T(8,128)S(1)}, f32[8,8,128]{2,1,0:T(8,128)S(1)}, u32[]{:S(2)}, u32[]{:S(2)}) %collective-permute-start) | collective-permute-done | bytes 32800 | tf_op jit(solution)/shard_map/ppermute | solution.py:311
  6.0 0.1 shard_map.31
  6.1 0.1 collective-permute-start.1
  6.2 2.1 %collective-permute-start.2 = (f32[48,128]{1,0:T(8,128)S(1)}, f32[48,128]{1,0:T(8,128)S(1)}, u32[]{:S(2)}, u32[]{:S(2)}) collective-permute-start(f32[48,128]{1,0:T(8,128)S(1)} %shard_map.31), channel_id=1, source_target_pairs={{0,12},{4,8},{8,4},{12,0},{1,13},{5,9},{9,5},{13,1},{2,14},{6,10},... | collective-permute-start | bytes 73736 | tf_op jit(solution)/shard_map/ppermute | solution.py:330
  8.3 0.4 %shard_map.30.moved = f32[8,7,48,128]{3,2,1,0:T(8,128)S(1)} custom-call(f32[8,48,128]{2,1,0:T(8,128)S(1)} %get-tuple-element.10.mine, f32[8,8,128]{2,1,0:T(8,128)S(1)} %collective-permute-done.layer), custom_call_target="tpu_custom_call" | custom-call | flops 4000000 | bytes 4000000 | tf_op jit(solution)/shard_map/pallas_call | solution.py:331
  8.6 0.0 collective-permute-done.1.near
  8.6 1.1 %collective-permute-done.2.far = f32[48,128]{1,0:T(8,128)S(1)} collective-permute-done((f32[48,128]{1,0:T(8,128)S(1)}, f32[48,128]{1,0:T(8,128)S(1)}, u32[]{:S(2)}, u32[]{:S(2)}) %collective-permute-start.2) | collective-permute-done | bytes 24608 | tf_op jit(solution)/shard_map/ppermute | solution.py:330
  9.8 11.0 %shard_map.32 = (f32[4,32,128]{2,1,0:T(8,128)S(1)}, f32[4,32,128]{2,1,0:T(8,128)S(1)}) custom-call(f32[8,7,48,128]{3,2,1,0:T(8,128)S(1)} %shard_map.30.moved, f32[8,4,8,128]{3,2,1,0:T(8,128)S(1)} %get-tuple-element.11.scale, f32[48,128]{1,0:T(8,128)S(1)} %collective-permute-done.1.near, f32[48,128]{1,0:T(8,128)S(1)} %collective-permute-done.2.far), custom_call_target="tpu_custom_call" | custom-call | tf_op jit(solution)/shard_map/pallas_call | solution.py:340
  20.8 2.8 %collective-permute-start.3 = (f32[4,32,128]{2,1,0:T(8,128)S(1)}, f32[4,32,128]{2,1,0:T(8,128)S(1)}, u32[]{:S(2)}, u32[]{:S(2)}) collective-permute-start(f32[4,32,128]{2,1,0:T(8,128)S(1)} %get-tuple-element.13.refs_0_), channel_id=1, source_target_pairs={{0,2},{1,3},{2,0},{3,1},{4,6},{5,7},{6,4},{7,5},{8,10},{9,11},{10,... | collective-permute-start | bytes 196616 | tf_op jit(solution)/shard_map/ppermute | solution.py:369
  23.6 0.2 collective-permute-start.5
  23.8 1.7 %collective-permute-start.7 = (f32[4,32,128]{2,1,0:T(8,128)S(1)}, f32[4,32,128]{2,1,0:T(8,128)S(1)}, u32[]{:S(2)}, u32[]{:S(2)}) collective-permute-start(f32[4,32,128]{2,1,0:T(8,128)S(1)} %get-tuple-element.13.refs_0_), channel_id=1, source_target_pairs={{0,1},{1,0},{2,3},{3,2},{4,5},{5,4},{6,7},{7,6},{8,9},{9,8},{10,11... | collective-permute-start | bytes 196616 | tf_op jit(solution)/shard_map/ppermute | solution.py:369
  25.5 0.3 collective-permute-start.8
  25.8 2.2 %collective-permute-done.3.refs_2_ = f32[4,32,128]{2,1,0:T(8,128)S(1)} collective-permute-done((f32[4,32,128]{2,1,0:T(8,128)S(1)}, f32[4,32,128]{2,1,0:T(8,128)S(1)}, u32[]{:S(2)}, u32[]{:S(2)}) %collective-permute-start.3) | collective-permute-done | bytes 65568 | tf_op jit(solution)/shard_map/ppermute | solution.py:369
  28.0 1.9 %collective-permute-start.4 = (f32[4,32,128]{2,1,0:T(8,128)S(1)}, f32[4,32,128]{2,1,0:T(8,128)S(1)}, u32[]{:S(2)}, u32[]{:S(2)}) collective-permute-start(f32[4,32,128]{2,1,0:T(8,128)S(1)} %collective-permute-done.3.refs_2_), channel_id=1, source_target_pairs={{0,1},{1,0},{2,3},{3,2},{4,5},{5,4},{6,7},{7,6},{8,9},{9,8},{10,11... | collective-permute-start | bytes 196616 | tf_op jit(solution)/shard_map/ppermute | solution.py:369
  29.9 0.7 %collective-permute-done.5.refs_3_ = f32[4,32,128]{2,1,0:T(8,128)S(1)} collective-permute-done((f32[4,32,128]{2,1,0:T(8,128)S(1)}, f32[4,32,128]{2,1,0:T(8,128)S(1)}, u32[]{:S(2)}, u32[]{:S(2)}) %collective-permute-start.5) | collective-permute-done | bytes 65568 | tf_op jit(solution)/shard_map/ppermute | solution.py:369
  30.6 0.7 %collective-permute-start.6 = (f32[4,32,128]{2,1,0:T(8,128)S(1)}, f32[4,32,128]{2,1,0:T(8,128)S(1)}, u32[]{:S(2)}, u32[]{:S(2)}) collective-permute-start(f32[4,32,128]{2,1,0:T(8,128)S(1)} %collective-permute-done.5.refs_3_), channel_id=1, source_target_pairs={{0,1},{1,0},{2,3},{3,2},{4,5},{5,4},{6,7},{7,6},{8,9},{9,8},{10,11... | collective-permute-start | bytes 196616 | tf_op jit(solution)/shard_map/ppermute | solution.py:369
  31.3 0.0 collective-permute-done.7.refs_4_
  31.3 0.0 collective-permute-done.8.refs_5_
  31.3 0.8 %shard_map.33.refs_2_ = f32[8,128,128]{2,1,0:T(8,128)} custom-call(f32[4,32,128]{2,1,0:T(8,128)S(1)} %get-tuple-element.13.refs_0_, f32[4,32,128]{2,1,0:T(8,128)S(1)} %get-tuple-element.14.refs_1_, f32[4,32,128]{2,1,0:T(8,128)S(1)} %collective-permute-done.3.refs_2_, f32[4,32,128]{2,1,0:T(8,128)S(1)} %collective-permute-done.5.refs_3_, ...), custom_call_target="tpu_custom_call" | custom-call | tf_op jit(solution)/shard_map/pallas_call | solution.py:358
  32.1 0.4 collective-permute-done.4.refs_0_
  32.5 2.4 %collective-permute-done.6.refs_1_ = f32[4,32,128]{2,1,0:T(8,128)S(1)} collective-permute-done((f32[4,32,128]{2,1,0:T(8,128)S(1)}, f32[4,32,128]{2,1,0:T(8,128)S(1)}, u32[]{:S(2)}, u32[]{:S(2)}) %collective-permute-start.6) | collective-permute-done | bytes 65568 | tf_op jit(solution)/shard_map/ppermute | solution.py:369
  34.9 0.7 %shard_map.34 = f32[8,128,128]{2,1,0:T(8,128)} custom-call(f32[4,32,128]{2,1,0:T(8,128)S(1)} %collective-permute-done.4.refs_0_, f32[4,32,128]{2,1,0:T(8,128)S(1)} %collective-permute-done.6.refs_1_, f32[8,128,128]{2,1,0:T(8,128)} %shard_map.33.refs_2_), custom_call_target="tpu_custom_call", output_to_operand_aliasing={{}: (2, {})} | custom-call | tf_op jit(solution)/shard_map/pallas_call | solution.py:358
  (1 shorter events, 0.0 us)
Async XLA Ops:
  0.0 1.0 %copy-start = (f32[8,128,128]{2,1,0:T(8,128)S(1)}, f32[8,128,128]{2,1,0:T(8,128)}, u32[]{:S(2)}) copy-start(f32[8,128,128]{2,1,0:T(8,128)} %volume.3) | copy-start | bytes 1572868
  1.1 4.9 %collective-permute-start = (f32[8,8,128]{2,1,0:T(8,128)S(1)}, f32[8,8,128]{2,1,0:T(8,128)S(1)}, u32[]{:S(2)}, u32[]{:S(2)}) collective-permute-start(f32[8,8,128]{2,1,0:T(8,128)S(1)} %shard_map.29), channel_id=1, source_target_pairs={{0,16},{1,17},{2,18},{3,19},{16,0},{17,1},{18,2},{19,3},{4,20},{5,... | collective-permute-start | bytes 98312 | tf_op jit(solution)/shard_map/ppermute | solution.py:311
  4.1 1.0 %copy-start.1 = (f32[8,128,128]{2,1,0:T(8,128)S(1)}, f32[8,128,128]{2,1,0:T(8,128)}, u32[]{:S(2)}) copy-start(f32[8,128,128]{2,1,0:T(8,128)} %strength.1) | copy-start | bytes 1572868
  6.1 2.6 %collective-permute-start.1 = (f32[48,128]{1,0:T(8,128)S(1)}, f32[48,128]{1,0:T(8,128)S(1)}, u32[]{:S(2)}, u32[]{:S(2)}) collective-permute-start(f32[48,128]{1,0:T(8,128)S(1)} %shard_map.31), channel_id=1, source_target_pairs={{0,4},{4,0},{8,12},{12,8},{1,5},{5,1},{9,13},{13,9},{2,6},{6,2},{1... | collective-permute-start | bytes 73736 | tf_op jit(solution)/shard_map/ppermute | solution.py:329
  6.2 3.6 %collective-permute-start.2 = (f32[48,128]{1,0:T(8,128)S(1)}, f32[48,128]{1,0:T(8,128)S(1)}, u32[]{:S(2)}, u32[]{:S(2)}) collective-permute-start(f32[48,128]{1,0:T(8,128)S(1)} %shard_map.31), channel_id=1, source_target_pairs={{0,12},{4,8},{8,4},{12,0},{1,13},{5,9},{9,5},{13,1},{2,14},{6,10},... | collective-permute-start | bytes 73736 | tf_op jit(solution)/shard_map/ppermute | solution.py:330
  20.8 7.2 %collective-permute-start.3 = (f32[4,32,128]{2,1,0:T(8,128)S(1)}, f32[4,32,128]{2,1,0:T(8,128)S(1)}, u32[]{:S(2)}, u32[]{:S(2)}) collective-permute-start(f32[4,32,128]{2,1,0:T(8,128)S(1)} %get-tuple-element.13.refs_0_), channel_id=1, source_target_pairs={{0,2},{1,3},{2,0},{3,1},{4,6},{5,7},{6,4},{7,5},{8,10},{9,11},{10,... | collective-permute-start | bytes 196616 | tf_op jit(solution)/shard_map/ppermute | solution.py:369
  23.6 7.0 %collective-permute-start.5 = (f32[4,32,128]{2,1,0:T(8,128)S(1)}, f32[4,32,128]{2,1,0:T(8,128)S(1)}, u32[]{:S(2)}, u32[]{:S(2)}) collective-permute-start(f32[4,32,128]{2,1,0:T(8,128)S(1)} %get-tuple-element.14.refs_1_), channel_id=1, source_target_pairs={{0,2},{1,3},{2,0},{3,1},{4,6},{5,7},{6,4},{7,5},{8,10},{9,11},{10,... | collective-permute-start | bytes 196616 | tf_op jit(solution)/shard_map/ppermute | solution.py:369
  23.8 7.5 %collective-permute-start.7 = (f32[4,32,128]{2,1,0:T(8,128)S(1)}, f32[4,32,128]{2,1,0:T(8,128)S(1)}, u32[]{:S(2)}, u32[]{:S(2)}) collective-permute-start(f32[4,32,128]{2,1,0:T(8,128)S(1)} %get-tuple-element.13.refs_0_), channel_id=1, source_target_pairs={{0,1},{1,0},{2,3},{3,2},{4,5},{5,4},{6,7},{7,6},{8,9},{9,8},{10,11... | collective-permute-start | bytes 196616 | tf_op jit(solution)/shard_map/ppermute | solution.py:369
  25.5 5.8 %collective-permute-start.8 = (f32[4,32,128]{2,1,0:T(8,128)S(1)}, f32[4,32,128]{2,1,0:T(8,128)S(1)}, u32[]{:S(2)}, u32[]{:S(2)}) collective-permute-start(f32[4,32,128]{2,1,0:T(8,128)S(1)} %get-tuple-element.14.refs_1_), channel_id=1, source_target_pairs={{0,1},{1,0},{2,3},{3,2},{4,5},{5,4},{6,7},{7,6},{8,9},{9,8},{10,11... | collective-permute-start | bytes 196616 | tf_op jit(solution)/shard_map/ppermute | solution.py:369
  28.0 4.5 %collective-permute-start.4 = (f32[4,32,128]{2,1,0:T(8,128)S(1)}, f32[4,32,128]{2,1,0:T(8,128)S(1)}, u32[]{:S(2)}, u32[]{:S(2)}) collective-permute-start(f32[4,32,128]{2,1,0:T(8,128)S(1)} %collective-permute-done.3.refs_2_), channel_id=1, source_target_pairs={{0,1},{1,0},{2,3},{3,2},{4,5},{5,4},{6,7},{7,6},{8,9},{9,8},{10,11... | collective-permute-start | bytes 196616 | tf_op jit(solution)/shard_map/ppermute | solution.py:369
  30.6 4.3 %collective-permute-start.6 = (f32[4,32,128]{2,1,0:T(8,128)S(1)}, f32[4,32,128]{2,1,0:T(8,128)S(1)}, u32[]{:S(2)}, u32[]{:S(2)}) collective-permute-start(f32[4,32,128]{2,1,0:T(8,128)S(1)} %collective-permute-done.5.refs_3_), channel_id=1, source_target_pairs={{0,1},{1,0},{2,3},{3,2},{4,5},{5,4},{6,7},{7,6},{8,9},{9,8},{10,11... | collective-permute-start | bytes 196616 | tf_op jit(solution)/shard_map/ppermute | solution.py:369

commit v11 on v10

--- a/solution.py
+++ b/solution.py
@@ -126,7 +126,7 @@
     wide = blocks + 6
     tall = rows // SUBS + 2
 
-    def kernel(moved, scale, near, far, low, high, flat, vals, cent, energy, *sums):
+    def kernel(moved, scale, near, far, out, low, high, flat, vals, cent, energy, *sums):
         lane = lanes()
         gy, gys = lax.axis_index("gy"), lax.axis_size("gy")
         outer = lane % 16 >= 13
@@ -186,7 +186,7 @@
         for c in range(5):
             energies(c)
 
-        weigh(depth, blocks, vals, cent, energy, scale, (low, high), *sums)
+        weigh(depth, blocks, vals, cent, energy, scale, (out, low, high), *sums)
 
     return kernel
 
@@ -259,8 +259,9 @@
         for i in range(blocks):
             t = top[z, i]
             value = (weighted[z, i] + t * vals[3, z + begin, i + 3]) / (total[z, i] + t)
-            part = outs[z // (depth // 2)]
-            part[z % (depth // 2), pl.ds(i, SUBS, stride=blocks), :] = value
+            part = outs[1 + z // (depth // 2)]
+            for ref, at in ((outs[0], z), (part, z % (depth // 2))):
+                ref[at, pl.ds(i, SUBS, stride=blocks), :] = value
 
 
 def place_kernel(sources, rows):
@@ -337,11 +338,11 @@
         compiler_params=small,
     )(mine, layer)
     half = depth // 2
-    halves = pl.pallas_call(
+    part, *halves = pl.pallas_call(
         main_kernel(depth, rows, blocks),
-        out_shape=[shape(half, rows, size_y)] * 2,
+        out_shape=[shape(depth, rows, size_y)] + [shape(half, rows, size_y)] * 2,
         in_specs=[VMEM] * 4,
-        out_specs=[VMEM] * 2,
+        out_specs=[VMEM] * 3,
         scratch_shapes=[
             pltpu.VMEM((depth, 7, tall, LANES), f32),
             pltpu.VMEM((7, depth, blocks + 6) + tile, f32),
@@ -352,16 +353,17 @@
         compiler_params=pltpu.CompilerParams(vmem_limit_bytes=16 * 2**20),
     )(moved, scale, near, far)
 
-    def place(blocks, whole):
+    def place(blocks, whole, keep=0):
         count = len(blocks)
         held = [] if whole is None else [whole]
+        outs = [shape(*block.shape) for _, block in blocks[:keep]]
         return pl.pallas_call(
             place_kernel([source for source, _ in blocks], rows),
-            out_shape=shape(depth, size_x, size_y),
+            out_shape=outs + [shape(depth, size_x, size_y)],
             in_specs=[VMEM] * count + [HBM] * len(held),
-            out_specs=HBM,
+            out_specs=[VMEM] * keep + [HBM],
             scratch_shapes=[pltpu.SemaphoreType.DMA((count,))],
-            input_output_aliases={count: 0} if held else {},
+            input_output_aliases={n: n for n in range(keep)} | ({count: keep} if held else {}),
             compiler_params=small,
         )(*(block for _, block in blocks), *held)
 
@@ -369,13 +371,19 @@
         return lax.ppermute(block, "off", [(i, i ^ bit) for i in range(offs)])
 
     assert offs & (offs - 1) == 0
-    bit = offs // 2
-    blocks = [((0, half * n), halves[n]) for n in range(2)]
-    blocks += [((bit, half * n), swapped(halves[n], bit)) for n in range(2)]
+    bit, ready = 1, [((0, 0), part)]
+    while 2 * bit < offs:
+        ready += [((step ^ bit, z), swapped(block, bit)) for (step, z), block in ready]
+        bit *= 2
+    *halves, whole = place([((0, half * n), halves[n]) for n in range(2)], None, keep=2)
+    late = [((bit, half * n), swapped(halves[n], bit)) for n in range(2)]
+    ready, last = ready[1:] + late, []
     while bit > 1:
         bit //= 2
-        blocks += [((step ^ bit, z), swapped(block, bit)) for (step, z), block in blocks]
-    return place(blocks[-2:], place(blocks[:-2], None))
+        last += [((step ^ bit, z), swapped(block, bit)) for (step, z), block in late + last]
+    (whole,) = place(ready, whole)
+    (whole,) = place(last, whole)
+    return whole
 
 
 def solution(mesh):

time: 35.8 us -> 38 us (1.061)
  waiting for transfers between devices: 7.52 us -> 9.41 us
  Pallas kernels: 13.1 us -> 13.7 us
    ppermute x6 -> x5, waiting for transfers between devices: 5.73 us -> 7.99 us  [swapped(): return lax.ppermute(block, 'off', [(i, i ^ bit) for i in range(offs)])]
    ppermute x1, starting transfers between devices: 2.11 us -> 0.35 us  [shards(): far = lax.ppermute(strips, 'gy', list(enumerate(second)))]
    ppermute x1, starting transfers between devices: 0.07 us -> 1.83 us  [shards(): near = lax.ppermute(strips, 'gy', list(enumerate(first)))]
    pallas_call x2 -> x3, Pallas kernels: 1.45 us -> 2.05 us  [place(): pl.pallas_call(place_kernel([source for source, _ in blocks], rows), out_...]
    ppermute x6 -> x5, starting transfers between devices: 7.6 us -> 7.31 us  [swapped(): return lax.ppermute(block, 'off', [(i, i ^ bit) for i in range(offs)])]
  transfers between devices with their start and end apart: 9 -> 8, of which waited for: 6 -> 6; matrix products, arithmetic and copies ran while one was open for 0% -> 0% of each run, Pallas kernels for 4% -> 5%
where the time goes in v11:
time: 38 us; the launch traced here: 37.8 us
  Pallas kernels  13.7 us (36%)
  starting transfers between devices  12.5 us (33%)
  waiting for transfers between devices  9.41 us (25%)
  local copies, waits for them, and re-layouts  2.08 us (5%)
    pallas_call x1, Pallas kernels, shards(): pl.pallas_call(main_kernel(depth, rows, blocks), out_shape=[shape(depth,...  11 us
    ppermute x5, waiting for transfers between devices, swapped(): return lax.ppermute(block, 'off', [(i, i ^ bit) for i in range(offs)])  7.99 us
    ppermute x5, starting transfers between devices, swapped(): return lax.ppermute(block, 'off', [(i, i ^ bit) for i in range(offs)])  7.31 us
    ppermute x1, starting transfers between devices, shards(): layer = lax.ppermute(layer, ('gx', 'off'), moves)  3.03 us
    unnamed x4, local copies, waits for them, and re-layouts  2.08 us
    pallas_call x3, Pallas kernels, place(): pl.pallas_call(place_kernel([source for source, _ in blocks], rows), out_...  2.05 us
    ppermute x1, starting transfers between devices, shards(): near = lax.ppermute(strips, 'gy', list(enumerate(first)))  1.83 us
    ppermute x1, waiting for transfers between devices, shards(): far = lax.ppermute(strips, 'gy', list(enumerate(second)))  0.78 us
  transfers between devices with their start and end apart: 8, of which 6 were waited for; matrix products, arithmetic and copies ran while one was open for 0% of the time, Pallas kernels for 5%

profile of v11, /device:TPU:0, one launch (start us, length us, event | category | flops | bytes accessed | tf_op | source)
XLA Modules:
  0.0 37.8 jit_solution(2502382213440996734)
XLA Ops:
  0.0 0.0 copy-start
  0.0 1.0 %copy-done = f32[8,128,128]{2,1,0:T(8,128)S(1)} copy-done((f32[8,128,128]{2,1,0:T(8,128)S(1)}, f32[8,128,128]{2,1,0:T(8,128)}, u32[]{:S(2)}) %copy-start) | copy-done | bytes 524312
  1.1 3.0 %collective-permute-start = (f32[8,8,128]{2,1,0:T(8,128)S(1)}, f32[8,8,128]{2,1,0:T(8,128)S(1)}, u32[]{:S(2)}, u32[]{:S(2)}) collective-permute-start(f32[8,8,128]{2,1,0:T(8,128)S(1)} %shard_map.29), channel_id=1, source_target_pairs={{0,16},{1,17},{2,18},{3,19},{16,0},{17,1},{18,2},{19,3},{4,20},{5,... | collective-permute-start | bytes 98312 | tf_op jit(solution)/shard_map/ppermute | solution.py:312
  4.1 0.0 copy-start.1
  4.1 1.0 %copy-done.1 = f32[8,128,128]{2,1,0:T(8,128)S(1)} copy-done((f32[8,128,128]{2,1,0:T(8,128)S(1)}, f32[8,128,128]{2,1,0:T(8,128)}, u32[]{:S(2)}) %copy-start.1) | copy-done | bytes 524312
  5.1 0.2 shard_map.28
  5.4 0.6 %collective-permute-done.layer = f32[8,8,128]{2,1,0:T(8,128)S(1)} collective-permute-done((f32[8,8,128]{2,1,0:T(8,128)S(1)}, f32[8,8,128]{2,1,0:T(8,128)S(1)}, u32[]{:S(2)}, u32[]{:S(2)}) %collective-permute-start) | collective-permute-done | bytes 32800 | tf_op jit(solution)/shard_map/ppermute | solution.py:312
  6.0 0.1 shard_map.31
  6.1 0.3 collective-permute-start.2
  6.4 1.8 %collective-permute-start.1 = (f32[48,128]{1,0:T(8,128)S(1)}, f32[48,128]{1,0:T(8,128)S(1)}, u32[]{:S(2)}, u32[]{:S(2)}) collective-permute-start(f32[48,128]{1,0:T(8,128)S(1)} %shard_map.31), channel_id=1, source_target_pairs={{0,4},{4,0},{8,12},{12,8},{1,5},{5,1},{9,13},{13,9},{2,6},{6,2},{1... | collective-permute-start | bytes 73736 | tf_op jit(solution)/shard_map/ppermute | solution.py:330
  8.2 0.4 shard_map.30.moved
  8.6 0.8 %collective-permute-done.2.far = f32[48,128]{1,0:T(8,128)S(1)} collective-permute-done((f32[48,128]{1,0:T(8,128)S(1)}, f32[48,128]{1,0:T(8,128)S(1)}, u32[]{:S(2)}, u32[]{:S(2)}) %collective-permute-start.2) | collective-permute-done | bytes 24608 | tf_op jit(solution)/shard_map/ppermute | solution.py:331
  9.4 0.0 collective-permute-done.1.near
  9.4 11.0 %shard_map.32 = (f32[8,32,128]{2,1,0:T(8,128)S(1)}, f32[4,32,128]{2,1,0:T(8,128)S(1)}, f32[4,32,128]{2,1,0:T(8,128)S(1)}) custom-call(f32[8,7,48,128]{3,2,1,0:T(8,128)S(1)} %shard_map.30.moved, f32[8,4,8,128]{3,2,1,0:T(8,128)S(1)} %get-tuple-element.15.scale, f32[48,128]{1,0:T(8,128)S(1)} %collective-permute-done.1.near, ...), custom_call_target="tpu_custom_call" | custom-call | tf_op jit(solution)/shard_map/pallas_call | solution.py:341
  20.4 2.4 %collective-permute-start.7 = (f32[8,32,128]{2,1,0:T(8,128)S(1)}, f32[8,32,128]{2,1,0:T(8,128)S(1)}, u32[]{:S(2)}, u32[]{:S(2)}) collective-permute-start(f32[8,32,128]{2,1,0:T(8,128)S(1)} %get-tuple-element.21), channel_id=1, source_target_pairs={{0,1},{1,0},{2,3},{3,2},{4,5},{5,4},{6,7},{7,6},{8,9},{9,8},{10,11... | collective-permute-start | bytes 393224 | tf_op jit(solution)/shard_map/ppermute | solution.py:371
  22.7 0.7 %shard_map.33 = (f32[4,32,128]{2,1,0:T(8,128)S(1)}, f32[4,32,128]{2,1,0:T(8,128)S(1)}, f32[8,128,128]{2,1,0:T(8,128)}) custom-call(f32[4,32,128]{2,1,0:T(8,128)S(1)} %get-tuple-element.17.refs_0_, f32[4,32,128]{2,1,0:T(8,128)S(1)} %get-tuple-element.18.refs_1_), custom_call_target="tpu_custom_call", output_to_operand_aliasing={{0}: (0, {}), {1}: (1, {})} | custom-call | tf_op jit(solution)/shard_map/pallas_call | solution.py:360
  23.4 2.7 %collective-permute-start.3 = (f32[4,32,128]{2,1,0:T(8,128)S(1)}, f32[4,32,128]{2,1,0:T(8,128)S(1)}, u32[]{:S(2)}, u32[]{:S(2)}) collective-permute-start(f32[4,32,128]{2,1,0:T(8,128)S(1)} %get-tuple-element.19), channel_id=1, source_target_pairs={{0,2},{1,3},{2,0},{3,1},{4,6},{5,7},{6,4},{7,5},{8,10},{9,11},{10,... | collective-permute-start | bytes 196616 | tf_op jit(solution)/shard_map/ppermute | solution.py:371
  26.1 0.3 collective-permute-start.5
  26.4 3.1 %collective-permute-done.3.refs_1_ = f32[4,32,128]{2,1,0:T(8,128)S(1)} collective-permute-done((f32[4,32,128]{2,1,0:T(8,128)S(1)}, f32[4,32,128]{2,1,0:T(8,128)S(1)}, u32[]{:S(2)}, u32[]{:S(2)}) %collective-permute-start.3) | collective-permute-done | bytes 65568 | tf_op jit(solution)/shard_map/ppermute | solution.py:371
  29.5 2.0 %collective-permute-start.4 = (f32[4,32,128]{2,1,0:T(8,128)S(1)}, f32[4,32,128]{2,1,0:T(8,128)S(1)}, u32[]{:S(2)}, u32[]{:S(2)}) collective-permute-start(f32[4,32,128]{2,1,0:T(8,128)S(1)} %collective-permute-done.3.refs_1_), channel_id=1, source_target_pairs={{0,1},{1,0},{2,3},{3,2},{4,5},{5,4},{6,7},{7,6},{8,9},{9,8},{10,11... | collective-permute-start | bytes 196616 | tf_op jit(solution)/shard_map/ppermute | solution.py:371
  31.5 1.3 %collective-permute-done.5.refs_2_ = f32[4,32,128]{2,1,0:T(8,128)S(1)} collective-permute-done((f32[4,32,128]{2,1,0:T(8,128)S(1)}, f32[4,32,128]{2,1,0:T(8,128)S(1)}, u32[]{:S(2)}, u32[]{:S(2)}) %collective-permute-start.5) | collective-permute-done | bytes 65568 | tf_op jit(solution)/shard_map/ppermute | solution.py:371
  32.8 0.0 collective-permute-start.6
  32.8 0.0 collective-permute-done.7.refs_0_
  32.8 0.7 %shard_map.34.refs_2_ = f32[8,128,128]{2,1,0:T(8,128)} custom-call(f32[8,32,128]{2,1,0:T(8,128)S(1)} %collective-permute-done.7.refs_0_, f32[4,32,128]{2,1,0:T(8,128)S(1)} %collective-permute-done.3.refs_1_, f32[4,32,128]{2,1,0:T(8,128)S(1)} %collective-permute-done.5.refs_2_, f32[8,128,128]{2,1,0:T(8,128)} %get-tuple-element.22.refs_3_), custom_call_target="tpu_custom_call", output_to_operand_aliasing={{}: (3, {})} | custom-call | tf_op jit(solution)/shard_map/pallas_call | solution.py:360
  33.6 0.2 collective-permute-done.4.refs_0_
  33.8 3.3 %collective-permute-done.6.refs_1_ = f32[4,32,128]{2,1,0:T(8,128)S(1)} collective-permute-done((f32[4,32,128]{2,1,0:T(8,128)S(1)}, f32[4,32,128]{2,1,0:T(8,128)S(1)}, u32[]{:S(2)}, u32[]{:S(2)}) %collective-permute-start.6) | collective-permute-done | bytes 65568 | tf_op jit(solution)/shard_map/ppermute | solution.py:371
  37.1 0.7 %shard_map.35 = f32[8,128,128]{2,1,0:T(8,128)} custom-call(f32[4,32,128]{2,1,0:T(8,128)S(1)} %collective-permute-done.4.refs_0_, f32[4,32,128]{2,1,0:T(8,128)S(1)} %collective-permute-done.6.refs_1_, f32[8,128,128]{2,1,0:T(8,128)} %shard_map.34.refs_2_), custom_call_target="tpu_custom_call", output_to_operand_aliasing={{}: (2, {})} | custom-call | tf_op jit(solution)/shard_map/pallas_call | solution.py:360
  (1 shorter events, 0.0 us)
Async XLA Ops:
  0.0 1.0 %copy-start = (f32[8,128,128]{2,1,0:T(8,128)S(1)}, f32[8,128,128]{2,1,0:T(8,128)}, u32[]{:S(2)}) copy-start(f32[8,128,128]{2,1,0:T(8,128)} %volume.3) | copy-start | bytes 1572868
  1.1 4.9 %collective-permute-start = (f32[8,8,128]{2,1,0:T(8,128)S(1)}, f32[8,8,128]{2,1,0:T(8,128)S(1)}, u32[]{:S(2)}, u32[]{:S(2)}) collective-permute-start(f32[8,8,128]{2,1,0:T(8,128)S(1)} %shard_map.29), channel_id=1, source_target_pairs={{0,16},{1,17},{2,18},{3,19},{16,0},{17,1},{18,2},{19,3},{4,20},{5,... | collective-permute-start | bytes 98312 | tf_op jit(solution)/shard_map/ppermute | solution.py:312
  4.1 1.0 %copy-start.1 = (f32[8,128,128]{2,1,0:T(8,128)S(1)}, f32[8,128,128]{2,1,0:T(8,128)}, u32[]{:S(2)}) copy-start(f32[8,128,128]{2,1,0:T(8,128)} %strength.1) | copy-start | bytes 1572868
  6.1 3.3 %collective-permute-start.2 = (f32[48,128]{1,0:T(8,128)S(1)}, f32[48,128]{1,0:T(8,128)S(1)}, u32[]{:S(2)}, u32[]{:S(2)}) collective-permute-start(f32[48,128]{1,0:T(8,128)S(1)} %shard_map.31), channel_id=1, source_target_pairs={{0,12},{4,8},{8,4},{12,0},{1,13},{5,9},{9,5},{13,1},{2,14},{6,10},... | collective-permute-start | bytes 73736 | tf_op jit(solution)/shard_map/ppermute | solution.py:331
  6.4 3.0 %collective-permute-start.1 = (f32[48,128]{1,0:T(8,128)S(1)}, f32[48,128]{1,0:T(8,128)S(1)}, u32[]{:S(2)}, u32[]{:S(2)}) collective-permute-start(f32[48,128]{1,0:T(8,128)S(1)} %shard_map.31), channel_id=1, source_target_pairs={{0,4},{4,0},{8,12},{12,8},{1,5},{5,1},{9,13},{13,9},{2,6},{6,2},{1... | collective-permute-start | bytes 73736 | tf_op jit(solution)/shard_map/ppermute | solution.py:330
  20.4 12.4 %collective-permute-start.7 = (f32[8,32,128]{2,1,0:T(8,128)S(1)}, f32[8,32,128]{2,1,0:T(8,128)S(1)}, u32[]{:S(2)}, u32[]{:S(2)}) collective-permute-start(f32[8,32,128]{2,1,0:T(8,128)S(1)} %get-tuple-element.21), channel_id=1, source_target_pairs={{0,1},{1,0},{2,3},{3,2},{4,5},{5,4},{6,7},{7,6},{8,9},{9,8},{10,11... | collective-permute-start | bytes 393224 | tf_op jit(solution)/shard_map/ppermute | solution.py:371
  23.4 6.1 %collective-permute-start.3 = (f32[4,32,128]{2,1,0:T(8,128)S(1)}, f32[4,32,128]{2,1,0:T(8,128)S(1)}, u32[]{:S(2)}, u32[]{:S(2)}) collective-permute-start(f32[4,32,128]{2,1,0:T(8,128)S(1)} %get-tuple-element.19), channel_id=1, source_target_pairs={{0,2},{1,3},{2,0},{3,1},{4,6},{5,7},{6,4},{7,5},{8,10},{9,11},{10,... | collective-permute-start | bytes 196616 | tf_op jit(solution)/shard_map/ppermute | solution.py:371
  26.1 6.8 %collective-permute-start.5 = (f32[4,32,128]{2,1,0:T(8,128)S(1)}, f32[4,32,128]{2,1,0:T(8,128)S(1)}, u32[]{:S(2)}, u32[]{:S(2)}) collective-permute-start(f32[4,32,128]{2,1,0:T(8,128)S(1)} %get-tuple-element.20), channel_id=1, source_target_pairs={{0,2},{1,3},{2,0},{3,1},{4,6},{5,7},{6,4},{7,5},{8,10},{9,11},{10,... | collective-permute-start | bytes 196616 | tf_op jit(solution)/shard_map/ppermute | solution.py:371
  29.5 4.3 %collective-permute-start.4 = (f32[4,32,128]{2,1,0:T(8,128)S(1)}, f32[4,32,128]{2,1,0:T(8,128)S(1)}, u32[]{:S(2)}, u32[]{:S(2)}) collective-permute-start(f32[4,32,128]{2,1,0:T(8,128)S(1)} %collective-permute-done.3.refs_1_), channel_id=1, source_target_pairs={{0,1},{1,0},{2,3},{3,2},{4,5},{5,4},{6,7},{7,6},{8,9},{9,8},{10,11... | collective-permute-start | bytes 196616 | tf_op jit(solution)/shard_map/ppermute | solution.py:371
  32.8 4.3 %collective-permute-start.6 = (f32[4,32,128]{2,1,0:T(8,128)S(1)}, f32[4,32,128]{2,1,0:T(8,128)S(1)}, u32[]{:S(2)}, u32[]{:S(2)}) collective-permute-start(f32[4,32,128]{2,1,0:T(8,128)S(1)} %collective-permute-done.5.refs_2_), channel_id=1, source_target_pairs={{0,1},{1,0},{2,3},{3,2},{4,5},{5,4},{6,7},{7,6},{8,9},{9,8},{10,11... | collective-permute-start | bytes 196616 | tf_op jit(solution)/shard_map/ppermute | solution.py:371

commit v12 on v10

--- a/solution.py
+++ b/solution.py
@@ -126,7 +126,7 @@
     wide = blocks + 6
     tall = rows // SUBS + 2
 
-    def kernel(moved, scale, near, far, low, high, flat, vals, cent, energy, *sums):
+    def kernel(moved, scale, near, far, low, vals, cent, energy, flat, *sums):
         lane = lanes()
         gy, gys = lax.axis_index("gy"), lax.axis_size("gy")
         outer = lane % 16 >= 13
@@ -186,13 +186,21 @@
         for c in range(5):
             energies(c)
 
-        weigh(depth, blocks, vals, cent, energy, scale, (low, high), *sums)
+        weigh(depth, blocks, (0, depth // 2), vals, cent, energy, scale, low, *sums)
 
     return kernel
 
 
-def weigh(depth, blocks, vals, cent, energy, scale, outs, top, total, weighted):
-    begin, end = 0, depth
+def second_kernel(depth, blocks):
+    def kernel(vals, cent, energy, scale, low, kept, high, *sums):
+        kept[...] = low[...]
+        weigh(depth, blocks, (depth // 2, depth), vals, cent, energy, scale, high, *sums)
+
+    return kernel
+
+
+def weigh(depth, blocks, slices, vals, cent, energy, scale, out, top, total, weighted):
+    begin, end = slices
     for z in range(end - begin):
         for i in range(blocks):
             for ref in (top, total, weighted):
@@ -259,8 +267,7 @@
         for i in range(blocks):
             t = top[z, i]
             value = (weighted[z, i] + t * vals[3, z + begin, i + 3]) / (total[z, i] + t)
-            part = outs[z // (depth // 2)]
-            part[z % (depth // 2), pl.ds(i, SUBS, stride=blocks), :] = value
+            out[z, pl.ds(i, SUBS, stride=blocks), :] = value
 
 
 def place_kernel(sources, rows):
@@ -337,20 +344,31 @@
         compiler_params=small,
     )(mine, layer)
     half = depth // 2
+    sums = [pltpu.VMEM((half, blocks) + tile, f32)] * 3
+    large = pltpu.CompilerParams(vmem_limit_bytes=16 * 2**20)
+    low, *prepared = pl.pallas_call(
+        main_kernel(depth, rows, blocks),
+        out_shape=[
+            shape(half, rows, size_y),
+            shape(7, depth, blocks + 6, *tile),
+            shape(3, depth, blocks + 2, *tile),
+            shape(5, depth + 2, blocks + 4, *tile),
+        ],
+        in_specs=[VMEM] * 4,
+        out_specs=[VMEM] * 4,
+        scratch_shapes=[pltpu.VMEM((depth, 7, tall, LANES), f32)] + sums,
+        compiler_params=large,
+    )(moved, scale, near, far)
+    work = 124 * 20 * half * rows * size_y
     halves = pl.pallas_call(
-        main_kernel(depth, rows, blocks),
+        second_kernel(depth, blocks),
         out_shape=[shape(half, rows, size_y)] * 2,
-        in_specs=[VMEM] * 4,
+        in_specs=[VMEM] * 5,
         out_specs=[VMEM] * 2,
-        scratch_shapes=[
-            pltpu.VMEM((depth, 7, tall, LANES), f32),
-            pltpu.VMEM((7, depth, blocks + 6) + tile, f32),
-            pltpu.VMEM((3, depth, blocks + 2) + tile, f32),
-            pltpu.VMEM((5, depth + 2, blocks + 4) + tile, f32),
-        ]
-        + [pltpu.VMEM((depth, blocks) + tile, f32)] * 3,
-        compiler_params=pltpu.CompilerParams(vmem_limit_bytes=16 * 2**20),
-    )(moved, scale, near, far)
+        scratch_shapes=sums,
+        cost_estimate=pl.CostEstimate(flops=work, bytes_accessed=work // 2, transcendentals=0),
+        compiler_params=large,
+    )(*prepared, scale, low)
 
     def place(blocks, whole):
         count = len(blocks)
@@ -370,8 +388,9 @@
 
     assert offs & (offs - 1) == 0
     bit = offs // 2
-    blocks = [((0, half * n), halves[n]) for n in range(2)]
-    blocks += [((bit, half * n), swapped(halves[n], bit)) for n in range(2)]
+    arrived = swapped(low, bit)
+    low, high, arrived = lax.optimization_barrier((*halves, arrived))
+    blocks = [((0, 0), low), ((0, half), high), ((bit, 0), arrived), ((bit, half), swapped(high, bit))]
     while bit > 1:
         bit //= 2
         blocks += [((step ^ bit, z), swapped(block, bit)) for (step, z), block in blocks]

time: 35.8 us -> 36.6 us (1.022)
  waiting for transfers between devices: 7.52 us -> 5.47 us
  Pallas kernels: 13.1 us -> 14.7 us
  starting transfers between devices: 12.8 us -> 14.1 us
    pallas_call x0 -> x1, Pallas kernels: none -> 5.87 us  [shards(): pl.pallas_call(second_kernel(depth, blocks), out_shape=[shape(half, rows,...]
    pallas_call x1, Pallas kernels: 11 us -> 6.73 us  [shards(): pl.pallas_call(main_kernel(depth, rows, blocks), out_shape=[shape(half, r...]
    ppermute x1, starting transfers between devices: 2.11 us -> 0.35 us  [shards(): far = lax.ppermute(strips, 'gy', list(enumerate(second)))]
    ppermute x1, starting transfers between devices: 0.07 us -> 1.83 us  [shards(): near = lax.ppermute(strips, 'gy', list(enumerate(first)))]
    ppermute x6, waiting for transfers between devices: 5.73 us -> 4.05 us  [swapped(): return lax.ppermute(block, 'off', [(i, i ^ bit) for i in range(offs)])]
    ppermute x6, starting transfers between devices: 7.6 us -> 8.85 us  [swapped(): return lax.ppermute(block, 'off', [(i, i ^ bit) for i in range(offs)])]
  transfers between devices with their start and end apart: 9 -> 9, of which waited for: 6 -> 6; matrix products, arithmetic and copies ran while one was open for 0% -> 0% of each run, Pallas kernels for 4% -> 20%
where the time goes in v12:
time: 36.6 us; the launch traced here: 36.4 us
  Pallas kernels  14.7 us (40%)
  starting transfers between devices  14.1 us (39%)
  waiting for transfers between devices  5.47 us (15%)
  local copies, waits for them, and re-layouts  2.08 us (6%)
    ppermute x6, starting transfers between devices, swapped(): return lax.ppermute(block, 'off', [(i, i ^ bit) for i in range(offs)])  8.85 us
    pallas_call x1, Pallas kernels, shards(): pl.pallas_call(main_kernel(depth, rows, blocks), out_shape=[shape(half, r...  6.73 us
    pallas_call x1, Pallas kernels, shards(): pl.pallas_call(second_kernel(depth, blocks), out_shape=[shape(half, rows,...  5.87 us
    ppermute x6, waiting for transfers between devices, swapped(): return lax.ppermute(block, 'off', [(i, i ^ bit) for i in range(offs)])  4.05 us
    ppermute x1, starting transfers between devices, shards(): layer = lax.ppermute(layer, ('gx', 'off'), moves)  3.03 us
    unnamed x4, local copies, waits for them, and re-layouts  2.08 us
    ppermute x1, starting transfers between devices, shards(): near = lax.ppermute(strips, 'gy', list(enumerate(first)))  1.83 us
    pallas_call x2, Pallas kernels, place(): pl.pallas_call(place_kernel([source for source, _ in blocks], rows), out_...  1.45 us
  transfers between devices with their start and end apart: 9, of which 6 were waited for; matrix products, arithmetic and copies ran while one was open for 0% of the time, Pallas kernels for 20%

profile of v12, /device:TPU:0, one launch (start us, length us, event | category | flops | bytes accessed | tf_op | source)
XLA Modules:
  0.0 36.4 jit_solution(5801514839461963653)
XLA Ops:
  0.0 0.0 copy-start
  0.0 1.0 %copy-done = f32[8,128,128]{2,1,0:T(8,128)S(1)} copy-done((f32[8,128,128]{2,1,0:T(8,128)S(1)}, f32[8,128,128]{2,1,0:T(8,128)}, u32[]{:S(2)}) %copy-start) | copy-done | bytes 524312
  1.1 3.0 %collective-permute-start = (f32[8,8,128]{2,1,0:T(8,128)S(1)}, f32[8,8,128]{2,1,0:T(8,128)S(1)}, u32[]{:S(2)}, u32[]{:S(2)}) collective-permute-start(f32[8,8,128]{2,1,0:T(8,128)S(1)} %shard_map.29), channel_id=1, source_target_pairs={{0,16},{1,17},{2,18},{3,19},{16,0},{17,1},{18,2},{19,3},{4,20},{5,... | collective-permute-start | bytes 98312 | tf_op jit(solution)/shard_map/ppermute | solution.py:318
  4.1 0.0 copy-start.1
  4.1 1.0 %copy-done.1 = f32[8,128,128]{2,1,0:T(8,128)S(1)} copy-done((f32[8,128,128]{2,1,0:T(8,128)S(1)}, f32[8,128,128]{2,1,0:T(8,128)}, u32[]{:S(2)}) %copy-start.1) | copy-done | bytes 524312
  5.1 0.2 shard_map.28
  5.4 0.6 %collective-permute-done.layer = f32[8,8,128]{2,1,0:T(8,128)S(1)} collective-permute-done((f32[8,8,128]{2,1,0:T(8,128)S(1)}, f32[8,8,128]{2,1,0:T(8,128)S(1)}, u32[]{:S(2)}, u32[]{:S(2)}) %collective-permute-start) | collective-permute-done | bytes 32800 | tf_op jit(solution)/shard_map/ppermute | solution.py:318
  6.0 0.1 shard_map.31
  6.1 0.3 collective-permute-start.2
  6.4 1.8 %collective-permute-start.1 = (f32[48,128]{1,0:T(8,128)S(1)}, f32[48,128]{1,0:T(8,128)S(1)}, u32[]{:S(2)}, u32[]{:S(2)}) collective-permute-start(f32[48,128]{1,0:T(8,128)S(1)} %shard_map.31), channel_id=1, source_target_pairs={{0,4},{4,0},{8,12},{12,8},{1,5},{5,1},{9,13},{13,9},{2,6},{6,2},{1... | collective-permute-start | bytes 73736 | tf_op jit(solution)/shard_map/ppermute | solution.py:336
  8.2 0.4 shard_map.30.moved
  8.6 0.8 %collective-permute-done.2.far = f32[48,128]{1,0:T(8,128)S(1)} collective-permute-done((f32[48,128]{1,0:T(8,128)S(1)}, f32[48,128]{1,0:T(8,128)S(1)}, u32[]{:S(2)}, u32[]{:S(2)}) %collective-permute-start.2) | collective-permute-done | bytes 24608 | tf_op jit(solution)/shard_map/ppermute | solution.py:337
  9.4 0.0 collective-permute-done.1.near
  9.4 6.7 %shard_map.32 = (f32[4,32,128]{2,1,0:T(8,128)S(1)}, f32[7,8,10,8,128]{4,3,2,1,0:T(8,128)S(1)}, f32[3,8,6,8,128]{4,3,2,1,0:T(8,128)S(1)}, f32[5,10,8,8,128]{4,3,2,1,0:T(8,128)S(1)}) custom-call(f32[8,7,48,128]{3,2,1,0:T(8,128)S(1)} %shard_map.30.moved, f32[8,4,8,128]{3,2,1,0:T(8,128)S(1)} %get-tuple-element.18.scale, ...), custom_call_target="tpu_custom_call" | custom-call | tf_op jit(solution)/shard_map/pallas_call | solution.py:349
  16.1 3.4 %collective-permute-start.3 = (f32[4,32,128]{2,1,0:T(8,128)S(1)}, f32[4,32,128]{2,1,0:T(8,128)S(1)}, u32[]{:S(2)}, u32[]{:S(2)}) collective-permute-start(f32[4,32,128]{2,1,0:T(8,128)S(1)} %get-tuple-element.23.low), channel_id=1, source_target_pairs={{0,2},{1,3},{2,0},{3,1},{4,6},{5,7},{6,4},{7,5},{8,10},{9,11},{10,... | collective-permute-start | bytes 196616 | tf_op jit(solution)/shard_map/ppermute | solution.py:387
  19.5 5.9 %shard_map.33 = (f32[4,32,128]{2,1,0:T(8,128)S(1)}, f32[4,32,128]{2,1,0:T(8,128)S(1)}) custom-call(f32[7,8,10,8,128]{4,3,2,1,0:T(8,128)S(1)} %get-tuple-element.20.vals, f32[3,8,6,8,128]{4,3,2,1,0:T(8,128)S(1)} %get-tuple-element.21.cent, f32[5,10,8,8,128]{4,3,2,1,0:T(8,128)S(1)} %get-tuple-element.22.energy, f32[8,4,8,128]{3,2,1,0:T(8,128)S(1)} %get-tuple-element.18.scale, ...), custom_call_target="tpu_custom_call" | custom-call | flops 40632320 | bytes 20316160 | tf_op jit(solution)/shard_map/pallas_call | solution.py:363
  25.4 0.0 collective-permute-done.3.refs_2_
  25.4 0.1 collective-permute-start.5
  25.5 1.9 %collective-permute-start.8 = (f32[4,32,128]{2,1,0:T(8,128)S(1)}, f32[4,32,128]{2,1,0:T(8,128)S(1)}, u32[]{:S(2)}, u32[]{:S(2)}) collective-permute-start(f32[4,32,128]{2,1,0:T(8,128)S(1)} %get-tuple-element.27.refs_1_), channel_id=1, source_target_pairs={{0,1},{1,0},{2,3},{3,2},{4,5},{5,4},{6,7},{7,6},{8,9},{9,8},{10,11... | collective-permute-start | bytes 196616 | tf_op jit(solution)/shard_map/ppermute | solution.py:387
  27.4 0.2 collective-permute-start.7
  27.6 1.9 %collective-permute-start.4 = (f32[4,32,128]{2,1,0:T(8,128)S(1)}, f32[4,32,128]{2,1,0:T(8,128)S(1)}, u32[]{:S(2)}, u32[]{:S(2)}) collective-permute-start(f32[4,32,128]{2,1,0:T(8,128)S(1)} %collective-permute-done.3.refs_2_), channel_id=1, source_target_pairs={{0,1},{1,0},{2,3},{3,2},{4,5},{5,4},{6,7},{7,6},{8,9},{9,8},{10,11... | collective-permute-start | bytes 196616 | tf_op jit(solution)/shard_map/ppermute | solution.py:387
  29.4 2.0 %collective-permute-done.5.refs_3_ = f32[4,32,128]{2,1,0:T(8,128)S(1)} collective-permute-done((f32[4,32,128]{2,1,0:T(8,128)S(1)}, f32[4,32,128]{2,1,0:T(8,128)S(1)}, u32[]{:S(2)}, u32[]{:S(2)}) %collective-permute-start.5) | collective-permute-done | bytes 65568 | tf_op jit(solution)/shard_map/ppermute | solution.py:387
  31.5 1.5 %collective-permute-start.6 = (f32[4,32,128]{2,1,0:T(8,128)S(1)}, f32[4,32,128]{2,1,0:T(8,128)S(1)}, u32[]{:S(2)}, u32[]{:S(2)}) collective-permute-start(f32[4,32,128]{2,1,0:T(8,128)S(1)} %collective-permute-done.5.refs_3_), channel_id=1, source_target_pairs={{0,1},{1,0},{2,3},{3,2},{4,5},{5,4},{6,7},{7,6},{8,9},{9,8},{10,11... | collective-permute-start | bytes 196616 | tf_op jit(solution)/shard_map/ppermute | solution.py:387
  32.9 0.1 collective-permute-done.7.refs_4_
  33.0 0.0 collective-permute-done.8.refs_5_
  33.0 0.8 %shard_map.34.refs_2_ = f32[8,128,128]{2,1,0:T(8,128)} custom-call(f32[4,32,128]{2,1,0:T(8,128)S(1)} %get-tuple-element.28.refs_0_, f32[4,32,128]{2,1,0:T(8,128)S(1)} %get-tuple-element.27.refs_1_, f32[4,32,128]{2,1,0:T(8,128)S(1)} %collective-permute-done.3.refs_2_, f32[4,32,128]{2,1,0:T(8,128)S(1)} %collective-permute-done.5.refs_3_, ...), custom_call_target="tpu_custom_call" | custom-call | tf_op jit(solution)/shard_map/pallas_call | solution.py:376
  33.8 0.6 %collective-permute-done.4.refs_0_ = f32[4,32,128]{2,1,0:T(8,128)S(1)} collective-permute-done((f32[4,32,128]{2,1,0:T(8,128)S(1)}, f32[4,32,128]{2,1,0:T(8,128)S(1)}, u32[]{:S(2)}, u32[]{:S(2)}) %collective-permute-start.4) | collective-permute-done | bytes 65568 | tf_op jit(solution)/shard_map/ppermute | solution.py:387
  34.4 1.3 %collective-permute-done.6.refs_1_ = f32[4,32,128]{2,1,0:T(8,128)S(1)} collective-permute-done((f32[4,32,128]{2,1,0:T(8,128)S(1)}, f32[4,32,128]{2,1,0:T(8,128)S(1)}, u32[]{:S(2)}, u32[]{:S(2)}) %collective-permute-start.6) | collective-permute-done | bytes 65568 | tf_op jit(solution)/shard_map/ppermute | solution.py:387
  35.7 0.7 %shard_map.35 = f32[8,128,128]{2,1,0:T(8,128)} custom-call(f32[4,32,128]{2,1,0:T(8,128)S(1)} %collective-permute-done.4.refs_0_, f32[4,32,128]{2,1,0:T(8,128)S(1)} %collective-permute-done.6.refs_1_, f32[8,128,128]{2,1,0:T(8,128)} %shard_map.34.refs_2_), custom_call_target="tpu_custom_call", output_to_operand_aliasing={{}: (2, {})} | custom-call | tf_op jit(solution)/shard_map/pallas_call | solution.py:376
  (1 shorter events, 0.0 us)
Async XLA Ops:
  0.0 1.0 %copy-start = (f32[8,128,128]{2,1,0:T(8,128)S(1)}, f32[8,128,128]{2,1,0:T(8,128)}, u32[]{:S(2)}) copy-start(f32[8,128,128]{2,1,0:T(8,128)} %volume.3) | copy-start | bytes 1572868
  1.1 4.9 %collective-permute-start = (f32[8,8,128]{2,1,0:T(8,128)S(1)}, f32[8,8,128]{2,1,0:T(8,128)S(1)}, u32[]{:S(2)}, u32[]{:S(2)}) collective-permute-start(f32[8,8,128]{2,1,0:T(8,128)S(1)} %shard_map.29), channel_id=1, source_target_pairs={{0,16},{1,17},{2,18},{3,19},{16,0},{17,1},{18,2},{19,3},{4,20},{5,... | collective-permute-start | bytes 98312 | tf_op jit(solution)/shard_map/ppermute | solution.py:318
  4.1 1.0 %copy-start.1 = (f32[8,128,128]{2,1,0:T(8,128)S(1)}, f32[8,128,128]{2,1,0:T(8,128)}, u32[]{:S(2)}) copy-start(f32[8,128,128]{2,1,0:T(8,128)} %strength.1) | copy-start | bytes 1572868
  6.1 3.3 %collective-permute-start.2 = (f32[48,128]{1,0:T(8,128)S(1)}, f32[48,128]{1,0:T(8,128)S(1)}, u32[]{:S(2)}, u32[]{:S(2)}) collective-permute-start(f32[48,128]{1,0:T(8,128)S(1)} %shard_map.31), channel_id=1, source_target_pairs={{0,12},{4,8},{8,4},{12,0},{1,13},{5,9},{9,5},{13,1},{2,14},{6,10},... | collective-permute-start | bytes 73736 | tf_op jit(solution)/shard_map/ppermute | solution.py:337
  6.4 3.0 %collective-permute-start.1 = (f32[48,128]{1,0:T(8,128)S(1)}, f32[48,128]{1,0:T(8,128)S(1)}, u32[]{:S(2)}, u32[]{:S(2)}) collective-permute-start(f32[48,128]{1,0:T(8,128)S(1)} %shard_map.31), channel_id=1, source_target_pairs={{0,4},{4,0},{8,12},{12,8},{1,5},{5,1},{9,13},{13,9},{2,6},{6,2},{1... | collective-permute-start | bytes 73736 | tf_op jit(solution)/shard_map/ppermute | solution.py:336
  16.1 9.2 %collective-permute-start.3 = (f32[4,32,128]{2,1,0:T(8,128)S(1)}, f32[4,32,128]{2,1,0:T(8,128)S(1)}, u32[]{:S(2)}, u32[]{:S(2)}) collective-permute-start(f32[4,32,128]{2,1,0:T(8,128)S(1)} %get-tuple-element.23.low), channel_id=1, source_target_pairs={{0,2},{1,3},{2,0},{3,1},{4,6},{5,7},{6,4},{7,5},{8,10},{9,11},{10,... | collective-permute-start | bytes 196616 | tf_op jit(solution)/shard_map/ppermute | solution.py:387
  25.4 6.1 %collective-permute-start.5 = (f32[4,32,128]{2,1,0:T(8,128)S(1)}, f32[4,32,128]{2,1,0:T(8,128)S(1)}, u32[]{:S(2)}, u32[]{:S(2)}) collective-permute-start(f32[4,32,128]{2,1,0:T(8,128)S(1)} %get-tuple-element.27.refs_1_), channel_id=1, source_target_pairs={{0,2},{1,3},{2,0},{3,1},{4,6},{5,7},{6,4},{7,5},{8,10},{9,11},{10,... | collective-permute-start | bytes 196616 | tf_op jit(solution)/shard_map/ppermute | solution.py:387
  25.5 7.5 %collective-permute-start.8 = (f32[4,32,128]{2,1,0:T(8,128)S(1)}, f32[4,32,128]{2,1,0:T(8,128)S(1)}, u32[]{:S(2)}, u32[]{:S(2)}) collective-permute-start(f32[4,32,128]{2,1,0:T(8,128)S(1)} %get-tuple-element.27.refs_1_), channel_id=1, source_target_pairs={{0,1},{1,0},{2,3},{3,2},{4,5},{5,4},{6,7},{7,6},{8,9},{9,8},{10,11... | collective-permute-start | bytes 196616 | tf_op jit(solution)/shard_map/ppermute | solution.py:387
  27.4 5.6 %collective-permute-start.7 = (f32[4,32,128]{2,1,0:T(8,128)S(1)}, f32[4,32,128]{2,1,0:T(8,128)S(1)}, u32[]{:S(2)}, u32[]{:S(2)}) collective-permute-start(f32[4,32,128]{2,1,0:T(8,128)S(1)} %get-tuple-element.28.refs_0_), channel_id=1, source_target_pairs={{0,1},{1,0},{2,3},{3,2},{4,5},{5,4},{6,7},{7,6},{8,9},{9,8},{10,11... | collective-permute-start | bytes 196616 | tf_op jit(solution)/shard_map/ppermute | solution.py:387
  27.6 6.8 %collective-permute-start.4 = (f32[4,32,128]{2,1,0:T(8,128)S(1)}, f32[4,32,128]{2,1,0:T(8,128)S(1)}, u32[]{:S(2)}, u32[]{:S(2)}) collective-permute-start(f32[4,32,128]{2,1,0:T(8,128)S(1)} %collective-permute-done.3.refs_2_), channel_id=1, source_target_pairs={{0,1},{1,0},{2,3},{3,2},{4,5},{5,4},{6,7},{7,6},{8,9},{9,8},{10,11... | collective-permute-start | bytes 196616 | tf_op jit(solution)/shard_map/ppermute | solution.py:387
  31.5 4.3 %collective-permute-start.6 = (f32[4,32,128]{2,1,0:T(8,128)S(1)}, f32[4,32,128]{2,1,0:T(8,128)S(1)}, u32[]{:S(2)}, u32[]{:S(2)}) collective-permute-start(f32[4,32,128]{2,1,0:T(8,128)S(1)} %collective-permute-done.5.refs_3_), channel_id=1, source_target_pairs={{0,1},{1,0},{2,3},{3,2},{4,5},{5,4},{6,7},{7,6},{8,9},{9,8},{10,11... | collective-permute-start | bytes 196616 | tf_op jit(solution)/shard_map/ppermute | solution.py:387

commit v13 on v12

--- a/solution.py
+++ b/solution.py
@@ -270,14 +270,15 @@
             out[z, pl.ds(i, SUBS, stride=blocks), :] = value
 
 
-def place_kernel(sources, rows):
+def place_kernel(sources, rows, slices):
     def kernel(*refs):
         parts, (*_, out, done) = refs[: len(sources)], refs[len(sources) :]
         off = lax.axis_index("off")
         copies = []
-        for n, (part, (step, z)) in enumerate(zip(parts, sources)):
+        for n, (part, (step, z, first)) in enumerate(zip(parts, sources)):
             at = pl.ds(pl.multiple_of((off ^ step) * rows, SUBS), rows)
-            target = out.at[z : z + part.shape[0], at, :]
+            target = out.at[z : z + slices, at, :]
+            part = part.at[first : first + slices]
             copies.append(pltpu.make_async_copy(part, target, done.at[n]))
             copies[n].start()
         for copy in copies:
@@ -374,7 +375,7 @@
         count = len(blocks)
         held = [] if whole is None else [whole]
         return pl.pallas_call(
-            place_kernel([source for source, _ in blocks], rows),
+            place_kernel([source for source, _ in blocks], rows, half),
             out_shape=shape(depth, size_x, size_y),
             in_specs=[VMEM] * count + [HBM] * len(held),
             out_specs=HBM,
@@ -390,11 +391,16 @@
     bit = offs // 2
     arrived = swapped(low, bit)
     low, high, arrived = lax.optimization_barrier((*halves, arrived))
-    blocks = [((0, 0), low), ((0, half), high), ((bit, 0), arrived), ((bit, half), swapped(high, bit))]
+    early = [((0, 0, 0), low), ((0, half, 0), high), ((bit, 0, 0), arrived)]
+    late = [((bit, half, 0), swapped(high, bit))]
     while bit > 1:
         bit //= 2
-        blocks += [((step ^ bit, z), swapped(block, bit)) for (step, z), block in blocks]
-    return place(blocks[-2:], place(blocks[:-2], None))
+        joined = [block[first : first + half] for (*_, first), block in early]
+        got = swapped(jnp.concatenate(joined), bit)
+        early += [((at[0] ^ bit, at[1], half * n), got) for n, (at, _) in enumerate(early)]
+        last = [((step ^ bit, z, 0), swapped(block, bit)) for (step, z, _), block in late]
+        late += last
+    return place(late[-1:], place(early + late[:-1], None))
 
 
 def solution(mesh):

time: 36.6 us -> 38.6 us (1.055)
  waiting for transfers between devices: 5.47 us -> 10.4 us
  starting transfers between devices: 14.1 us -> 11.1 us
    ppermute x6 -> x4, waiting for transfers between devices: 4.05 us -> 9.01 us  [swapped(): return lax.ppermute(block, 'off', [(i, i ^ bit) for i in range(offs)])]
    ppermute x6 -> x4, starting transfers between devices: 8.85 us -> 5.91 us  [swapped(): return lax.ppermute(block, 'off', [(i, i ^ bit) for i in range(offs)])]
  transfers between devices with their start and end apart: 9 -> 7, of which waited for: 6 -> 4; matrix products, arithmetic and copies ran while one was open for 0% -> 0% of each run, Pallas kernels for 20% -> 19%
where the time goes in v13:
time: 38.6 us; the launch traced here: 38.4 us
  Pallas kernels  14.7 us (38%)
  starting transfers between devices  11.1 us (29%)
  waiting for transfers between devices  10.4 us (27%)
  local copies, waits for them, and re-layouts  2.08 us (5%)
    ppermute x4, waiting for transfers between devices, swapped(): return lax.ppermute(block, 'off', [(i, i ^ bit) for i in range(offs)])  9.01 us
    pallas_call x1, Pallas kernels, shards(): pl.pallas_call(main_kernel(depth, rows, blocks), out_shape=[shape(half, r...  6.73 us
    ppermute x4, starting transfers between devices, swapped(): return lax.ppermute(block, 'off', [(i, i ^ bit) for i in range(offs)])  5.91 us
    pallas_call x1, Pallas kernels, shards(): pl.pallas_call(second_kernel(depth, blocks), out_shape=[shape(half, rows,...  5.87 us
    ppermute x1, starting transfers between devices, shards(): layer = lax.ppermute(layer, ('gx', 'off'), moves)  3.03 us
    unnamed x4, local copies, waits for them, and re-layouts  2.08 us
    ppermute x1, starting transfers between devices, shards(): near = lax.ppermute(strips, 'gy', list(enumerate(first)))  1.83 us
    pallas_call x2, Pallas kernels, place(): pl.pallas_call(place_kernel([source for source, _ in blocks], rows, half)...  1.45 us
  transfers between devices with their start and end apart: 7, of which 4 were waited for; matrix products, arithmetic and copies ran while one was open for 0% of the time, Pallas kernels for 19%

profile of v13, /device:TPU:0, one launch (start us, length us, event | category | flops | bytes accessed | tf_op | source)
XLA Modules:
  0.0 38.4 jit_solution(2772820697464587434)
XLA Ops:
  0.0 0.0 copy-start
  0.0 1.0 %copy-done = f32[8,128,128]{2,1,0:T(8,128)S(1)} copy-done((f32[8,128,128]{2,1,0:T(8,128)S(1)}, f32[8,128,128]{2,1,0:T(8,128)}, u32[]{:S(2)}) %copy-start) | copy-done | bytes 524312
  1.1 3.0 %collective-permute-start = (f32[8,8,128]{2,1,0:T(8,128)S(1)}, f32[8,8,128]{2,1,0:T(8,128)S(1)}, u32[]{:S(2)}, u32[]{:S(2)}) collective-permute-start(f32[8,8,128]{2,1,0:T(8,128)S(1)} %shard_map.29), channel_id=1, source_target_pairs={{0,16},{1,17},{2,18},{3,19},{16,0},{17,1},{18,2},{19,3},{4,20},{5,... | collective-permute-start | bytes 98312 | tf_op jit(solution)/shard_map/ppermute | solution.py:319
  4.1 0.0 copy-start.1
  4.1 1.0 %copy-done.1 = f32[8,128,128]{2,1,0:T(8,128)S(1)} copy-done((f32[8,128,128]{2,1,0:T(8,128)S(1)}, f32[8,128,128]{2,1,0:T(8,128)}, u32[]{:S(2)}) %copy-start.1) | copy-done | bytes 524312
  5.1 0.2 shard_map.28
  5.4 0.6 %collective-permute-done.layer = f32[8,8,128]{2,1,0:T(8,128)S(1)} collective-permute-done((f32[8,8,128]{2,1,0:T(8,128)S(1)}, f32[8,8,128]{2,1,0:T(8,128)S(1)}, u32[]{:S(2)}, u32[]{:S(2)}) %collective-permute-start) | collective-permute-done | bytes 32800 | tf_op jit(solution)/shard_map/ppermute | solution.py:319
  6.0 0.1 shard_map.31
  6.1 0.3 collective-permute-start.2
  6.4 1.8 %collective-permute-start.1 = (f32[48,128]{1,0:T(8,128)S(1)}, f32[48,128]{1,0:T(8,128)S(1)}, u32[]{:S(2)}, u32[]{:S(2)}) collective-permute-start(f32[48,128]{1,0:T(8,128)S(1)} %shard_map.31), channel_id=1, source_target_pairs={{0,4},{4,0},{8,12},{12,8},{1,5},{5,1},{9,13},{13,9},{2,6},{6,2},{1... | collective-permute-start | bytes 73736 | tf_op jit(solution)/shard_map/ppermute | solution.py:337
  8.2 0.4 shard_map.30.moved
  8.6 0.8 %collective-permute-done.2.far = f32[48,128]{1,0:T(8,128)S(1)} collective-permute-done((f32[48,128]{1,0:T(8,128)S(1)}, f32[48,128]{1,0:T(8,128)S(1)}, u32[]{:S(2)}, u32[]{:S(2)}) %collective-permute-start.2) | collective-permute-done | bytes 24608 | tf_op jit(solution)/shard_map/ppermute | solution.py:338
  9.4 0.0 collective-permute-done.1.near
  9.4 6.7 %shard_map.32 = (f32[4,32,128]{2,1,0:T(8,128)S(1)}, f32[7,8,10,8,128]{4,3,2,1,0:T(8,128)S(1)}, f32[3,8,6,8,128]{4,3,2,1,0:T(8,128)S(1)}, f32[5,10,8,8,128]{4,3,2,1,0:T(8,128)S(1)}) custom-call(f32[8,7,48,128]{3,2,1,0:T(8,128)S(1)} %shard_map.30.moved, f32[8,4,8,128]{3,2,1,0:T(8,128)S(1)} %get-tuple-element.18.scale, ...), custom_call_target="tpu_custom_call" | custom-call | tf_op jit(solution)/shard_map/pallas_call | solution.py:350
  16.1 3.4 %collective-permute-start.3 = (f32[4,32,128]{2,1,0:T(8,128)S(1)}, f32[4,32,128]{2,1,0:T(8,128)S(1)}, u32[]{:S(2)}, u32[]{:S(2)}) collective-permute-start(f32[4,32,128]{2,1,0:T(8,128)S(1)} %get-tuple-element.23.low), channel_id=1, source_target_pairs={{0,2},{1,3},{2,0},{3,1},{4,6},{5,7},{6,4},{7,5},{8,10},{9,11},{10,... | collective-permute-start | bytes 196616 | tf_op jit(solution)/shard_map/ppermute | solution.py:388
  19.5 5.9 %shard_map.33 = (f32[4,32,128]{2,1,0:T(8,128)S(1)}, f32[4,32,128]{2,1,0:T(8,128)S(1)}) custom-call(f32[7,8,10,8,128]{4,3,2,1,0:T(8,128)S(1)} %get-tuple-element.20.vals, f32[3,8,6,8,128]{4,3,2,1,0:T(8,128)S(1)} %get-tuple-element.21.cent, f32[5,10,8,8,128]{4,3,2,1,0:T(8,128)S(1)} %get-tuple-element.22.energy, f32[8,4,8,128]{3,2,1,0:T(8,128)S(1)} %get-tuple-element.18.scale, ...), custom_call_target="tpu_custom_call" | custom-call | flops 40632320 | bytes 20316160 | tf_op jit(solution)/shard_map/pallas_call | solution.py:364
  25.4 0.0 collective-permute-done.3.refs_2_
  25.4 1.6 %collective-permute-start.6 = (f32[12,32,128]{2,1,0:T(8,128)S(1)}, f32[12,32,128]{2,1,0:T(8,128)S(1)}, u32[]{:S(2)}, u32[]{:S(2)}) collective-permute-start(f32[12,32,128]{2,1,0:T(8,128)S(1)} %pad_maximum_fusion), channel_id=1, source_target_pairs={{0,1},{1,0},{2,3},{3,2},{4,5},{5,4},{6,7},{7,6},{8,9},{9,8},{10,11... | collective-permute-start | bytes 589832 | tf_op jit(solution)/shard_map/ppermute | solution.py:388
  27.1 0.4 %collective-permute-start.4 = (f32[4,32,128]{2,1,0:T(8,128)S(1)}, f32[4,32,128]{2,1,0:T(8,128)S(1)}, u32[]{:S(2)}, u32[]{:S(2)}) collective-permute-start(f32[4,32,128]{2,1,0:T(8,128)S(1)} %get-tuple-element.26.refs_1_), channel_id=1, source_target_pairs={{0,2},{1,3},{2,0},{3,1},{4,6},{5,7},{6,4},{7,5},{8,10},{9,11},{10,... | collective-permute-start | bytes 196616 | tf_op jit(solution)/shard_map/ppermute | solution.py:388
  27.5 6.1 %collective-permute-done.4.refs_6_ = f32[4,32,128]{2,1,0:T(8,128)S(1)} collective-permute-done((f32[4,32,128]{2,1,0:T(8,128)S(1)}, f32[4,32,128]{2,1,0:T(8,128)S(1)}, u32[]{:S(2)}, u32[]{:S(2)}) %collective-permute-start.4) | collective-permute-done | bytes 65568 | tf_op jit(solution)/shard_map/ppermute | solution.py:388
  33.5 0.5 %collective-permute-start.5 = (f32[4,32,128]{2,1,0:T(8,128)S(1)}, f32[4,32,128]{2,1,0:T(8,128)S(1)}, u32[]{:S(2)}, u32[]{:S(2)}) collective-permute-start(f32[4,32,128]{2,1,0:T(8,128)S(1)} %collective-permute-done.4.refs_6_), channel_id=1, source_target_pairs={{0,1},{1,0},{2,3},{3,2},{4,5},{5,4},{6,7},{7,6},{8,9},{9,8},{10,11... | collective-permute-start | bytes 196616 | tf_op jit(solution)/shard_map/ppermute | solution.py:388
  34.0 0.0 collective-permute-done.6.refs_3_.refs_4_.refs_5_
  34.0 0.8 %shard_map.34.refs_1_ = f32[8,128,128]{2,1,0:T(8,128)} custom-call(f32[4,32,128]{2,1,0:T(8,128)S(1)} %get-tuple-element.27.refs_0_, f32[4,32,128]{2,1,0:T(8,128)S(1)} %get-tuple-element.26.refs_1_, f32[4,32,128]{2,1,0:T(8,128)S(1)} %collective-permute-done.3.refs_2_, f32[12,32,128]{2,1,0:T(8,128)S(1)} %collective-permute-done.6.refs_3_.refs_4_.refs_5_, ...), custom_call_target="tpu_custom_call" | custom-call | tf_op jit(solution)/shard_map/pallas_call | solution.py:377
  34.8 3.0 %collective-permute-done.5.refs_0_ = f32[4,32,128]{2,1,0:T(8,128)S(1)} collective-permute-done((f32[4,32,128]{2,1,0:T(8,128)S(1)}, f32[4,32,128]{2,1,0:T(8,128)S(1)}, u32[]{:S(2)}, u32[]{:S(2)}) %collective-permute-start.5) | collective-permute-done | bytes 65568 | tf_op jit(solution)/shard_map/ppermute | solution.py:388
  37.8 0.6 %shard_map.35 = f32[8,128,128]{2,1,0:T(8,128)} custom-call(f32[4,32,128]{2,1,0:T(8,128)S(1)} %collective-permute-done.5.refs_0_, f32[8,128,128]{2,1,0:T(8,128)} %shard_map.34.refs_1_), custom_call_target="tpu_custom_call", output_to_operand_aliasing={{}: (1, {})} | custom-call | tf_op jit(solution)/shard_map/pallas_call | solution.py:377
  (2 shorter events, 0.0 us)
Async XLA Ops:
  0.0 1.0 %copy-start = (f32[8,128,128]{2,1,0:T(8,128)S(1)}, f32[8,128,128]{2,1,0:T(8,128)}, u32[]{:S(2)}) copy-start(f32[8,128,128]{2,1,0:T(8,128)} %volume.3) | copy-start | bytes 1572868
  1.1 4.9 %collective-permute-start = (f32[8,8,128]{2,1,0:T(8,128)S(1)}, f32[8,8,128]{2,1,0:T(8,128)S(1)}, u32[]{:S(2)}, u32[]{:S(2)}) collective-permute-start(f32[8,8,128]{2,1,0:T(8,128)S(1)} %shard_map.29), channel_id=1, source_target_pairs={{0,16},{1,17},{2,18},{3,19},{16,0},{17,1},{18,2},{19,3},{4,20},{5,... | collective-permute-start | bytes 98312 | tf_op jit(solution)/shard_map/ppermute | solution.py:319
  4.1 1.0 %copy-start.1 = (f32[8,128,128]{2,1,0:T(8,128)S(1)}, f32[8,128,128]{2,1,0:T(8,128)}, u32[]{:S(2)}) copy-start(f32[8,128,128]{2,1,0:T(8,128)} %strength.1) | copy-start | bytes 1572868
  6.1 3.3 %collective-permute-start.2 = (f32[48,128]{1,0:T(8,128)S(1)}, f32[48,128]{1,0:T(8,128)S(1)}, u32[]{:S(2)}, u32[]{:S(2)}) collective-permute-start(f32[48,128]{1,0:T(8,128)S(1)} %shard_map.31), channel_id=1, source_target_pairs={{0,12},{4,8},{8,4},{12,0},{1,13},{5,9},{9,5},{13,1},{2,14},{6,10},... | collective-permute-start | bytes 73736 | tf_op jit(solution)/shard_map/ppermute | solution.py:338
  6.4 3.0 %collective-permute-start.1 = (f32[48,128]{1,0:T(8,128)S(1)}, f32[48,128]{1,0:T(8,128)S(1)}, u32[]{:S(2)}, u32[]{:S(2)}) collective-permute-start(f32[48,128]{1,0:T(8,128)S(1)} %shard_map.31), channel_id=1, source_target_pairs={{0,4},{4,0},{8,12},{12,8},{1,5},{5,1},{9,13},{13,9},{2,6},{6,2},{1... | collective-permute-start | bytes 73736 | tf_op jit(solution)/shard_map/ppermute | solution.py:337
  16.1 9.2 %collective-permute-start.3 = (f32[4,32,128]{2,1,0:T(8,128)S(1)}, f32[4,32,128]{2,1,0:T(8,128)S(1)}, u32[]{:S(2)}, u32[]{:S(2)}) collective-permute-start(f32[4,32,128]{2,1,0:T(8,128)S(1)} %get-tuple-element.23.low), channel_id=1, source_target_pairs={{0,2},{1,3},{2,0},{3,1},{4,6},{5,7},{6,4},{7,5},{8,10},{9,11},{10,... | collective-permute-start | bytes 196616 | tf_op jit(solution)/shard_map/ppermute | solution.py:388
  25.4 8.6 %collective-permute-start.6 = (f32[12,32,128]{2,1,0:T(8,128)S(1)}, f32[12,32,128]{2,1,0:T(8,128)S(1)}, u32[]{:S(2)}, u32[]{:S(2)}) collective-permute-start(f32[12,32,128]{2,1,0:T(8,128)S(1)} %pad_maximum_fusion), channel_id=1, source_target_pairs={{0,1},{1,0},{2,3},{3,2},{4,5},{5,4},{6,7},{7,6},{8,9},{9,8},{10,11... | collective-permute-start | bytes 589832 | tf_op jit(solution)/shard_map/ppermute | solution.py:388
  27.1 6.5 %collective-permute-start.4 = (f32[4,32,128]{2,1,0:T(8,128)S(1)}, f32[4,32,128]{2,1,0:T(8,128)S(1)}, u32[]{:S(2)}, u32[]{:S(2)}) collective-permute-start(f32[4,32,128]{2,1,0:T(8,128)S(1)} %get-tuple-element.26.refs_1_), channel_id=1, source_target_pairs={{0,2},{1,3},{2,0},{3,1},{4,6},{5,7},{6,4},{7,5},{8,10},{9,11},{10,... | collective-permute-start | bytes 196616 | tf_op jit(solution)/shard_map/ppermute | solution.py:388
  33.5 4.3 %collective-permute-start.5 = (f32[4,32,128]{2,1,0:T(8,128)S(1)}, f32[4,32,128]{2,1,0:T(8,128)S(1)}, u32[]{:S(2)}, u32[]{:S(2)}) collective-permute-start(f32[4,32,128]{2,1,0:T(8,128)S(1)} %collective-permute-done.4.refs_6_), channel_id=1, source_target_pairs={{0,1},{1,0},{2,3},{3,2},{4,5},{5,4},{6,7},{7,6},{8,9},{9,8},{10,11... | collective-permute-start | bytes 196616 | tf_op jit(solution)/shard_map/ppermute | solution.py:388

commit v14 on v10

--- a/solution.py
+++ b/solution.py
@@ -33,14 +33,6 @@
 
 def lanes():
     return lax.broadcasted_iota(jnp.int32, (SUBS, LANES), 1)
-
-
-def layer_kernel(volume, layer, arrived):
-    off, size_x = lax.axis_index("off"), volume.shape[1]
-    at = pl.multiple_of(jnp.where(off == 0, size_x - SUBS, 0), SUBS)
-    copy = pltpu.make_async_copy(volume.at[:, pl.ds(at, SUBS), :], layer, arrived)
-    copy.start()
-    copy.wait()
 
 
 def window(off, rows, size_x):
@@ -295,14 +287,8 @@
     def shape(*sizes):
         return jax.ShapeDtypeStruct(sizes, f32)
 
-    layer = pl.pallas_call(
-        layer_kernel,
-        out_shape=shape(depth, *tile),
-        in_specs=[HBM],
-        out_specs=VMEM,
-        scratch_shapes=[pltpu.SemaphoreType.DMA],
-        compiler_params=small,
-    )(volume)
+    at = jnp.where(lax.axis_index("off") == 0, size_x - SUBS, 0)
+    layer = lax.dynamic_slice_in_dim(volume, at, SUBS, 1)
     moves = []
     for x in range(gxs):
         for k in range(offs):

time: 35.8 us -> 35.5 us (level)
  local copies, waits for them, and re-layouts: 2.08 us -> 2.84 us
  waiting for transfers between devices: 7.52 us -> 6.91 us
  starting transfers between devices: 12.8 us -> 12.3 us
    dynamic_slice x0 -> x1, local copies, waits for them, and re-layouts: none -> 0.76 us  [shards(): layer = lax.dynamic_slice_in_dim(volume, at, SUBS, 1)]
    ppermute x1, waiting for transfers between devices: 0.64 us -> 0.01 us  [shards(): layer = lax.ppermute(layer, ('gx', 'off'), moves)]
    ppermute x1, starting transfers between devices: 2.11 us -> 1.69 us  [shards(): far = lax.ppermute(strips, 'gy', list(enumerate(second)))]
where the time goes in v14:
time: 35.5 us; the launch traced here: 35.2 us
  Pallas kernels  13.1 us (37%)
  starting transfers between devices  12.3 us (35%)
  waiting for transfers between devices  6.91 us (19%)
  local copies, waits for them, and re-layouts  2.84 us (8%)
    pallas_call x1, Pallas kernels, shards(): pl.pallas_call(main_kernel(depth, rows, blocks), out_shape=[shape(half, r...  11 us
    ppermute x6, starting transfers between devices, swapped(): return lax.ppermute(block, 'off', [(i, i ^ bit) for i in range(offs)])  7.58 us
    ppermute x6, waiting for transfers between devices, swapped(): return lax.ppermute(block, 'off', [(i, i ^ bit) for i in range(offs)])  5.65 us
    ppermute x1, starting transfers between devices, shards(): layer = lax.ppermute(layer, ('gx', 'off'), moves)  2.97 us
    unnamed x4, local copies, waits for them, and re-layouts  2.08 us
    ppermute x1, starting transfers between devices, shards(): far = lax.ppermute(strips, 'gy', list(enumerate(second)))  1.69 us
    pallas_call x2, Pallas kernels, place(): pl.pallas_call(place_kernel([source for source, _ in blocks], rows), out_...  1.45 us
    ppermute x1, waiting for transfers between devices, shards(): far = lax.ppermute(strips, 'gy', list(enumerate(second)))  1.25 us
  transfers between devices with their start and end apart: 9, of which 6 were waited for; matrix products, arithmetic and copies ran while one was open for 0% of the time, Pallas kernels for 4%

profile of v14, /device:TPU:0, one launch (start us, length us, event | category | flops | bytes accessed | tf_op | source)
XLA Modules:
  0.0 35.2 jit_solution(794340961878918862)
XLA Ops:
  0.0 0.8 %constant_dynamic-slice_fusion = f32[8,8,128]{2,1,0:T(8,128)S(1)} fusion(f32[8,128,128]{2,1,0:T(8,128)} %volume.1, s32[]{:T(128)S(6)} %select_n.5), kind=kLoop, calls=%fused_computation | loop fusion | bytes 65540 | tf_op jit(solution)/shard_map/dynamic_slice | solution.py:291
  0.8 3.0 %collective-permute-start = (f32[8,8,128]{2,1,0:T(8,128)S(1)}, f32[8,8,128]{2,1,0:T(8,128)S(1)}, u32[]{:S(2)}, u32[]{:S(2)}) collective-permute-start(f32[8,8,128]{2,1,0:T(8,128)S(1)} %constant_dynamic-slice_fusion), channel_id=1, source_target_pairs={{0,16},{1,17},{2,18},{3,19},{16,0},{17,1},{18,2},{19,3},{4,20},{5,... | collective-permute-start | bytes 98312 | tf_op jit(solution)/shard_map/ppermute | solution.py:297
  3.7 0.0 copy-start
  3.7 1.0 %copy-done = f32[8,128,128]{2,1,0:T(8,128)S(1)} copy-done((f32[8,128,128]{2,1,0:T(8,128)S(1)}, f32[8,128,128]{2,1,0:T(8,128)}, u32[]{:S(2)}) %copy-start) | copy-done | bytes 524312
  4.8 0.0 copy-start.1
  4.8 1.0 %copy-done.1 = f32[8,128,128]{2,1,0:T(8,128)S(1)} copy-done((f32[8,128,128]{2,1,0:T(8,128)S(1)}, f32[8,128,128]{2,1,0:T(8,128)}, u32[]{:S(2)}) %copy-start.1) | copy-done | bytes 524312
  5.8 0.2 shard_map.28
  6.0 0.0 collective-permute-done.layer
  6.0 0.1 shard_map.30
  6.1 0.1 collective-permute-start.1
  6.2 1.7 %collective-permute-start.2 = (f32[48,128]{1,0:T(8,128)S(1)}, f32[48,128]{1,0:T(8,128)S(1)}, u32[]{:S(2)}, u32[]{:S(2)}) collective-permute-start(f32[48,128]{1,0:T(8,128)S(1)} %shard_map.30), channel_id=1, source_target_pairs={{0,12},{4,8},{8,4},{12,0},{1,13},{5,9},{9,5},{13,1},{2,14},{6,10},... | collective-permute-start | bytes 73736 | tf_op jit(solution)/shard_map/ppermute | solution.py:316
  7.9 0.4 %shard_map.29.moved = f32[8,7,48,128]{3,2,1,0:T(8,128)S(1)} custom-call(f32[8,48,128]{2,1,0:T(8,128)S(1)} %get-tuple-element.10.mine, f32[8,8,128]{2,1,0:T(8,128)S(1)} %collective-permute-done.layer), custom_call_target="tpu_custom_call" | custom-call | flops 4000000 | bytes 4000000 | tf_op jit(solution)/shard_map/pallas_call | solution.py:317
  8.3 0.0 collective-permute-done.1.near
  8.3 1.3 %collective-permute-done.2.far = f32[48,128]{1,0:T(8,128)S(1)} collective-permute-done((f32[48,128]{1,0:T(8,128)S(1)}, f32[48,128]{1,0:T(8,128)S(1)}, u32[]{:S(2)}, u32[]{:S(2)}) %collective-permute-start.2) | collective-permute-done | bytes 24608 | tf_op jit(solution)/shard_map/ppermute | solution.py:316
  9.5 11.0 %shard_map.31 = (f32[4,32,128]{2,1,0:T(8,128)S(1)}, f32[4,32,128]{2,1,0:T(8,128)S(1)}) custom-call(f32[8,7,48,128]{3,2,1,0:T(8,128)S(1)} %shard_map.29.moved, f32[8,4,8,128]{3,2,1,0:T(8,128)S(1)} %get-tuple-element.11.scale, f32[48,128]{1,0:T(8,128)S(1)} %collective-permute-done.1.near, f32[48,128]{1,0:T(8,128)S(1)} %collective-permute-done.2.far), custom_call_target="tpu_custom_call" | custom-call | tf_op jit(solution)/shard_map/pallas_call | solution.py:326
  20.5 2.7 %collective-permute-start.3 = (f32[4,32,128]{2,1,0:T(8,128)S(1)}, f32[4,32,128]{2,1,0:T(8,128)S(1)}, u32[]{:S(2)}, u32[]{:S(2)}) collective-permute-start(f32[4,32,128]{2,1,0:T(8,128)S(1)} %get-tuple-element.13.refs_0_), channel_id=1, source_target_pairs={{0,2},{1,3},{2,0},{3,1},{4,6},{5,7},{6,4},{7,5},{8,10},{9,11},{10,... | collective-permute-start | bytes 196616 | tf_op jit(solution)/shard_map/ppermute | solution.py:355
  23.2 0.3 collective-permute-start.5
  23.5 1.7 %collective-permute-start.7 = (f32[4,32,128]{2,1,0:T(8,128)S(1)}, f32[4,32,128]{2,1,0:T(8,128)S(1)}, u32[]{:S(2)}, u32[]{:S(2)}) collective-permute-start(f32[4,32,128]{2,1,0:T(8,128)S(1)} %get-tuple-element.13.refs_0_), channel_id=1, source_target_pairs={{0,1},{1,0},{2,3},{3,2},{4,5},{5,4},{6,7},{7,6},{8,9},{9,8},{10,11... | collective-permute-start | bytes 196616 | tf_op jit(solution)/shard_map/ppermute | solution.py:355
  25.1 0.4 %collective-permute-start.8 = (f32[4,32,128]{2,1,0:T(8,128)S(1)}, f32[4,32,128]{2,1,0:T(8,128)S(1)}, u32[]{:S(2)}, u32[]{:S(2)}) collective-permute-start(f32[4,32,128]{2,1,0:T(8,128)S(1)} %get-tuple-element.14.refs_1_), channel_id=1, source_target_pairs={{0,1},{1,0},{2,3},{3,2},{4,5},{5,4},{6,7},{7,6},{8,9},{9,8},{10,11... | collective-permute-start | bytes 196616 | tf_op jit(solution)/shard_map/ppermute | solution.py:355
  25.5 2.1 %collective-permute-done.3.refs_2_ = f32[4,32,128]{2,1,0:T(8,128)S(1)} collective-permute-done((f32[4,32,128]{2,1,0:T(8,128)S(1)}, f32[4,32,128]{2,1,0:T(8,128)S(1)}, u32[]{:S(2)}, u32[]{:S(2)}) %collective-permute-start.3) | collective-permute-done | bytes 65568 | tf_op jit(solution)/shard_map/ppermute | solution.py:355
  27.6 1.9 %collective-permute-start.4 = (f32[4,32,128]{2,1,0:T(8,128)S(1)}, f32[4,32,128]{2,1,0:T(8,128)S(1)}, u32[]{:S(2)}, u32[]{:S(2)}) collective-permute-start(f32[4,32,128]{2,1,0:T(8,128)S(1)} %collective-permute-done.3.refs_2_), channel_id=1, source_target_pairs={{0,1},{1,0},{2,3},{3,2},{4,5},{5,4},{6,7},{7,6},{8,9},{9,8},{10,11... | collective-permute-start | bytes 196616 | tf_op jit(solution)/shard_map/ppermute | solution.py:355
  29.5 0.7 %collective-permute-done.5.refs_3_ = f32[4,32,128]{2,1,0:T(8,128)S(1)} collective-permute-done((f32[4,32,128]{2,1,0:T(8,128)S(1)}, f32[4,32,128]{2,1,0:T(8,128)S(1)}, u32[]{:S(2)}, u32[]{:S(2)}) %collective-permute-start.5) | collective-permute-done | bytes 65568 | tf_op jit(solution)/shard_map/ppermute | solution.py:355
  30.3 0.7 %collective-permute-start.6 = (f32[4,32,128]{2,1,0:T(8,128)S(1)}, f32[4,32,128]{2,1,0:T(8,128)S(1)}, u32[]{:S(2)}, u32[]{:S(2)}) collective-permute-start(f32[4,32,128]{2,1,0:T(8,128)S(1)} %collective-permute-done.5.refs_3_), channel_id=1, source_target_pairs={{0,1},{1,0},{2,3},{3,2},{4,5},{5,4},{6,7},{7,6},{8,9},{9,8},{10,11... | collective-permute-start | bytes 196616 | tf_op jit(solution)/shard_map/ppermute | solution.py:355
  30.9 0.0 collective-permute-done.7.refs_4_
  30.9 0.2 collective-permute-done.8.refs_5_
  31.2 0.8 %shard_map.32.refs_2_ = f32[8,128,128]{2,1,0:T(8,128)} custom-call(f32[4,32,128]{2,1,0:T(8,128)S(1)} %get-tuple-element.13.refs_0_, f32[4,32,128]{2,1,0:T(8,128)S(1)} %get-tuple-element.14.refs_1_, f32[4,32,128]{2,1,0:T(8,128)S(1)} %collective-permute-done.3.refs_2_, f32[4,32,128]{2,1,0:T(8,128)S(1)} %collective-permute-done.5.refs_3_, ...), custom_call_target="tpu_custom_call" | custom-call | tf_op jit(solution)/shard_map/pallas_call | solution.py:344
  31.9 0.3 collective-permute-done.4.refs_0_
  32.2 2.3 %collective-permute-done.6.refs_1_ = f32[4,32,128]{2,1,0:T(8,128)S(1)} collective-permute-done((f32[4,32,128]{2,1,0:T(8,128)S(1)}, f32[4,32,128]{2,1,0:T(8,128)S(1)}, u32[]{:S(2)}, u32[]{:S(2)}) %collective-permute-start.6) | collective-permute-done | bytes 65568 | tf_op jit(solution)/shard_map/ppermute | solution.py:355
  34.5 0.7 %shard_map.33 = f32[8,128,128]{2,1,0:T(8,128)} custom-call(f32[4,32,128]{2,1,0:T(8,128)S(1)} %collective-permute-done.4.refs_0_, f32[4,32,128]{2,1,0:T(8,128)S(1)} %collective-permute-done.6.refs_1_, f32[8,128,128]{2,1,0:T(8,128)} %shard_map.32.refs_2_), custom_call_target="tpu_custom_call", output_to_operand_aliasing={{}: (2, {})} | custom-call | tf_op jit(solution)/shard_map/pallas_call | solution.py:344
Async XLA Ops:
  0.8 5.3 %collective-permute-start = (f32[8,8,128]{2,1,0:T(8,128)S(1)}, f32[8,8,128]{2,1,0:T(8,128)S(1)}, u32[]{:S(2)}, u32[]{:S(2)}) collective-permute-start(f32[8,8,128]{2,1,0:T(8,128)S(1)} %constant_dynamic-slice_fusion), channel_id=1, source_target_pairs={{0,16},{1,17},{2,18},{3,19},{16,0},{17,1},{18,2},{19,3},{4,20},{5,... | collective-permute-start | bytes 98312 | tf_op jit(solution)/shard_map/ppermute | solution.py:297
  3.7 1.0 %copy-start = (f32[8,128,128]{2,1,0:T(8,128)S(1)}, f32[8,128,128]{2,1,0:T(8,128)}, u32[]{:S(2)}) copy-start(f32[8,128,128]{2,1,0:T(8,128)} %volume.1) | copy-start | bytes 1572868
  4.8 1.0 %copy-start.1 = (f32[8,128,128]{2,1,0:T(8,128)S(1)}, f32[8,128,128]{2,1,0:T(8,128)}, u32[]{:S(2)}) copy-start(f32[8,128,128]{2,1,0:T(8,128)} %strength.1) | copy-start | bytes 1572868
  6.1 2.1 %collective-permute-start.1 = (f32[48,128]{1,0:T(8,128)S(1)}, f32[48,128]{1,0:T(8,128)S(1)}, u32[]{:S(2)}, u32[]{:S(2)}) collective-permute-start(f32[48,128]{1,0:T(8,128)S(1)} %shard_map.30), channel_id=1, source_target_pairs={{0,4},{4,0},{8,12},{12,8},{1,5},{5,1},{9,13},{13,9},{2,6},{6,2},{1... | collective-permute-start | bytes 73736 | tf_op jit(solution)/shard_map/ppermute | solution.py:315
  6.2 3.3 %collective-permute-start.2 = (f32[48,128]{1,0:T(8,128)S(1)}, f32[48,128]{1,0:T(8,128)S(1)}, u32[]{:S(2)}, u32[]{:S(2)}) collective-permute-start(f32[48,128]{1,0:T(8,128)S(1)} %shard_map.30), channel_id=1, source_target_pairs={{0,12},{4,8},{8,4},{12,0},{1,13},{5,9},{9,5},{13,1},{2,14},{6,10},... | collective-permute-start | bytes 73736 | tf_op jit(solution)/shard_map/ppermute | solution.py:316
  20.5 7.1 %collective-permute-start.3 = (f32[4,32,128]{2,1,0:T(8,128)S(1)}, f32[4,32,128]{2,1,0:T(8,128)S(1)}, u32[]{:S(2)}, u32[]{:S(2)}) collective-permute-start(f32[4,32,128]{2,1,0:T(8,128)S(1)} %get-tuple-element.13.refs_0_), channel_id=1, source_target_pairs={{0,2},{1,3},{2,0},{3,1},{4,6},{5,7},{6,4},{7,5},{8,10},{9,11},{10,... | collective-permute-start | bytes 196616 | tf_op jit(solution)/shard_map/ppermute | solution.py:355
  23.2 7.0 %collective-permute-start.5 = (f32[4,32,128]{2,1,0:T(8,128)S(1)}, f32[4,32,128]{2,1,0:T(8,128)S(1)}, u32[]{:S(2)}, u32[]{:S(2)}) collective-permute-start(f32[4,32,128]{2,1,0:T(8,128)S(1)} %get-tuple-element.14.refs_1_), channel_id=1, source_target_pairs={{0,2},{1,3},{2,0},{3,1},{4,6},{5,7},{6,4},{7,5},{8,10},{9,11},{10,... | collective-permute-start | bytes 196616 | tf_op jit(solution)/shard_map/ppermute | solution.py:355
  23.5 7.4 %collective-permute-start.7 = (f32[4,32,128]{2,1,0:T(8,128)S(1)}, f32[4,32,128]{2,1,0:T(8,128)S(1)}, u32[]{:S(2)}, u32[]{:S(2)}) collective-permute-start(f32[4,32,128]{2,1,0:T(8,128)S(1)} %get-tuple-element.13.refs_0_), channel_id=1, source_target_pairs={{0,1},{1,0},{2,3},{3,2},{4,5},{5,4},{6,7},{7,6},{8,9},{9,8},{10,11... | collective-permute-start | bytes 196616 | tf_op jit(solution)/shard_map/ppermute | solution.py:355
  25.1 6.0 %collective-permute-start.8 = (f32[4,32,128]{2,1,0:T(8,128)S(1)}, f32[4,32,128]{2,1,0:T(8,128)S(1)}, u32[]{:S(2)}, u32[]{:S(2)}) collective-permute-start(f32[4,32,128]{2,1,0:T(8,128)S(1)} %get-tuple-element.14.refs_1_), channel_id=1, source_target_pairs={{0,1},{1,0},{2,3},{3,2},{4,5},{5,4},{6,7},{7,6},{8,9},{9,8},{10,11... | collective-permute-start | bytes 196616 | tf_op jit(solution)/shard_map/ppermute | solution.py:355
  27.6 4.6 %collective-permute-start.4 = (f32[4,32,128]{2,1,0:T(8,128)S(1)}, f32[4,32,128]{2,1,0:T(8,128)S(1)}, u32[]{:S(2)}, u32[]{:S(2)}) collective-permute-start(f32[4,32,128]{2,1,0:T(8,128)S(1)} %collective-permute-done.3.refs_2_), channel_id=1, source_target_pairs={{0,1},{1,0},{2,3},{3,2},{4,5},{5,4},{6,7},{7,6},{8,9},{9,8},{10,11... | collective-permute-start | bytes 196616 | tf_op jit(solution)/shard_map/ppermute | solution.py:355
  30.3 4.3 %collective-permute-start.6 = (f32[4,32,128]{2,1,0:T(8,128)S(1)}, f32[4,32,128]{2,1,0:T(8,128)S(1)}, u32[]{:S(2)}, u32[]{:S(2)}) collective-permute-start(f32[4,32,128]{2,1,0:T(8,128)S(1)} %collective-permute-done.5.refs_3_), channel_id=1, source_target_pairs={{0,1},{1,0},{2,3},{3,2},{4,5},{5,4},{6,7},{7,6},{8,9},{9,8},{10,11... | collective-permute-start | bytes 196616 | tf_op jit(solution)/shard_map/ppermute | solution.py:355
